TPU v7x, 256 devices: a whole 4x4x8 slice. The times are simulated.
256 devices in a mesh: rep: 8 (over z), shard: 32 (over x, y, core).
Axes of the slice: x: 4, y: 4, z: 8, core: 2. Of those that a mesh axis runs over, the one named last changes fastest.
Arguments:
- partials: bfloat16 [8, 4096, 16384], P('rep', None, 'shard'), may hold values from -45 to 45
- moment: float32 [4096, 16384], P('rep', 'shard'), may hold values from 0.5 to 50
- owner: int32 [8, 32], P('rep'), may hold values from 0 to 31, as said below
- roots: float32 [8, 32, 3, 2, 512, 512], P('rep', 'shard'), may hold values from -2 to 2, as said below
Outputs:
- direction: bfloat16 [4096, 16384], P('rep', 'shard')
- moment_new: float32 [4096, 16384], P('rep', 'shard')
Inputs may be any that keep to these rules, and one draw needn't show every extreme that they name: Entry [r, c] names the owner, an index along shard, of block c of block row r. No owner holds more than 3 blocks of one row, and in every row one owner holds exactly 3. `roots`: slot k of owner o in row r holds the factors of the k-th block in column order that o owns in row r; slots past an owner's count are never read. Each matrix is symmetric.
All inputs are finite; a program needn't handle non-finite values.
Results may differ from a plain program's by a relative error of at most 0.024.
Values may be sent and summed in bfloat16 or wider, within the bound.
No kernel may reach another device: no remote copies, remote signals or barrier semaphores. Data moves between devices by JAX's collectives and lax.ppermute only.
A program may use at most 64 MiB of HBM per device.

v0:
```python
import jax
import jax.numpy as jnp
from jax import lax
from jax.sharding import PartitionSpec as P

moment_decay = 0.95
adam_offset = 1e-08
norm_offset = 1e-06


def precondition(blocks, root_pairs):
    grad_float = blocks.astype(jnp.float32)
    left_part = jnp.einsum(
        "kij,kjl->kil",
        root_pairs[:, 0],
        grad_float,
        precision=lax.Precision.HIGHEST,
        preferred_element_type=jnp.float32,
    )
    return jnp.einsum(
        "kij,kjl->kil",
        left_part,
        root_pairs[:, 1],
        precision=lax.Precision.HIGHEST,
        preferred_element_type=jnp.float32,
    )


def grafted(conditioned, targets):
    graft_scale = targets / jnp.sqrt(jnp.sum(conditioned * conditioned, axis=(1, 2)) + norm_offset)
    return (conditioned * graft_scale[:, None, None]).astype(jnp.bfloat16)


def body(partials, moment, owner, roots):
    devices = lax.axis_size("shard")
    summed = lax.psum_scatter(partials, "rep", scatter_dimension=1, tiled=True).astype(jnp.float32)
    gradient = summed[0].astype(jnp.bfloat16)
    block_size = gradient.shape[0]
    stripe = gradient.shape[1]
    local_blocks = stripe // block_size
    piece_rows = block_size // devices
    grad_float = gradient.astype(jnp.float32)
    moment_new = moment_decay * moment + (1.0 - moment_decay) * grad_float * grad_float
    adam_step = grad_float / (jnp.sqrt(moment_new) + adam_offset)
    home_blocks = gradient.reshape(block_size, local_blocks, block_size).transpose(1, 0, 2)
    adam_norms = jnp.sqrt(
        jnp.sum(jnp.square(adam_step.reshape(block_size, local_blocks, block_size)), axis=(0, 2))
    )
    owner_row = owner[0]
    block_cols = owner_row.shape[0]
    capacity = roots.shape[2]
    block_ids = jnp.arange(block_cols, dtype=jnp.int32)
    earlier = block_ids[None, :] < block_ids[:, None]
    same_owner = owner_row[:, None] == owner_row[None, :]
    slot_rank = jnp.sum((same_owner & earlier).astype(jnp.int32), axis=1)
    owner_ids = jnp.arange(devices, dtype=jnp.int32)
    slot_ids = jnp.arange(capacity, dtype=jnp.int32)
    matches = (owner_row[None, None, :] == owner_ids[None, :, None]) & (
        slot_rank[None, None, :] == slot_ids[:, None, None]
    )
    chosen = jnp.sum(matches.astype(jnp.int32) * block_ids[None, None, :], axis=2)
    flat_place = owner_row * capacity + slot_rank
    pieces = lax.all_to_all(home_blocks[None], "shard", split_axis=2, concat_axis=0, tiled=True)
    pieces = pieces.reshape(block_cols, piece_rows, block_size)
    all_norms = lax.all_gather(adam_norms, "shard", axis=0, tiled=True)
    outgoing = jnp.take(pieces, chosen, axis=0)
    owned_blocks = lax.all_to_all(outgoing, "shard", split_axis=1, concat_axis=2, tiled=True)[:, 0]
    position = lax.axis_index("shard")
    own_ids = lax.dynamic_index_in_dim(chosen, position, axis=1, keepdims=False)
    targets = jnp.take(all_norms, own_ids)
    conditioned = precondition(owned_blocks, roots[0, 0])
    directions = grafted(conditioned, targets)
    returned = lax.all_to_all(directions[None], "shard", split_axis=2, concat_axis=0, tiled=True)
    returned = returned.reshape(devices * capacity, piece_rows, block_size)
    picked = jnp.take(returned, flat_place, axis=0).reshape(
        devices, local_blocks, piece_rows, block_size
    )
    direction_blocks = lax.all_to_all(picked, "shard", split_axis=0, concat_axis=2, tiled=True)[0]
    direction = direction_blocks.transpose(1, 0, 2).reshape(block_size, stripe)
    return (direction, moment_new)


def solution(mesh):
    placed = (
        P("rep", None, "shard"),
        P("rep", "shard"),
        P("rep", None),
        P("rep", "shard", None, None, None, None),
    )
    return jax.shard_map(
        body,
        mesh=mesh,
        in_specs=placed,
        out_specs=(P("rep", "shard"), P("rep", "shard")),
        check_vma=False,
    )
```

profile of v0, /device:TPU:1, one launch (start us, length us, event | category | flops | bytes accessed | tf_op | source)
XLA Modules:
  0.0 255.0 jit_solution(12169587724967848807)
XLA Ops:
  7.2 0.0 copy-start.2
  7.2 0.0 reduce-scatter.2.cloned.1.call-start
  7.2 0.7 reduce-scatter.2.cloned.1.call-update
  7.9 0.0 copy-done.2
  7.9 0.2 convert_reduce_fusion
  8.1 0.2 select_reduce_fusion
  8.3 61.5 %reduce-scatter.2.cloned.1.call-done = bf16[1,512,512]{2,1,0:T(8,128)(2,1)} async-done(((bf16[1,4096,512]{2,1,0:T(8,128)(2,1)}), bf16[1,512,512]{2,1,0:T(8,128)(2,1)}) %reduce-scatter.2.cloned.1.call-update) | async-done | bytes 524304 | tf_op jit(solution)/shard_map/reduce_scatter | solution.py:36
  69.7 1.9 copy.57
  71.6 0.5 broadcast.155
  72.1 3.8 %reduce.6 = bf16[512,512]{1,0:T(8,128)(2,1)S(1)} reduce(bf16[512,1,1,512]{3,2,1,0:T(2,128)(2,1)S(1)} %bitcast.64, bf16[]{:T(256)} %broadcast.155), dimensions={1,2}, to_apply=%bitcast.54.reduce_sub_computation | reduce | bytes 1048578
  75.9 1.2 reshape.202
  77.1 7.5 %all-to-all-start = ((bf16[32,2,4096]{2,1,0:T(2,128)(2,1)}), bf16[32,2,4096]{2,1,0:T(2,128)(2,1)S(1)}, u32[]{:S(2)}, u32[]{:S(2)}) async-start(bf16[32,2,4096]{2,1,0:T(2,128)(2,1)} %reshape.202), calls=%async_computation.1 | async-start | bytes 1048576 | tf_op jit(solution)/shard_map/all_to_all | solution.py:63
  84.6 0.1 reshape.172
  84.7 11.5 %all-to-all-done = bf16[32,2,4096]{2,1,0:T(2,128)(2,1)S(1)} async-done(((bf16[32,2,4096]{2,1,0:T(2,128)(2,1)}), bf16[32,2,4096]{2,1,0:T(2,128)(2,1)S(1)}, u32[]{:S(2)}, u32[]{:S(2)}) %all-to-all-start) | async-done | bytes 524320 | tf_op jit(solution)/shard_map/all_to_all | solution.py:63
  96.2 0.5 reshape.203
  96.8 0.1 copy.53
  96.9 0.7 gather_fusion
  97.6 0.2 broadcast_select_fusion
  97.8 1.3 copy.42
  99.2 4.5 %all-to-all-start.1 = ((bf16[3,32,16,512]{3,2,0,1:T(8,128)(2,1)}), bf16[3,32,16,512]{3,2,0,1:T(8,128)(2,1)}, u32[]{:S(2)}, u32[]{:S(2)}) async-start(bf16[3,32,16,512]{3,2,0,1:T(8,128)(2,1)} %copy.42), calls=%async_computation.2 | async-start | bytes 3145728 | tf_op jit(solution)/shard_map/all_to_all | solution.py:67
  103.7 0.0 copy-start.3
  103.7 0.0 copy-start
  103.7 0.0 copy-start.1
  103.7 7.0 %copy.56 = f32[1,1,3,2,512,512]{5,4,2,3,1,0:T(8,128)} copy(f32[1,1,3,2,512,512]{5,4,3,2,1,0:T(8,128)} %param.7) | data formatting | bytes 12582912 | tf_op args[3]
  110.7 0.0 copy-done.3
  110.7 0.6 dynamic-slice
  111.2 0.2 fusion.8
  111.4 0.2 and_reduce_fusion
  111.6 0.0 copy-done
  111.6 0.0 copy-done.1
  111.6 2.1 fusion.5
  114.5 0.7 dynamic-update-slice
  115.1 65.3 %all-reduce = f32[32]{0:T(128)S(1)} all-reduce(f32[32]{0:T(128)S(1)} %dynamic-update-slice), channel_id=1, replica_groups=mesh['rep'=8,'shard'=32] {'shard'}, use_global_device_ids=true, to_apply=%add | all-reduce | flops 32 | bytes 256
  180.4 0.0 slice-start
  180.4 0.6 gather_fusion.1
  181.0 0.0 all-to-all-done.1
  181.0 1.5 copy.43
  182.5 0.0 slice-start.1
  182.6 4.8 %fusion.1 = f32[3,512,512]{1,2,0:T(8,128)S(1)} fusion(bf16[3,512,512]{2,1,0:T(8,128)(2,1)S(1)} %bitcast.62, f32[3,2,512,512]{3,2,0,1:T(8,128)} %bitcast.55), kind=kOutput, calls=%fused_computation.7 | convolution fusion | flops 4831838208 | bytes 7864320 | tf_op jit(solution)/shard_map/kij,kjl->kil/dot_general | solution.py:13
  187.3 0.0 slice-done
  187.3 0.0 slice-done.1
  187.4 5.7 %multiply_reduce_fusion = (f32[3]{0:T(128)S(1)}, f32[3,512,512]{2,1,0:T(8,128)S(1)}) fusion(f32[3,512,512]{1,2,0:T(8,128)S(1)} %fusion.1, f32[3,2,512,512]{3,2,0,1:T(8,128)S(1)} %bitcast.58), kind=kOutput, calls=%fused_computation.9 | convolution fusion | flops 4833411072 | bytes 9437196 | tf_op jit(solution)/shard_map/kij,kjl->kil/dot_general | solution.py:20
  193.1 0.5 fusion.2
  193.6 2.7 %copy.47 = bf16[1,3,512,512]{3,1,0,2:T(4,128)(2,1)} copy(bf16[1,3,512,512]{3,2,1,0:T(8,128)(2,1)S(1)} %fusion.2) | data formatting | bytes 3145728 | tf_op jit(solution)/shard_map/broadcast_in_dim | solution.py:73
  196.3 6.1 %all-to-all-start.2 = ((bf16[1,3,512,512]{3,1,0,2:T(4,128)(2,1)}), bf16[1,3,512,512]{3,1,0,2:T(4,128)(2,1)S(1)}, u32[]{:S(2)}, u32[]{:S(2)}) async-start(bf16[1,3,512,512]{3,1,0,2:T(4,128)(2,1)} %copy.47), calls=%async_computation.3 | async-start | bytes 4194304 | tf_op jit(solution)/shard_map/all_to_all | solution.py:73
  202.5 28.3 %all-to-all-done.2 = bf16[1,3,512,512]{3,1,0,2:T(4,128)(2,1)S(1)} async-done(((bf16[1,3,512,512]{3,1,0,2:T(4,128)(2,1)}), bf16[1,3,512,512]{3,1,0,2:T(4,128)(2,1)S(1)}, u32[]{:S(2)}, u32[]{:S(2)}) %all-to-all-start.2) | async-done | bytes 1572896 | tf_op jit(solution)/shard_map/all_to_all | solution.py:73
  230.9 0.4 copy.48
  231.2 0.1 copy.49
  231.4 0.6 gather_fusion.2
  232.0 0.1 fusion.6
  232.1 15.3 %all_to_all.42 = bf16[32,1,16,512]{3,2,1,0:T(8,128)(2,1)S(1)} all-to-all(bf16[32,1,16,512]{3,2,1,0:T(8,128)(2,1)S(1)} %fusion.6), channel_id=1, replica_groups=mesh['rep'=8,'shard'=32] {'shard'}, dimensions={0} | all-to-all | bytes 1048576 | tf_op jit(solution)/shard_map/all_to_all | solution.py:78
  247.3 0.8 copy.60
  (12 shorter events, 0.1 us)
Async XLA Ops:
  7.2 0.7 copy-start.2
  7.2 62.6 %reduce-scatter.2.cloned.1.call-start = ((), (), s32[]{:S(2)}) async-start(), calls=%async_computation.5 | async-start | bytes 4718592 | tf_op jit(solution)/shard_map/reduce_scatter | solution.py:36
  77.1 19.1 %all-to-all-start = ((bf16[32,2,4096]{2,1,0:T(2,128)(2,1)}), bf16[32,2,4096]{2,1,0:T(2,128)(2,1)S(1)}, u32[]{:S(2)}, u32[]{:S(2)}) async-start(bf16[32,2,4096]{2,1,0:T(2,128)(2,1)} %reshape.202), calls=%async_computation.1 | async-start | bytes 1048576 | tf_op jit(solution)/shard_map/all_to_all | solution.py:63
  99.2 81.8 %all-to-all-start.1 = ((bf16[3,32,16,512]{3,2,0,1:T(8,128)(2,1)}), bf16[3,32,16,512]{3,2,0,1:T(8,128)(2,1)}, u32[]{:S(2)}, u32[]{:S(2)}) async-start(bf16[3,32,16,512]{3,2,0,1:T(8,128)(2,1)} %copy.42), calls=%async_computation.2 | async-start | bytes 3145728 | tf_op jit(solution)/shard_map/all_to_all | solution.py:67
  103.7 7.0 %copy-start.3 = (u32[256]{0:T(256)S(1)}, u32[256]{0:T(256)}, u32[]{:S(2)}) copy-start(u32[256]{0:T(256)} %constant.70) | copy-start | bytes 3076
  103.7 7.9 %copy-start = (bf16[1,512,512]{2,1,0:T(8,128)(2,1)S(1)}, bf16[1,512,512]{2,1,0:T(8,128)(2,1)}, u32[]{:S(2)}) copy-start(bf16[1,512,512]{2,1,0:T(8,128)(2,1)} %reduce-scatter.2.cloned.1.call-done) | copy-start | bytes 1572868
  103.7 7.9 %copy-start.1 = (f32[512,512]{1,0:T(8,128)S(1)}, f32[512,512]{1,0:T(8,128)}, u32[]{:S(2)}) copy-start(f32[512,512]{1,0:T(8,128)} %param.5) | copy-start | bytes 3145732
  180.4 7.0 %slice-start = ((s8[6291456]{0:T(1024)(128)(4,1)}), s8[2097152]{0:T(1024)(128)(4,1)S(1)}, s32[]{:S(2)}) async-start(s8[6291456]{0:T(1024)(128)(4,1)} %bitcast.56), calls=%async_computation.6 | async-start | bytes 4194304
  182.5 4.8 %slice-start.1 = ((s8[6291456]{0:T(1024)(128)(4,1)}), s8[4194304]{0:T(1024)(128)(4,1)S(1)}, s32[]{:S(2)}) async-start(s8[6291456]{0:T(1024)(128)(4,1)} %bitcast.56), calls=%async_computation.7 | async-start | bytes 8388608
  196.3 34.5 %all-to-all-start.2 = ((bf16[1,3,512,512]{3,1,0,2:T(4,128)(2,1)}), bf16[1,3,512,512]{3,1,0,2:T(4,128)(2,1)S(1)}, u32[]{:S(2)}, u32[]{:S(2)}) async-start(bf16[1,3,512,512]{3,1,0,2:T(4,128)(2,1)} %copy.47), calls=%async_computation.3 | async-start | bytes 4194304 | tf_op jit(solution)/shard_map/all_to_all | solution.py:73
Sparse Core Ops, SparseCore 0:
  10.6 59.1 reduce-scatter.1
where the time goes:
time: 255 us
  waiting for transfers between devices  102 us (40%)
  blocking collectives  80.5 us (32%)
  local copies, waits for them, and re-layouts  21.3 us (8%)
  starting transfers between devices  18.2 us (7%)
  between operations  15 us (6%)
  matrix products  10.5 us (4%)
  other arithmetic  7.58 us (3%)
    unnamed x1, blocking collectives  65.3 us
    reduce_scatter x1, waiting for transfers between devices, body(): lax.psum_scatter(partials, 'rep', scatter_dimension=1, tiled=True)  61.5 us
    all_to_all x1, waiting for transfers between devices, body(): lax.all_to_all(directions[None], 'shard', split_axis=2, concat_axis=0, ti...  28.3 us
    all_to_all x1, blocking collectives, body(): lax.all_to_all(picked, 'shard', split_axis=0, concat_axis=2, tiled=True)[0]  15.3 us
    all_to_all x1, waiting for transfers between devices, body(): lax.all_to_all(home_blocks[None], 'shard', split_axis=2, concat_axis=0, t...  11.5 us
    unnamed x21, local copies, waits for them, and re-layouts  11.3 us
    all_to_all x1, starting transfers between devices, body(): lax.all_to_all(home_blocks[None], 'shard', split_axis=2, concat_axis=0, t...  7.5 us
    all_to_all x1, starting transfers between devices, body(): lax.all_to_all(directions[None], 'shard', split_axis=2, concat_axis=0, ti...  6.14 us
  transfers between devices with their start and end apart: 4, of which 3 were waited for; matrix products, arithmetic and copies ran while one was open for 5% of the time, Pallas kernels for 0%

commit v1 on v0

v1 whole, which is shorter than its diff:
```python
import jax
import jax.numpy as jnp
from jax import lax
from jax.experimental import pallas as pl
from jax.experimental.pallas import tpu as pltpu
from jax.sharding import PartitionSpec as P

moment_decay = 0.95
adam_offset = 1e-08
norm_offset = 1e-06

B = 512
ROWS = 16
LANES = 128
QUARTERS = B // LANES


def iotas(shape):
    return lax.broadcasted_iota(jnp.int32, shape, 0), lax.broadcasted_iota(jnp.int32, shape, 1)


def pack_kernel(roots_ref, out_ref):
    k = pl.program_id(0)
    devices = out_ref.shape[0]
    row, col = iotas((B, LANES))
    diag_row, diag_col = iotas((LANES, LANES))
    diag_parts = []
    for q in range(QUARTERS):
        cols = slice(q * LANES, (q + 1) * LANES)
        left = roots_ref[0, 0, 0, 0, :, cols]
        right = roots_ref[0, 0, 0, 1, :, cols]
        mixed = jnp.where(row <= col + q * LANES, left, right).astype(jnp.bfloat16)
        out_ref[:, QUARTERS * k + q] = mixed.reshape(devices, ROWS, LANES)
        square = roots_ref[0, 0, 0, 1, cols, cols]
        diag_parts.append(jnp.sum(jnp.where(diag_row == diag_col, square, 0.0), axis=1, keepdims=True))
    diagonal = jnp.broadcast_to(jnp.concatenate(diag_parts, axis=0), (B, LANES))
    diagonal = diagonal.astype(jnp.bfloat16).reshape(devices, ROWS, LANES)
    lane = lax.broadcasted_iota(jnp.int32, (devices, ROWS, LANES), 2)
    last = out_ref.shape[1] - 1

    @pl.when(k == 0)
    def _():
        out_ref[:, last] = diagonal

    @pl.when(k != 0)
    def _():
        out_ref[:, last] = jnp.where(lane // 32 == k, diagonal, out_ref[:, last])


def pack(roots, devices):
    slots = roots.shape[2]
    tiles = QUARTERS * slots + 1
    return pl.pallas_call(
        pack_kernel,
        grid=(slots,),
        in_specs=[pl.BlockSpec((1, 1, 1, 2, B, B), lambda k: (0, 0, k, 0, 0, 0))],
        out_specs=pl.BlockSpec((devices, tiles, ROWS, LANES), lambda k: (0, 0, 0, 0)),
        out_shape=jax.ShapeDtypeStruct((devices, tiles, ROWS, LANES), jnp.bfloat16),
        compiler_params=pltpu.CompilerParams(vmem_limit_bytes=24 * 1024 * 1024),
        cost_estimate=pl.CostEstimate(flops=0, bytes_accessed=8 * 1024 * 1024, transcendentals=0),
    )(roots)


def pick_kernel(owner_ref, slot_ref, in_ref, out_ref):
    last = in_ref.shape[1] - 1

    def one(c, carry):
        o = owner_ref[c]
        s = slot_ref[c]
        for q in range(QUARTERS):
            out_ref[c, q] = in_ref[o, QUARTERS * s + q]
        out_ref[c, QUARTERS] = in_ref[o, last]
        return carry

    lax.fori_loop(0, out_ref.shape[0], one, 0)


def pick(owner_row, slot_rank, pieces):
    cols = owner_row.shape[0]
    return pl.pallas_call(
        pick_kernel,
        in_specs=[
            pl.BlockSpec(memory_space=pltpu.SMEM),
            pl.BlockSpec(memory_space=pltpu.SMEM),
            pl.BlockSpec(memory_space=pltpu.VMEM),
        ],
        out_specs=pl.BlockSpec(memory_space=pltpu.VMEM),
        out_shape=jax.ShapeDtypeStruct((cols, QUARTERS + 1, ROWS, LANES), jnp.bfloat16),
        compiler_params=pltpu.CompilerParams(vmem_limit_bytes=16 * 1024 * 1024),
        cost_estimate=pl.CostEstimate(flops=0, bytes_accessed=3 * 1024 * 1024, transcendentals=0),
    )(owner_row, slot_rank, pieces)


def unpack_kernel(slot_ref, in_ref, left_ref, right_ref):
    slot = slot_ref[0]
    row, col = iotas((LANES, LANES))
    for i in range(QUARTERS):
        rows = slice(i * LANES, (i + 1) * LANES)
        chunk = LANES // ROWS
        members = slice(i * chunk, (i + 1) * chunk)
        tile = in_ref[members, QUARTERS].reshape(LANES, LANES).astype(jnp.float32)
        diagonal = jnp.sum(jnp.where(col == slot * 32, tile, 0.0), axis=1, keepdims=True)
        for j in range(i, QUARTERS):
            cols = slice(j * LANES, (j + 1) * LANES)
            upper = in_ref[members, j].reshape(LANES, LANES).astype(jnp.float32)
            if i == j:
                turned = upper.T
                left_ref[rows, cols] = jnp.where(row <= col, upper, turned).astype(jnp.bfloat16)
                right = jnp.where(row > col, upper, turned)
                right_ref[rows, cols] = jnp.where(row == col, diagonal, right).astype(jnp.bfloat16)
            else:
                others = slice(j * chunk, (j + 1) * chunk)
                lower = in_ref[others, i].reshape(LANES, LANES).astype(jnp.float32)
                left_ref[rows, cols] = upper.astype(jnp.bfloat16)
                left_ref[cols, rows] = upper.T.astype(jnp.bfloat16)
                right_ref[cols, rows] = lower.astype(jnp.bfloat16)
                right_ref[rows, cols] = lower.T.astype(jnp.bfloat16)


def unpack(slot, pieces):
    whole = jax.ShapeDtypeStruct((B, B), jnp.bfloat16)
    return pl.pallas_call(
        unpack_kernel,
        in_specs=[pl.BlockSpec(memory_space=pltpu.SMEM), pl.BlockSpec(memory_space=pltpu.VMEM)],
        out_specs=[pl.BlockSpec(memory_space=pltpu.VMEM)] * 2,
        out_shape=[whole, whole],
        compiler_params=pltpu.CompilerParams(vmem_limit_bytes=16 * 1024 * 1024),
        cost_estimate=pl.CostEstimate(flops=0, bytes_accessed=2 * 1024 * 1024, transcendentals=0),
    )(slot, pieces)


def finish_kernel(grad_ref, moment_ref, left_ref, right_ref, direction_ref, moment_out_ref):
    gradient = grad_ref[...]
    grad_float = gradient.astype(jnp.float32)
    moment_new = moment_decay * moment_ref[...] + (1.0 - moment_decay) * grad_float * grad_float
    moment_out_ref[...] = moment_new
    adam_step = grad_float / (jnp.sqrt(moment_new) + adam_offset)
    target = jnp.sqrt(jnp.sum(adam_step * adam_step))
    left_part = jnp.dot(left_ref[...], gradient, preferred_element_type=jnp.float32)
    conditioned = jnp.dot(
        left_part.astype(jnp.bfloat16), right_ref[...], preferred_element_type=jnp.float32
    )
    scale = target / jnp.sqrt(jnp.sum(conditioned * conditioned) + norm_offset)
    direction_ref[...] = (conditioned * scale).astype(jnp.bfloat16)


def finish(gradient, moment, left, right):
    return pl.pallas_call(
        finish_kernel,
        in_specs=[pl.BlockSpec(memory_space=pltpu.VMEM)] * 4,
        out_specs=[pl.BlockSpec(memory_space=pltpu.VMEM)] * 2,
        out_shape=[
            jax.ShapeDtypeStruct((B, B), jnp.bfloat16),
            jax.ShapeDtypeStruct((B, B), jnp.float32),
        ],
        compiler_params=pltpu.CompilerParams(vmem_limit_bytes=32 * 1024 * 1024),
        cost_estimate=pl.CostEstimate(
            flops=4 * B * B * B, bytes_accessed=5 * 1024 * 1024, transcendentals=0
        ),
    )(gradient, moment, left, right)


def body(partials, moment, owner, roots):
    devices = lax.axis_size("shard")
    gradient = lax.psum_scatter(partials, "rep", scatter_dimension=1, tiled=True)[0]
    owner_row = owner[0]
    block_ids = jnp.arange(owner_row.shape[0], dtype=jnp.int32)
    earlier = block_ids[None, :] < block_ids[:, None]
    same_owner = owner_row[:, None] == owner_row[None, :]
    slot_rank = jnp.sum((same_owner & earlier).astype(jnp.int32), axis=1)
    own_slot = lax.dynamic_slice_in_dim(slot_rank, lax.axis_index("shard"), 1)
    packed = pack(roots, devices)
    pieces = lax.all_to_all(packed, "shard", split_axis=0, concat_axis=0, tiled=True)
    picked = pick(owner_row, slot_rank, pieces)
    arrived = lax.all_to_all(picked, "shard", split_axis=0, concat_axis=0, tiled=True)
    left, right = unpack(own_slot, arrived)
    return tuple(finish(gradient, moment, left, right))


def solution(mesh):
    placed = (
        P("rep", None, "shard"),
        P("rep", "shard"),
        P("rep", None),
        P("rep", "shard", None, None, None, None),
    )
    return jax.shard_map(
        body,
        mesh=mesh,
        in_specs=placed,
        out_specs=(P("rep", "shard"), P("rep", "shard")),
        check_vma=False,
    )
```

time: 255 us -> 80.4 us (0.32)
  blocking collectives: 80.5 us -> 0 us
  waiting for transfers between devices: 102 us -> 41.2 us
  local copies, waits for them, and re-layouts: 21.3 us -> 4.41 us
  matrix products: 10.5 us -> 0 us
  other arithmetic: 7.58 us -> 0.18 us
  Pallas kernels: 0 us -> 7.13 us
  starting transfers between devices: 18.2 us -> 13 us
    unnamed x1 -> x0, blocking collectives: 65.3 us -> none
    reduce_scatter x1, waiting for transfers between devices: 61.5 us -> 4.16 us  [body(): lax.psum_scatter(partials, 'rep', scatter_dimension=1, tiled=True)[0]]
    all_to_all x1 -> x0, blocking collectives: 15.3 us -> none  [body(): lax.all_to_all(picked, 'shard', split_axis=0, concat_axis=2, tiled=True)[0]]
    dot_general x2 -> x0, matrix products: 10.5 us -> none  [the longest x1 5.75 us: precondition(): jnp.einsum('kij,kjl->kil', left_part, root_pairs[:, 1], precision=lax.Pre...]
    unnamed x21 -> x8, local copies, waits for them, and re-layouts: 11.3 us -> 3.83 us
    pallas_call x0 -> x4, Pallas kernels: none -> 7.13 us  [the longest x1 2.41 us: finish(): pl.pallas_call(finish_kernel, in_specs=[pl.BlockSpec(memory_space=pltpu.V...]
    all_to_all x3 -> x2, starting transfers between devices: 18.1 us -> 13 us  [the longest x1 8.72 us: body(): lax.all_to_all(packed, 'shard', split_axis=0, concat_axis=0, tiled=True)]
    unnamed x2 -> x0, other arithmetic: 3.82 us -> none
  transfers between devices with their start and end apart: 4 -> 3, of which waited for: 3 -> 3; matrix products, arithmetic and copies ran while one was open for 5% -> 1% of each run, Pallas kernels for 0% -> 6%
where the time goes in v1:
time: 80.4 us; the launch traced here: 80 us
  waiting for transfers between devices  41.2 us (51%)
  between operations  14.1 us (18%)
  starting transfers between devices  13 us (16%)
  Pallas kernels  7.13 us (9%)
  local copies, waits for them, and re-layouts  4.41 us (5%)
    all_to_all x1, waiting for transfers between devices, body(): lax.all_to_all(packed, 'shard', split_axis=0, concat_axis=0, tiled=True)  23.9 us
    all_to_all x1, waiting for transfers between devices, body(): lax.all_to_all(picked, 'shard', split_axis=0, concat_axis=0, tiled=True)  12.5 us
    all_to_all x1, starting transfers between devices, body(): lax.all_to_all(packed, 'shard', split_axis=0, concat_axis=0, tiled=True)  8.72 us
    all_to_all x1, starting transfers between devices, body(): lax.all_to_all(picked, 'shard', split_axis=0, concat_axis=0, tiled=True)  4.29 us
    reduce_scatter x1, waiting for transfers between devices, body(): lax.psum_scatter(partials, 'rep', scatter_dimension=1, tiled=True)[0]  4.16 us
    unnamed x8, local copies, waits for them, and re-layouts  3.83 us
    pallas_call x1, Pallas kernels, finish(): pl.pallas_call(finish_kernel, in_specs=[pl.BlockSpec(memory_space=pltpu.V...  2.41 us
    pallas_call x1, Pallas kernels, pack(): pl.pallas_call(pack_kernel, grid=(slots,), in_specs=[pl.BlockSpec((1, 1,...  2.14 us
  transfers between devices with their start and end apart: 3, of which 3 were waited for; matrix products, arithmetic and copies ran while one was open for 1% of the time, Pallas kernels for 6%

profile of v1, /device:TPU:1, one launch (start us, length us, event | category | flops | bytes accessed | tf_op | source)
XLA Modules:
  0.0 80.0 jit_solution(11452456997889634819)
XLA Ops:
  7.2 0.0 reduce-scatter.2.cloned.1.call-start
  7.2 0.7 reduce-scatter.2.cloned.1.call-update
  7.9 0.0 copy-start
  7.9 2.8 %copy-done = f32[1,1,3,2,512,512]{5,4,3,2,1,0:T(8,128)S(1)} copy-done((f32[1,1,3,2,512,512]{5,4,3,2,1,0:T(8,128)S(1)}, f32[1,1,3,2,512,512]{5,4,3,2,1,0:T(8,128)}, u32[]{:S(2)}) %copy-start) | copy-done | bytes 6291480
  10.7 0.0 copy-start.3
  10.7 2.1 %shard_map.59 = bf16[32,13,16,128]{3,2,1,0:T(8,128)(2,1)} custom-call(f32[1,1,3,2,512,512]{5,4,3,2,1,0:T(8,128)S(1)} %copy-done), custom_call_target="tpu_custom_call" | custom-call | bytes 8388608 | tf_op jit(solution)/shard_map/pallas_call | solution.py:53
  12.8 0.0 copy-start.1
  12.8 8.7 %all-to-all-start = ((bf16[32,13,16,128]{3,2,1,0:T(8,128)(2,1)}), bf16[32,13,16,128]{3,2,1,0:T(8,128)(2,1)S(1)}, u32[]{:S(2)}, u32[]{:S(2)}) async-start(bf16[32,13,16,128]{3,2,1,0:T(8,128)(2,1)} %shard_map.59), calls=%async_computation.1 | async-start | bytes 3407872 | tf_op jit(solution)/shard_map/all_to_all | solution.py:173
  21.6 0.0 copy-done.3
  21.6 0.2 convert_reduce_fusion.slot_ref
  21.7 23.9 %all-to-all-done.in_ref = bf16[32,13,16,128]{3,2,1,0:T(8,128)(2,1)S(1)} async-done(((bf16[32,13,16,128]{3,2,1,0:T(8,128)(2,1)}), bf16[32,13,16,128]{3,2,1,0:T(8,128)(2,1)S(1)}, u32[]{:S(2)}, u32[]{:S(2)}) %all-to-all-start) | async-done | bytes 1703968 | tf_op jit(solution)/shard_map/all_to_all | solution.py:173
  45.6 1.6 %shard_map.60 = bf16[32,5,16,128]{3,2,1,0:T(8,128)(2,1)} custom-call(s32[32]{0:T(128)S(1)} %bitcast.4, s32[32]{0:T(128)S(1)} %convert_reduce_fusion.slot_ref, bf16[32,13,16,128]{3,2,1,0:T(8,128)(2,1)S(1)} %all-to-all-done.in_ref), custom_call_target="tpu_custom_call" | custom-call | bytes 3145728 | tf_op jit(solution)/shard_map/pallas_call | solution.py:80
  47.3 4.3 %all-to-all-start.1 = ((bf16[32,5,16,128]{3,2,1,0:T(8,128)(2,1)}), bf16[32,5,16,128]{3,2,1,0:T(8,128)(2,1)S(1)}, u32[]{:S(2)}, u32[]{:S(2)}) async-start(bf16[32,5,16,128]{3,2,1,0:T(8,128)(2,1)} %shard_map.60), calls=%async_computation.2 | async-start | bytes 1310720 | tf_op jit(solution)/shard_map/all_to_all | solution.py:175
  51.6 0.6 dynamic_slice.3.slot_ref
  52.2 12.5 %all-to-all-done.1.in_ref = bf16[32,5,16,128]{3,2,1,0:T(8,128)(2,1)S(1)} async-done(((bf16[32,5,16,128]{3,2,1,0:T(8,128)(2,1)}), bf16[32,5,16,128]{3,2,1,0:T(8,128)(2,1)S(1)}, u32[]{:S(2)}, u32[]{:S(2)}) %all-to-all-start.1) | async-done | bytes 655392 | tf_op jit(solution)/shard_map/all_to_all | solution.py:175
  64.6 0.9 %shard_map.61 = (bf16[512,512]{1,0:T(8,128)(2,1)S(1)}, bf16[512,512]{1,0:T(8,128)(2,1)S(1)}) custom-call(s32[1]{0:T(128)} %dynamic_slice.3.slot_ref, bf16[32,5,16,128]{3,2,1,0:T(8,128)(2,1)S(1)} %all-to-all-done.1.in_ref), custom_call_target="tpu_custom_call" | custom-call | bytes 2097152 | tf_op jit(solution)/shard_map/pallas_call | solution.py:122
  65.6 4.2 %reduce-scatter.2.cloned.1.call-done = bf16[1,512,512]{2,1,0:T(8,128)(2,1)} async-done(((bf16[1,4096,512]{2,1,0:T(8,128)(2,1)}), bf16[1,512,512]{2,1,0:T(8,128)(2,1)}) %reduce-scatter.2.cloned.1.call-update) | async-done | bytes 524304 | tf_op jit(solution)/shard_map/reduce_scatter | solution.py:165
  69.7 0.0 copy-done.1
  69.7 0.0 copy-start.2
  69.7 1.0 %copy-done.2 = bf16[1,512,512]{2,1,0:T(8,128)(2,1)S(1)} copy-done((bf16[1,512,512]{2,1,0:T(8,128)(2,1)S(1)}, bf16[1,512,512]{2,1,0:T(8,128)(2,1)}, u32[]{:S(2)}) %copy-start.2) | copy-done | bytes 524312
  70.8 2.4 %shard_map.62 = (bf16[512,512]{1,0:T(8,128)(2,1)}, f32[512,512]{1,0:T(8,128)}) custom-call(bf16[512,512]{1,0:T(8,128)(2,1)S(1)} %bitcast.2, f32[512,512]{1,0:T(8,128)S(1)} %copy-done.1, bf16[512,512]{1,0:T(8,128)(2,1)S(1)} %get-tuple-element.4.left_ref, bf16[512,512]{1,0:T(8,128)(2,1)S(1)} %get-tuple-element.5.right_ref), custom_call_target="tpu_custom_call" | custom-call | flops 536870912 | bytes 5242880 | tf_op jit(solution)/shard_map/pallas_call | solution.py:148
Async XLA Ops:
  7.2 62.6 %reduce-scatter.2.cloned.1.call-start = ((), (), s32[]{:S(2)}) async-start(), calls=%async_computation.3 | async-start | bytes 4718592 | tf_op jit(solution)/shard_map/reduce_scatter | solution.py:165
  7.9 2.8 %copy-start = (f32[1,1,3,2,512,512]{5,4,3,2,1,0:T(8,128)S(1)}, f32[1,1,3,2,512,512]{5,4,3,2,1,0:T(8,128)}, u32[]{:S(2)}) copy-start(f32[1,1,3,2,512,512]{5,4,3,2,1,0:T(8,128)} %roots_ref.1) | copy-start | bytes 18874372
  10.7 10.9 %copy-start.3 = (s32[1,32]{1,0:T(1,128)S(1)}, s32[1,32]{1,0:T(1,128)}, u32[]{:S(2)}) copy-start(s32[1,32]{1,0:T(1,128)} %param.6) | copy-start | bytes 388
  12.8 56.9 %copy-start.1 = (f32[512,512]{1,0:T(8,128)S(1)}, f32[512,512]{1,0:T(8,128)}, u32[]{:S(2)}) copy-start(f32[512,512]{1,0:T(8,128)} %moment_ref.1) | copy-start | bytes 3145732
  12.8 32.8 %all-to-all-start = ((bf16[32,13,16,128]{3,2,1,0:T(8,128)(2,1)}), bf16[32,13,16,128]{3,2,1,0:T(8,128)(2,1)S(1)}, u32[]{:S(2)}, u32[]{:S(2)}) async-start(bf16[32,13,16,128]{3,2,1,0:T(8,128)(2,1)} %shard_map.59), calls=%async_computation.1 | async-start | bytes 3407872 | tf_op jit(solution)/shard_map/all_to_all | solution.py:173
  47.3 17.3 %all-to-all-start.1 = ((bf16[32,5,16,128]{3,2,1,0:T(8,128)(2,1)}), bf16[32,5,16,128]{3,2,1,0:T(8,128)(2,1)S(1)}, u32[]{:S(2)}, u32[]{:S(2)}) async-start(bf16[32,5,16,128]{3,2,1,0:T(8,128)(2,1)} %shard_map.60), calls=%async_computation.2 | async-start | bytes 1310720 | tf_op jit(solution)/shard_map/all_to_all | solution.py:175
  69.7 1.0 %copy-start.2 = (bf16[1,512,512]{2,1,0:T(8,128)(2,1)S(1)}, bf16[1,512,512]{2,1,0:T(8,128)(2,1)}, u32[]{:S(2)}) copy-start(bf16[1,512,512]{2,1,0:T(8,128)(2,1)} %reduce-scatter.2.cloned.1.call-done) | copy-start | bytes 1572868
Sparse Core Ops, SparseCore 0:
  10.5 59.1 reduce-scatter.1

commit v2 on v1

v2 whole, which is shorter than its diff:
```python
import jax
import jax.numpy as jnp
from jax import lax
from jax.experimental import pallas as pl
from jax.experimental.pallas import tpu as pltpu
from jax.sharding import PartitionSpec as P

moment_decay = 0.95
adam_offset = 1e-08
norm_offset = 1e-06

B = 512
ROWS = 16
FULL = 60 * 1024 * 1024
LANES = 128
QUARTERS = B // LANES


def iotas(shape):
    return lax.broadcasted_iota(jnp.int32, shape, 0), lax.broadcasted_iota(jnp.int32, shape, 1)


def pack_kernel(roots_ref, out_ref, held, sems):
    slots = roots_ref.shape[2]
    devices, tiles = out_ref.shape[:2]
    rows = B // PARTS
    members = devices // PARTS
    copies = []
    for k in range(slots):
        for p in range(PARTS):
            copies.append(
                pltpu.make_async_copy(
                    roots_ref.at[0, 0, k, :, p * rows : (p + 1) * rows, :],
                    held.at[k, :, p * rows : (p + 1) * rows, :],
                    sems.at[k, p],
                )
            )
    for copy in copies:
        copy.start()
    row, col = iotas((rows, LANES))
    diag_row, diag_col = iotas((LANES, LANES))
    lane = lax.broadcasted_iota(jnp.int32, (rows, LANES), 1)
    diagonal = [jnp.zeros((rows, LANES), jnp.float32)] * PARTS
    for k in range(slots):
        for p in range(PARTS):
            copies[k * PARTS + p].wait()
            here = slice(p * rows, (p + 1) * rows)
            group = slice(p * members, (p + 1) * members)
            parts = []
            for q in range(QUARTERS):
                cols = slice(q * LANES, (q + 1) * LANES)
                left = held[k, 0, here, cols]
                right = held[k, 1, here, cols]
                mixed = jnp.where(row + p * rows <= col + q * LANES, left, right)
                out_ref[group, QUARTERS * k + q] = mixed.astype(jnp.bfloat16).reshape(
                    members, ROWS, LANES
                )
                if p * rows <= q * LANES < (p + 1) * rows:
                    square = held[k, 1, q * LANES : (q + 1) * LANES, cols]
                    parts.append(
                        jnp.sum(jnp.where(diag_row == diag_col, square, 0.0), axis=1, keepdims=True)
                    )
            spread = jnp.broadcast_to(jnp.concatenate(parts, axis=0), (rows, LANES))
            diagonal[p] = jnp.where(lane // 32 == k, spread, diagonal[p])
    for p in range(PARTS):
        out_ref[p * members : (p + 1) * members, tiles - 1] = (
            diagonal[p].astype(jnp.bfloat16).reshape(members, ROWS, LANES)
        )


PARTS = 2
PACKCOST = 0


def pack(roots, devices):
    slots = roots.shape[2]
    tiles = QUARTERS * slots + 1
    return pl.pallas_call(
        pack_kernel,
        in_specs=[pl.BlockSpec(memory_space=pl.ANY)],
        out_specs=pl.BlockSpec(memory_space=pltpu.VMEM),
        out_shape=jax.ShapeDtypeStruct((devices, tiles, ROWS, LANES), jnp.bfloat16),
        scratch_shapes=[
            pltpu.VMEM((slots, 2, B, B), jnp.float32),
            pltpu.SemaphoreType.DMA((slots, PARTS)),
        ],
        compiler_params=pltpu.CompilerParams(vmem_limit_bytes=58 * 1024 * 1024),
        cost_estimate=pl.CostEstimate(flops=PACKCOST, bytes_accessed=8 * 1024 * 1024, transcendentals=0),
        name="pack",
    )(roots)


def pick_kernel(owner_ref, in_ref, out_ref, counts):
    devices, tiles = in_ref.shape[:2]
    lane = lax.broadcasted_iota(jnp.int32, (ROWS, LANES), 1)
    for o in range(devices):
        counts[o] = 0
    for c in range(out_ref.shape[0]):
        o = owner_ref[0, c]
        slot = counts[o]
        counts[o] = slot + 1
        for q in range(QUARTERS):
            out_ref[c, q] = in_ref[o, QUARTERS * slot + q]
        diagonal = in_ref[o, tiles - 1].astype(jnp.float32)
        kept = jnp.where(lane == slot * 32, diagonal, 0.0)
        out_ref[c, QUARTERS] = kept.astype(jnp.bfloat16)


def pick(owner, pieces):
    cols = owner.shape[1]
    return pl.pallas_call(
        pick_kernel,
        in_specs=[pl.BlockSpec(memory_space=pltpu.SMEM), pl.BlockSpec(memory_space=pltpu.VMEM)],
        out_specs=pl.BlockSpec(memory_space=pltpu.VMEM),
        out_shape=jax.ShapeDtypeStruct((cols, QUARTERS + 1, ROWS, LANES), jnp.bfloat16),
        scratch_shapes=[pltpu.SMEM((pieces.shape[0],), jnp.int32)],
        compiler_params=pltpu.CompilerParams(vmem_limit_bytes=8 * 1024 * 1024),
        cost_estimate=pl.CostEstimate(flops=0, bytes_accessed=3 * 1024 * 1024, transcendentals=0),
        name="pick",
    )(owner, pieces)


def unpack_kernel(in_ref, left_ref, right_ref):
    row, col = iotas((LANES, LANES))
    for i in range(QUARTERS):
        rows = slice(i * LANES, (i + 1) * LANES)
        chunk = LANES // ROWS
        members = slice(i * chunk, (i + 1) * chunk)
        tile = in_ref[members, QUARTERS].reshape(LANES, LANES).astype(jnp.float32)
        diagonal = jnp.sum(tile, axis=1, keepdims=True)
        for j in range(i, QUARTERS):
            cols = slice(j * LANES, (j + 1) * LANES)
            upper = in_ref[members, j].reshape(LANES, LANES).astype(jnp.float32)
            if i == j:
                turned = upper.T
                left_ref[rows, cols] = jnp.where(row <= col, upper, turned).astype(jnp.bfloat16)
                right = jnp.where(row > col, upper, turned)
                right_ref[rows, cols] = jnp.where(row == col, diagonal, right).astype(jnp.bfloat16)
            else:
                others = slice(j * chunk, (j + 1) * chunk)
                lower = in_ref[others, i].reshape(LANES, LANES).astype(jnp.float32)
                left_ref[rows, cols] = upper.astype(jnp.bfloat16)
                left_ref[cols, rows] = upper.T.astype(jnp.bfloat16)
                right_ref[cols, rows] = lower.astype(jnp.bfloat16)
                right_ref[rows, cols] = lower.T.astype(jnp.bfloat16)


def unpack(pieces):
    whole = jax.ShapeDtypeStruct((B, B), jnp.bfloat16)
    return pl.pallas_call(
        unpack_kernel,
        in_specs=[pl.BlockSpec(memory_space=pltpu.VMEM)],
        out_specs=[pl.BlockSpec(memory_space=pltpu.VMEM)] * 2,
        out_shape=[whole, whole],
        compiler_params=pltpu.CompilerParams(vmem_limit_bytes=8 * 1024 * 1024),
        cost_estimate=pl.CostEstimate(flops=0, bytes_accessed=2 * 1024 * 1024, transcendentals=0),
        name="unpack",
    )(pieces)


def finish_kernel(
    own_ref, up_ref, down_ref, up_last_ref, down_last_ref, moment_ref, left_ref, right_ref,
    direction_ref, moment_out_ref,
):
    own = own_ref[...].astype(jnp.float32)
    up = jnp.concatenate([up_last_ref[...], up_ref[HALF:]], axis=0).astype(jnp.float32)
    down = jnp.concatenate([down_ref[:HALF], down_last_ref[...]], axis=0).astype(jnp.float32)
    gradient = (own + up + down).astype(jnp.bfloat16)
    grad_float = gradient.astype(jnp.float32)
    moment_new = moment_decay * moment_ref[...] + (1.0 - moment_decay) * grad_float * grad_float
    moment_out_ref[...] = moment_new
    adam_step = grad_float / (jnp.sqrt(moment_new) + adam_offset)
    target = jnp.sqrt(jnp.sum(adam_step * adam_step))
    left_part = jnp.dot(left_ref[...], gradient, preferred_element_type=jnp.float32)
    conditioned = jnp.dot(
        left_part.astype(jnp.bfloat16), right_ref[...], preferred_element_type=jnp.float32
    )
    scale = target / jnp.sqrt(jnp.sum(conditioned * conditioned) + norm_offset)
    direction_ref[...] = (conditioned * scale).astype(jnp.bfloat16)


def finish(sums, moment, left, right):
    return pl.pallas_call(
        finish_kernel,
        in_specs=[pl.BlockSpec(memory_space=pltpu.VMEM)] * 8,
        out_specs=[pl.BlockSpec(memory_space=pltpu.VMEM)] * 2,
        out_shape=[
            jax.ShapeDtypeStruct((B, B), jnp.bfloat16),
            jax.ShapeDtypeStruct((B, B), jnp.float32),
        ],
        compiler_params=pltpu.CompilerParams(vmem_limit_bytes=24 * 1024 * 1024),
        cost_estimate=pl.CostEstimate(
            flops=4 * B * B * B, bytes_accessed=5 * 1024 * 1024, transcendentals=0
        ),
    )(*sums, moment, left, right)


HALF = B // 2


def reduce_chunks(partials, packed):
    groups = lax.axis_size("rep")
    pairs_up = [(k, (k + 1) % groups) for k in range(groups)]
    pairs_down = [(k, (k - 1) % groups) for k in range(groups)]

    def move(up, down):
        return lax.ppermute(up, "rep", pairs_up), lax.ppermute(down, "rep", pairs_down)

    def mine(offset, start=0, rows=B):
        chunk = lax.rem(lax.axis_index("rep") + offset + groups, groups)
        return lax.dynamic_slice(partials, (chunk * B + start, 0), (rows, B))

    def add(a, b):
        return (a.astype(jnp.float32) + b.astype(jnp.float32)).astype(jnp.bfloat16)

    def pair(first, second):
        return mine(first, 0, HALF), mine(second, HALF, HALF)

    def join(arrived, parts):
        return jnp.concatenate([add(arrived[:HALF], parts[0]), add(arrived[HALF:], parts[1])])

    up, down = move(jnp.concatenate(pair(4, 3)), jnp.concatenate(pair(-3, -4)))
    up, down, packed = lax.optimization_barrier((up, down, packed))
    up, down = move(*lax.optimization_barrier((join(up, pair(3, 2)), join(down, pair(-2, -3)))))
    up, down = lax.optimization_barrier((up, down))
    up, down = move(*lax.optimization_barrier((join(up, pair(2, 1)), join(down, pair(-1, -2)))))
    up, down = lax.optimization_barrier((up, down))
    up_last, down_last = move(
        *lax.optimization_barrier(
            (add(up[:HALF], mine(1, 0, HALF)), add(down[HALF:], mine(-1, HALF, HALF)))
        )
    )
    return (mine(0), up, down, up_last, down_last), packed


def body(partials, moment, owner, roots):
    devices = lax.axis_size("shard")
    packed = pack(roots, devices)
    sums, _ = reduce_chunks(partials[0], packed)
    pieces = lax.all_to_all(packed, "shard", split_axis=0, concat_axis=0, tiled=True)
    picked = pick(owner, pieces)
    arrived = lax.all_to_all(picked, "shard", split_axis=0, concat_axis=0, tiled=True)
    left, right = unpack(arrived)
    return tuple(finish(sums, moment, left, right))


def solution(mesh):
    placed = (
        P("rep", None, "shard"),
        P("rep", "shard"),
        P("rep", None),
        P("rep", "shard", None, None, None, None),
    )
    return jax.shard_map(
        body,
        mesh=mesh,
        in_specs=placed,
        out_specs=(P("rep", "shard"), P("rep", "shard")),
        check_vma=False,
    )
```

time: 80.4 us -> 70.3 us (0.87)
  waiting for transfers between devices: 41.2 us -> 22.3 us
  starting transfers between devices: 13 us -> 28.9 us
  between operations: 14.1 us -> 0.85 us
  other arithmetic: 0.18 us -> 5.46 us
  Pallas kernels: 7.13 us -> 8.75 us
  local copies, waits for them, and re-layouts: 4.41 us -> 3.57 us
    all_to_all x1, waiting for transfers between devices: 23.9 us -> 2.65 us  [body(): lax.all_to_all(packed, 'shard', split_axis=0, concat_axis=0, tiled=True)]
    ppermute x0 -> x8, starting transfers between devices: none -> 14.8 us  [the longest x4 10.1 us: move(): lax.ppermute(down, 'rep', pairs_down)]
    ppermute x0 -> x8, waiting for transfers between devices: none -> 12.4 us  [the longest x4 12.3 us: move(): lax.ppermute(up, 'rep', pairs_up)]
    all_to_all x1, waiting for transfers between devices: 12.5 us -> 7.27 us  [body(): lax.all_to_all(picked, 'shard', split_axis=0, concat_axis=0, tiled=True)]
    convert_element_type x0 -> x3, other arithmetic: none -> 4.45 us  [add(): return (a.astype(jnp.float32) + b.astype(jnp.float32)).astype(jnp.bfloat16)]
    reduce_scatter x1 -> x0, waiting for transfers between devices: 4.16 us -> none  [body(): lax.psum_scatter(partials, 'rep', scatter_dimension=1, tiled=True)[0]]
    unnamed x8 -> x4, local copies, waits for them, and re-layouts: 3.83 us -> 1.23 us
    all_to_all x1, starting transfers between devices: 4.29 us -> 6.11 us  [body(): lax.all_to_all(picked, 'shard', split_axis=0, concat_axis=0, tiled=True)]
  transfers between devices with their start and end apart: 3 -> 10, of which waited for: 3 -> 4; matrix products, arithmetic and copies ran while one was open for 1% -> 9% of each run, Pallas kernels for 6% -> 9%
where the time goes in v2:
time: 70.3 us; the launch traced here: 69.8 us
  starting transfers between devices  28.9 us (41%)
  waiting for transfers between devices  22.3 us (32%)
  Pallas kernels  8.75 us (12%)
  other arithmetic  5.46 us (8%)
  local copies, waits for them, and re-layouts  3.57 us (5%)
  between operations  0.85 us (1%)
    ppermute x4, waiting for transfers between devices, move(): lax.ppermute(up, 'rep', pairs_up)  12.3 us
    ppermute x4, starting transfers between devices, move(): lax.ppermute(down, 'rep', pairs_down)  10.1 us
    all_to_all x1, starting transfers between devices, body(): lax.all_to_all(packed, 'shard', split_axis=0, concat_axis=0, tiled=True)  8.05 us
    all_to_all x1, waiting for transfers between devices, body(): lax.all_to_all(picked, 'shard', split_axis=0, concat_axis=0, tiled=True)  7.27 us
    all_to_all x1, starting transfers between devices, body(): lax.all_to_all(picked, 'shard', split_axis=0, concat_axis=0, tiled=True)  6.11 us
    ppermute x4, starting transfers between devices, move(): lax.ppermute(up, 'rep', pairs_up)  4.67 us
    convert_element_type x3, other arithmetic, add(): return (a.astype(jnp.float32) + b.astype(jnp.float32)).astype(jnp.bfloat16)  4.45 us
    pallas_call x1, Pallas kernels, pack(): pl.pallas_call(pack_kernel, in_specs=[pl.BlockSpec(memory_space=pl.ANY)],...  4.27 us
  transfers between devices with their start and end apart: 10, of which 4 were waited for; matrix products, arithmetic and copies ran while one was open for 9% of the time, Pallas kernels for 9%

profile of v2, /device:TPU:1, one launch (start us, length us, event | category | flops | bytes accessed | tf_op | source)
XLA Modules:
  0.0 69.8 jit_solution(5253364460252096677)
XLA Ops:
  0.7 1.3 %dynamic-slice_bitcast_fusion.2 = (bf16[256,512]{1,0:T(8,128)(2,1)S(1)}, bf16[256,512]{1,0:T(8,128)(2,1)S(1)}, bf16[256,512]{1,0:T(8,128)(2,1)S(1)}, bf16[256,512]{1,0:T(8,128)(2,1)S(1)}) fusion(bf16[1,4096,512]{2,1,0:T(8,128)(2,1)} %param.4, s32[]{:T(128)S(6)} %select_n.48, s32[]{:T(128)S(6)} %select_n.49, s32[]{:T(128)S(6)} %select_n.47, s32[]{:T(128)S(6)} %select_n.46), kind=kLoop, calls=%fused_computation.28 | loop fusion | bytes 2097168 | tf_op jit(solution)/shard_map/dynamic_slice | solution.py:211
  2.0 2.5 %collective-permute-start = (bf16[512,512]{1,0:T(8,128)(2,1)S(1)}, bf16[512,512]{1,0:T(8,128)(2,1)S(1)}, u32[]{:S(2)}, u32[]{:S(2)}) collective-permute-start(bf16[512,512]{1,0:T(8,128)(2,1)S(1)} %pad_maximum_fusion), channel_id=1, source_target_pairs={{0,32},{32,64},{64,96},{96,128},{128,160},{160,192},{192,224},{224... | collective-permute-start | bytes 1572872 | tf_op jit(solution)/shard_map/ppermute | solution.py:207
  4.6 4.0 %collective-permute-start.1 = (bf16[512,512]{1,0:T(8,128)(2,1)S(1)}, bf16[512,512]{1,0:T(8,128)(2,1)}, u32[]{:S(2)}, u32[]{:S(2)}) collective-permute-start(bf16[512,512]{1,0:T(8,128)(2,1)S(1)} %pad_maximum_fusion.1), channel_id=1, source_target_pairs={{0,224},{32,0},{64,32},{96,64},{128,96},{160,128},{192,160},{224,1... | collective-permute-start | bytes 1572872 | tf_op jit(solution)/shard_map/ppermute | solution.py:207
  8.6 4.3 %pack.1 = bf16[32,13,16,128]{3,2,1,0:T(8,128)(2,1)} custom-call(f32[1,1,3,2,512,512]{5,4,3,2,1,0:T(8,128)} %roots_ref.1), custom_call_target="tpu_custom_call" | custom-call | bytes 8388608 | tf_op jit(solution)/shard_map/pack/pallas_call | solution.py:78
  12.9 8.1 %all-to-all-start = ((bf16[32,13,16,128]{3,2,1,0:T(8,128)(2,1)}), bf16[32,13,16,128]{3,2,1,0:T(8,128)(2,1)S(1)}, u32[]{:S(2)}, u32[]{:S(2)}) async-start(bf16[32,13,16,128]{3,2,1,0:T(8,128)(2,1)} %pack.1), calls=%async_computation | async-start | bytes 3407872 | tf_op jit(solution)/shard_map/all_to_all | solution.py:240
  21.0 0.0 collective-permute-done
  21.0 0.0 collective-permute-done.1
  21.0 1.6 %fusion.7 = (bf16[256,512]{1,0:T(8,128)(2,1)S(1)}, bf16[256,512]{1,0:T(8,128)(2,1)S(1)}, bf16[256,512]{1,0:T(8,128)(2,1)S(1)}, bf16[256,512]{1,0:T(8,128)(2,1)S(1)}) fusion(bf16[1,4096,512]{2,1,0:T(8,128)(2,1)} %param.4, s32[]{:T(128)S(6)} %select_n.52, bf16[512,512]{1,0:T(8,128)(2,1)} %collective-permute-done.1, s32[]{:T(128)S(6)} %select_n.53, ...), kind=kLoop, calls=%fused_computation.21 | loop fusion | flops 2097152 | bytes 3145744 | tf_op jit(solution)/shard_map/convert_element_type | solution.py:214
  22.6 0.0 copy-start.1
  22.6 0.1 pad_maximum_fusion.2
  22.7 0.1 collective-permute-start.2
  22.8 2.7 %collective-permute-start.3 = (bf16[512,512]{1,0:T(8,128)(2,1)S(1)}, bf16[512,512]{1,0:T(8,128)(2,1)}, u32[]{:S(2)}, u32[]{:S(2)}) collective-permute-start(bf16[512,512]{1,0:T(8,128)(2,1)S(1)} %get-tuple-element.19), channel_id=1, source_target_pairs={{0,224},{32,0},{64,32},{96,64},{128,96},{160,128},{192,160},{224,1... | collective-permute-start | bytes 1572872 | tf_op jit(solution)/shard_map/ppermute | solution.py:207
  25.5 11.7 %collective-permute-done.2 = bf16[512,512]{1,0:T(8,128)(2,1)S(1)} collective-permute-done((bf16[512,512]{1,0:T(8,128)(2,1)S(1)}, bf16[512,512]{1,0:T(8,128)(2,1)S(1)}, u32[]{:S(2)}, u32[]{:S(2)}) %collective-permute-start.2) | collective-permute-done | bytes 524320 | tf_op jit(solution)/shard_map/ppermute | solution.py:207
  37.2 0.0 collective-permute-done.3
  37.2 1.6 %fusion.3 = (bf16[256,512]{1,0:T(8,128)(2,1)S(1)}, bf16[256,512]{1,0:T(8,128)(2,1)S(1)}, bf16[256,512]{1,0:T(8,128)(2,1)S(1)}, bf16[256,512]{1,0:T(8,128)(2,1)S(1)}) fusion(bf16[1,4096,512]{2,1,0:T(8,128)(2,1)} %param.4, s32[]{:T(128)S(6)} %select_n.56, bf16[512,512]{1,0:T(8,128)(2,1)} %collective-permute-done.3, s32[]{:T(128)S(6)} %select_n.57, ...), kind=kLoop, calls=%fused_computation.13 | loop fusion | flops 2097152 | bytes 3145744 | tf_op jit(solution)/shard_map/convert_element_type | solution.py:214
  38.9 0.8 %pad_maximum_fusion.4 = bf16[512,512]{1,0:T(8,128)(2,1)} fusion(bf16[256,512]{1,0:T(8,128)(2,1)S(1)} %get-tuple-element.40, bf16[256,512]{1,0:T(8,128)(2,1)S(1)} %get-tuple-element.41), kind=kLoop, calls=%fused_computation.4 | loop fusion | flops 1048576 | bytes 1048576 | tf_op jit(solution)/shard_map/concatenate | solution.py:220
  39.7 0.0 collective-permute-start.4
  39.7 2.7 %collective-permute-start.5 = (bf16[512,512]{1,0:T(8,128)(2,1)S(1)}, bf16[512,512]{1,0:T(8,128)(2,1)S(1)}, u32[]{:S(2)}, u32[]{:S(2)}) collective-permute-start(bf16[512,512]{1,0:T(8,128)(2,1)S(1)} %pad_maximum_fusion.5), channel_id=1, source_target_pairs={{0,224},{32,0},{64,32},{96,64},{128,96},{160,128},{192,160},{224,1... | collective-permute-start | bytes 1572872 | tf_op jit(solution)/shard_map/ppermute | solution.py:207
  42.4 2.6 %all-to-all-done.in_ref = bf16[32,13,16,128]{3,2,1,0:T(8,128)(2,1)S(1)} async-done(((bf16[32,13,16,128]{3,2,1,0:T(8,128)(2,1)}), bf16[32,13,16,128]{3,2,1,0:T(8,128)(2,1)S(1)}, u32[]{:S(2)}, u32[]{:S(2)}) %all-to-all-start) | async-done | bytes 1703968 | tf_op jit(solution)/shard_map/all_to_all | solution.py:240
  45.0 0.0 copy-done.1
  45.0 1.5 %pick.1 = bf16[32,5,16,128]{3,2,1,0:T(8,128)(2,1)} custom-call(s32[1,32]{1,0:T(1,128)S(1)} %copy-done.1, bf16[32,13,16,128]{3,2,1,0:T(8,128)(2,1)S(1)} %all-to-all-done.in_ref), custom_call_target="tpu_custom_call" | custom-call | bytes 3145728 | tf_op jit(solution)/shard_map/pick/pallas_call | solution.py:111
  46.6 6.1 %all-to-all-start.1 = ((bf16[32,5,16,128]{3,2,1,0:T(8,128)(2,1)}), bf16[32,5,16,128]{3,2,1,0:T(8,128)(2,1)S(1)}, u32[]{:S(2)}, u32[]{:S(2)}) async-start(bf16[32,5,16,128]{3,2,1,0:T(8,128)(2,1)} %pick.1), calls=%async_computation.1 | async-start | bytes 1310720 | tf_op jit(solution)/shard_map/all_to_all | solution.py:242
  52.7 0.6 collective-permute-done.4.up_ref
  53.3 0.0 collective-permute-done.5.down_ref
  53.3 1.2 %fusion = (bf16[256,512]{1,0:T(8,128)(2,1)S(1)}, bf16[256,512]{1,0:T(8,128)(2,1)S(1)}) fusion(bf16[1,4096,512]{2,1,0:T(8,128)(2,1)} %param.4, s32[]{:T(128)S(6)} %select_n.59, bf16[512,512]{1,0:T(8,128)(2,1)S(1)} %collective-permute-done.5.down_ref, s32[]{:T(128)S(6)} %select_n.58, bf16[512,512]{1,0:T(8,128)(2,1)S(1)} %collective-permute-done.4.up_ref), kind=kLoop, calls=%fused_computation.7 | loop fusion | flops 1048576 | bytes 1572872 | tf_op jit(solution)/shard_map/convert_element_type | solution.py:214
  54.5 2.0 %collective-permute-start.6 = (bf16[256,512]{1,0:T(8,128)(2,1)S(1)}, bf16[256,512]{1,0:T(8,128)(2,1)S(1)}, u32[]{:S(2)}, u32[]{:S(2)}) collective-permute-start(bf16[256,512]{1,0:T(8,128)(2,1)S(1)} %get-tuple-element.26), channel_id=1, source_target_pairs={{0,32},{32,64},{64,96},{96,128},{128,160},{160,192},{192,224},{224... | collective-permute-start | bytes 786440 | tf_op jit(solution)/shard_map/ppermute | solution.py:207
  56.6 0.7 %collective-permute-start.7 = (bf16[256,512]{1,0:T(8,128)(2,1)S(1)}, bf16[256,512]{1,0:T(8,128)(2,1)S(1)}, u32[]{:S(2)}, u32[]{:S(2)}) collective-permute-start(bf16[256,512]{1,0:T(8,128)(2,1)S(1)} %get-tuple-element.27), channel_id=1, source_target_pairs={{0,224},{32,0},{64,32},{96,64},{128,96},{160,128},{192,160},{224,1... | collective-permute-start | bytes 786440 | tf_op jit(solution)/shard_map/ppermute | solution.py:207
  57.3 1.1 %dynamic-slice_bitcast_fusion.own_ref = bf16[512,512]{1,0:T(8,128)(2,1)S(1)} fusion(bf16[1,4096,512]{2,1,0:T(8,128)(2,1)} %param.4, s32[]{:T(128)S(6)} %select_n.45), kind=kLoop, calls=%fused_computation.26 | loop fusion | bytes 1048580 | tf_op jit(solution)/shard_map/dynamic_slice | solution.py:211
  58.4 7.3 %all-to-all-done.1.in_ref = bf16[32,5,16,128]{3,2,1,0:T(8,128)(2,1)S(1)} async-done(((bf16[32,5,16,128]{3,2,1,0:T(8,128)(2,1)}), bf16[32,5,16,128]{3,2,1,0:T(8,128)(2,1)S(1)}, u32[]{:S(2)}, u32[]{:S(2)}) %all-to-all-start.1) | async-done | bytes 655392 | tf_op jit(solution)/shard_map/all_to_all | solution.py:242
  65.6 0.3 unpack.1
  65.9 0.0 collective-permute-done.6.up_last_ref
  65.9 0.0 collective-permute-done.7.down_last_ref
  66.0 0.0 copy-start
  66.0 1.2 %copy-done = f32[512,512]{1,0:T(8,128)S(1)} copy-done((f32[512,512]{1,0:T(8,128)S(1)}, f32[512,512]{1,0:T(8,128)}, u32[]{:S(2)}) %copy-start) | copy-done | bytes 1048600
  67.2 2.6 %shard_map.59 = (bf16[512,512]{1,0:T(8,128)(2,1)}, f32[512,512]{1,0:T(8,128)}) custom-call(bf16[512,512]{1,0:T(8,128)(2,1)S(1)} %dynamic-slice_bitcast_fusion.own_ref, bf16[512,512]{1,0:T(8,128)(2,1)S(1)} %collective-permute-done.4.up_ref, bf16[512,512]{1,0:T(8,128)(2,1)S(1)} %collective-permute-done.5.down_ref, ...), custom_call_target="tpu_custom_call" | custom-call | flops 536870912 | bytes 5242880 | tf_op jit(solution)/shard_map/pallas_call | solution.py:183
  (3 shorter events, 0.1 us)
Async XLA Ops:
  2.0 19.0 %collective-permute-start = (bf16[512,512]{1,0:T(8,128)(2,1)S(1)}, bf16[512,512]{1,0:T(8,128)(2,1)S(1)}, u32[]{:S(2)}, u32[]{:S(2)}) collective-permute-start(bf16[512,512]{1,0:T(8,128)(2,1)S(1)} %pad_maximum_fusion), channel_id=1, source_target_pairs={{0,32},{32,64},{64,96},{96,128},{128,160},{160,192},{192,224},{224... | collective-permute-start | bytes 1572872 | tf_op jit(solution)/shard_map/ppermute | solution.py:207
  4.6 16.4 %collective-permute-start.1 = (bf16[512,512]{1,0:T(8,128)(2,1)S(1)}, bf16[512,512]{1,0:T(8,128)(2,1)}, u32[]{:S(2)}, u32[]{:S(2)}) collective-permute-start(bf16[512,512]{1,0:T(8,128)(2,1)S(1)} %pad_maximum_fusion.1), channel_id=1, source_target_pairs={{0,224},{32,0},{64,32},{96,64},{128,96},{160,128},{192,160},{224,1... | collective-permute-start | bytes 1572872 | tf_op jit(solution)/shard_map/ppermute | solution.py:207
  12.9 32.1 %all-to-all-start = ((bf16[32,13,16,128]{3,2,1,0:T(8,128)(2,1)}), bf16[32,13,16,128]{3,2,1,0:T(8,128)(2,1)S(1)}, u32[]{:S(2)}, u32[]{:S(2)}) async-start(bf16[32,13,16,128]{3,2,1,0:T(8,128)(2,1)} %pack.1), calls=%async_computation | async-start | bytes 3407872 | tf_op jit(solution)/shard_map/all_to_all | solution.py:240
  22.6 22.4 %copy-start.1 = (s32[1,32]{1,0:T(1,128)S(1)}, s32[1,32]{1,0:T(1,128)}, u32[]{:S(2)}) copy-start(s32[1,32]{1,0:T(1,128)} %owner_ref.1) | copy-start | bytes 388
  22.7 14.4 %collective-permute-start.2 = (bf16[512,512]{1,0:T(8,128)(2,1)S(1)}, bf16[512,512]{1,0:T(8,128)(2,1)S(1)}, u32[]{:S(2)}, u32[]{:S(2)}) collective-permute-start(bf16[512,512]{1,0:T(8,128)(2,1)S(1)} %get-tuple-element.18), channel_id=1, source_target_pairs={{0,32},{32,64},{64,96},{96,128},{128,160},{160,192},{192,224},{224... | collective-permute-start | bytes 1572872 | tf_op jit(solution)/shard_map/ppermute | solution.py:207
  22.8 14.4 %collective-permute-start.3 = (bf16[512,512]{1,0:T(8,128)(2,1)S(1)}, bf16[512,512]{1,0:T(8,128)(2,1)}, u32[]{:S(2)}, u32[]{:S(2)}) collective-permute-start(bf16[512,512]{1,0:T(8,128)(2,1)S(1)} %get-tuple-element.19), channel_id=1, source_target_pairs={{0,224},{32,0},{64,32},{96,64},{128,96},{160,128},{192,160},{224,1... | collective-permute-start | bytes 1572872 | tf_op jit(solution)/shard_map/ppermute | solution.py:207
  39.7 13.7 %collective-permute-start.4 = (bf16[512,512]{1,0:T(8,128)(2,1)}, bf16[512,512]{1,0:T(8,128)(2,1)S(1)}, u32[]{:S(2)}, u32[]{:S(2)}) collective-permute-start(bf16[512,512]{1,0:T(8,128)(2,1)} %pad_maximum_fusion.4), channel_id=1, source_target_pairs={{0,32},{32,64},{64,96},{96,128},{128,160},{160,192},{192,224},{224... | collective-permute-start | bytes 1572872 | tf_op jit(solution)/shard_map/ppermute | solution.py:207
  39.7 13.7 %collective-permute-start.5 = (bf16[512,512]{1,0:T(8,128)(2,1)S(1)}, bf16[512,512]{1,0:T(8,128)(2,1)S(1)}, u32[]{:S(2)}, u32[]{:S(2)}) collective-permute-start(bf16[512,512]{1,0:T(8,128)(2,1)S(1)} %pad_maximum_fusion.5), channel_id=1, source_target_pairs={{0,224},{32,0},{64,32},{96,64},{128,96},{160,128},{192,160},{224,1... | collective-permute-start | bytes 1572872 | tf_op jit(solution)/shard_map/ppermute | solution.py:207
  46.6 19.1 %all-to-all-start.1 = ((bf16[32,5,16,128]{3,2,1,0:T(8,128)(2,1)}), bf16[32,5,16,128]{3,2,1,0:T(8,128)(2,1)S(1)}, u32[]{:S(2)}, u32[]{:S(2)}) async-start(bf16[32,5,16,128]{3,2,1,0:T(8,128)(2,1)} %pick.1), calls=%async_computation.1 | async-start | bytes 1310720 | tf_op jit(solution)/shard_map/all_to_all | solution.py:242
  54.5 11.4 %collective-permute-start.6 = (bf16[256,512]{1,0:T(8,128)(2,1)S(1)}, bf16[256,512]{1,0:T(8,128)(2,1)S(1)}, u32[]{:S(2)}, u32[]{:S(2)}) collective-permute-start(bf16[256,512]{1,0:T(8,128)(2,1)S(1)} %get-tuple-element.26), channel_id=1, source_target_pairs={{0,32},{32,64},{64,96},{96,128},{128,160},{160,192},{192,224},{224... | collective-permute-start | bytes 786440 | tf_op jit(solution)/shard_map/ppermute | solution.py:207
  56.6 9.4 %collective-permute-start.7 = (bf16[256,512]{1,0:T(8,128)(2,1)S(1)}, bf16[256,512]{1,0:T(8,128)(2,1)S(1)}, u32[]{:S(2)}, u32[]{:S(2)}) collective-permute-start(bf16[256,512]{1,0:T(8,128)(2,1)S(1)} %get-tuple-element.27), channel_id=1, source_target_pairs={{0,224},{32,0},{64,32},{96,64},{128,96},{160,128},{192,160},{224,1... | collective-permute-start | bytes 786440 | tf_op jit(solution)/shard_map/ppermute | solution.py:207
  66.0 1.2 %copy-start = (f32[512,512]{1,0:T(8,128)S(1)}, f32[512,512]{1,0:T(8,128)}, u32[]{:S(2)}) copy-start(f32[512,512]{1,0:T(8,128)} %moment_ref.1) | copy-start | bytes 3145732

commit v3 on v2

v3 whole, which is shorter than its diff:
```python
import jax
import jax.numpy as jnp
from jax import lax
from jax.experimental import pallas as pl
from jax.experimental.pallas import tpu as pltpu
from jax.sharding import PartitionSpec as P

moment_decay = 0.95
adam_offset = 1e-08
norm_offset = 1e-06

B = 512
ROWS = 16
FULL = 60 * 1024 * 1024
LANES = 128
QUARTERS = B // LANES


def iotas(shape):
    return lax.broadcasted_iota(jnp.int32, shape, 0), lax.broadcasted_iota(jnp.int32, shape, 1)


def pack_kernel(roots_ref, out_ref, held, sems):
    slots = roots_ref.shape[2]
    tiles = out_ref.shape[1]
    chunk = LANES // ROWS
    copies = {}
    for k in range(slots):
        for i in range(QUARTERS):
            rows = slice(i * LANES, (i + 1) * LANES)
            for side, cols in ((0, slice(i * LANES, B)), (1, slice(0, (i + 1) * LANES))):
                copies[k, i, side] = pltpu.make_async_copy(
                    roots_ref.at[0, 0, k, side, rows, cols],
                    held.at[k, side, rows, cols],
                    sems.at[k, i, side],
                )
                copies[k, i, side].start()
    row, col = iotas((LANES, LANES))
    diagonal = [jnp.zeros((LANES, LANES), jnp.float32)] * QUARTERS
    for k in range(slots):
        for i in range(QUARTERS):
            rows = slice(i * LANES, (i + 1) * LANES)
            copies[k, i, 0].wait()
            copies[k, i, 1].wait()
            for j in range(QUARTERS):
                cols = slice(j * LANES, (j + 1) * LANES)
                if i == j:
                    right = held[k, 1, rows, cols]
                    block = jnp.where(row <= col, held[k, 0, rows, cols], right)
                    only = jnp.sum(jnp.where(row == col, right, 0.0), axis=1, keepdims=True)
                    diagonal[i] = jnp.where(col // 32 == k, only, diagonal[i])
                else:
                    block = held[k, 0 if i < j else 1, rows, cols]
                out_ref[i * chunk : (i + 1) * chunk, QUARTERS * k + j] = block.astype(
                    jnp.bfloat16
                ).reshape(chunk, ROWS, LANES)
    for i in range(QUARTERS):
        out_ref[i * chunk : (i + 1) * chunk, tiles - 1] = (
            diagonal[i].astype(jnp.bfloat16).reshape(chunk, ROWS, LANES)
        )


def pack(roots, devices):
    slots = roots.shape[2]
    tiles = QUARTERS * slots + 1
    return pl.pallas_call(
        pack_kernel,
        in_specs=[pl.BlockSpec(memory_space=pl.ANY)],
        out_specs=pl.BlockSpec(memory_space=pltpu.VMEM),
        out_shape=jax.ShapeDtypeStruct((devices, tiles, ROWS, LANES), jnp.bfloat16),
        scratch_shapes=[
            pltpu.VMEM((slots, 2, B, B), jnp.float32),
            pltpu.SemaphoreType.DMA((slots, QUARTERS, 2)),
        ],
        compiler_params=pltpu.CompilerParams(vmem_limit_bytes=58 * 1024 * 1024),
        cost_estimate=pl.CostEstimate(flops=0, bytes_accessed=8 * 1024 * 1024, transcendentals=0),
        name="pack",
    )(roots)


def pick_kernel(owner_ref, in_ref, out_ref, counts):
    devices, tiles = in_ref.shape[:2]
    lane = lax.broadcasted_iota(jnp.int32, (ROWS, LANES), 1)
    for o in range(devices):
        counts[o] = 0
    owners = owner_ref[...]
    for c in range(out_ref.shape[0]):
        o = owners[0, c]
        slot = counts[o]
        counts[o] = slot + 1
        for q in range(QUARTERS):
            out_ref[c, q] = in_ref[o, QUARTERS * slot + q]
        diagonal = in_ref[o, tiles - 1].astype(jnp.float32)
        kept = jnp.where(lane == slot * 32, diagonal, 0.0)
        out_ref[c, QUARTERS] = kept.astype(jnp.bfloat16)


def pick(owner, pieces):
    cols = owner.shape[1]
    return pl.pallas_call(
        pick_kernel,
        in_specs=[pl.BlockSpec(memory_space=pltpu.VMEM)] * 2,
        out_specs=pl.BlockSpec(memory_space=pltpu.VMEM),
        out_shape=jax.ShapeDtypeStruct((cols, QUARTERS + 1, ROWS, LANES), jnp.bfloat16),
        scratch_shapes=[pltpu.SMEM((pieces.shape[0],), jnp.int32)],
        compiler_params=pltpu.CompilerParams(vmem_limit_bytes=8 * 1024 * 1024),
        cost_estimate=pl.CostEstimate(flops=0, bytes_accessed=3 * 1024 * 1024, transcendentals=0),
        name="pick",
    )(owner, pieces)


def adam_kernel(
    own_ref, up_a_ref, up_b_ref, down_a_ref, down_b_ref, moment_ref,
    gradient_ref, moment_out_ref, target_ref,
):
    total = jnp.float32(0.0)
    first, second = slice(0, HALF), slice(HALF, B)
    for rows, up, down in (
        (first, up_a_ref[...], down_a_ref[...]),
        (second, up_b_ref[...], down_b_ref[...]),
    ):
        own = own_ref[rows].astype(jnp.float32)
        summed = own + up.astype(jnp.float32) + down.astype(jnp.float32)
        gradient = summed.astype(jnp.bfloat16)
        gradient_ref[rows] = gradient
        grad_float = gradient.astype(jnp.float32)
        moment_new = (
            moment_decay * moment_ref[rows] + (1.0 - moment_decay) * grad_float * grad_float
        )
        moment_out_ref[rows] = moment_new
        adam_step = grad_float / (jnp.sqrt(moment_new) + adam_offset)
        total += jnp.sum(adam_step * adam_step)
    target_ref[...] = jnp.broadcast_to(jnp.sqrt(total), target_ref.shape)


def adam(sums, moment):
    return pl.pallas_call(
        adam_kernel,
        in_specs=[pl.BlockSpec(memory_space=pltpu.VMEM)] * 6,
        out_specs=[pl.BlockSpec(memory_space=pltpu.VMEM)] * 3,
        out_shape=[
            jax.ShapeDtypeStruct((B, B), jnp.bfloat16),
            jax.ShapeDtypeStruct((B, B), jnp.float32),
            jax.ShapeDtypeStruct((1, LANES), jnp.float32),
        ],
        compiler_params=pltpu.CompilerParams(vmem_limit_bytes=16 * 1024 * 1024),
        cost_estimate=pl.CostEstimate(flops=0, bytes_accessed=5 * 1024 * 1024, transcendentals=0),
        name="adam",
    )(*sums, moment)


def direction_kernel(in_ref, gradient_ref, target_ref, direction_ref, left_ref, right_ref):
    row, col = iotas((LANES, LANES))
    chunk = LANES // ROWS
    for i in range(QUARTERS):
        rows = slice(i * LANES, (i + 1) * LANES)
        members = slice(i * chunk, (i + 1) * chunk)
        tile = in_ref[members, QUARTERS].reshape(LANES, LANES).astype(jnp.float32)
        diagonal = jnp.sum(tile, axis=1, keepdims=True)
        for j in range(i, QUARTERS):
            cols = slice(j * LANES, (j + 1) * LANES)
            upper = in_ref[members, j].reshape(LANES, LANES).astype(jnp.float32)
            if i == j:
                turned = upper.T
                left_ref[rows, cols] = jnp.where(row <= col, upper, turned).astype(jnp.bfloat16)
                right = jnp.where(row > col, upper, turned)
                right_ref[rows, cols] = jnp.where(row == col, diagonal, right).astype(jnp.bfloat16)
            else:
                others = slice(j * chunk, (j + 1) * chunk)
                lower = in_ref[others, i].reshape(LANES, LANES).astype(jnp.float32)
                left_ref[rows, cols] = upper.astype(jnp.bfloat16)
                left_ref[cols, rows] = upper.T.astype(jnp.bfloat16)
                right_ref[cols, rows] = lower.astype(jnp.bfloat16)
                right_ref[rows, cols] = lower.T.astype(jnp.bfloat16)
    left_part = jnp.dot(left_ref[...], gradient_ref[...], preferred_element_type=jnp.float32)
    conditioned = jnp.dot(
        left_part.astype(jnp.bfloat16), right_ref[...], preferred_element_type=jnp.float32
    )
    scale = target_ref[:, :1] / jnp.sqrt(jnp.sum(conditioned * conditioned) + norm_offset)
    direction_ref[...] = (conditioned * scale).astype(jnp.bfloat16)


def direct(pieces, gradient, target):
    return pl.pallas_call(
        direction_kernel,
        in_specs=[pl.BlockSpec(memory_space=pltpu.VMEM)] * 3,
        out_specs=pl.BlockSpec(memory_space=pltpu.VMEM),
        out_shape=jax.ShapeDtypeStruct((B, B), jnp.bfloat16),
        scratch_shapes=[pltpu.VMEM((B, B), jnp.bfloat16)] * 2,
        compiler_params=pltpu.CompilerParams(vmem_limit_bytes=16 * 1024 * 1024),
        cost_estimate=pl.CostEstimate(
            flops=4 * B * B * B, bytes_accessed=2 * 1024 * 1024, transcendentals=0
        ),
        name="direction",
    )(pieces, gradient, target)


HALF = B // 2


def add_kernel(up_ref, down_ref, up_own_ref, down_own_ref, up_out_ref, down_out_ref):
    for in_ref, own_ref, out_ref in (
        (up_ref, up_own_ref, up_out_ref),
        (down_ref, down_own_ref, down_out_ref),
    ):
        total = in_ref[...].astype(jnp.float32) + own_ref[...].astype(jnp.float32)
        out_ref[...] = total.astype(jnp.bfloat16)


def add_own(up, down, own, name, flops=40*10**8):
    return pl.pallas_call(
        add_kernel,
        in_specs=[pl.BlockSpec(memory_space=pltpu.VMEM)] * (2 + len(own)),
        out_specs=[pl.BlockSpec(memory_space=pltpu.VMEM)] * 2,
        out_shape=[jax.ShapeDtypeStruct((HALF, B), jnp.bfloat16)] * 2,
        compiler_params=pltpu.CompilerParams(vmem_limit_bytes=8 * 1024 * 1024),
        cost_estimate=pl.CostEstimate(flops=flops, bytes_accessed=3 * 1024 * 1024, transcendentals=0),
        name=name,
    )(up, down, *own)


def reduce_chunks(partials, packed):
    groups = lax.axis_size("rep")
    pairs_up = [(k, (k + 1) % groups) for k in range(groups)]
    pairs_down = [(k, (k - 1) % groups) for k in range(groups)]

    def move(up, down):
        return lax.ppermute(up, "rep", pairs_up), lax.ppermute(down, "rep", pairs_down)

    def mine(offset, start=0, rows=B, source=partials):
        chunk = lax.rem(lax.axis_index("rep") + offset + groups, groups)
        return lax.dynamic_slice(source, (chunk * B + start, 0), (rows, B))

    def add(a, b):
        return (a.astype(jnp.float32) + b.astype(jnp.float32)).astype(jnp.bfloat16)

    def half(offset, part, source=partials):
        return mine(offset, part * HALF, HALF, source)

    def parts(step, part, source=partials):
        return [half(step, part, source), half(-step, 1 - part, source)]

    barrier = lax.optimization_barrier
    up, down = move(
        jnp.concatenate([half(4, 0), half(3, 1)]), jnp.concatenate([half(-3, 0), half(-4, 1)])
    )
    up, down, packed = barrier((up, down, packed))
    own = parts(3, 0)
    sent = barrier((add(up[:HALF], own[0]), add(down[HALF:], own[1])))
    long = move(*sent)
    up, down, later, _ = barrier((up, down, partials, sent))
    own = parts(2, 1, later)
    sent = barrier((add(up[HALF:], own[0]), add(down[:HALF], own[1])))
    short = move(*sent)
    later, _ = barrier((later, sent))
    long = move(*add_own(*long, parts(2, 0, later), "long_3"))
    sent = add_own(*short, parts(1, 1, later), "short_3")
    short = move(*sent)
    later, _ = barrier((later, sent))
    long = move(*add_own(*long, parts(1, 0, later), "long_4"))
    return mine(0, source=later), long[0], short[0], short[1], long[1]


def body(partials, moment, owner, roots):
    devices = lax.axis_size("shard")
    packed = pack(roots, devices)
    sums = reduce_chunks(partials[0], packed)
    pieces = lax.all_to_all(packed, "shard", split_axis=0, concat_axis=0, tiled=True)
    picked = pick(owner, pieces)
    arrived = lax.all_to_all(picked, "shard", split_axis=0, concat_axis=0, tiled=True)
    gradient, moment_new, target = adam(sums, moment)
    return direct(arrived, gradient, target), moment_new


def solution(mesh):
    placed = (
        P("rep", None, "shard"),
        P("rep", "shard"),
        P("rep", None),
        P("rep", "shard", None, None, None, None),
    )
    return jax.shard_map(
        body,
        mesh=mesh,
        in_specs=placed,
        out_specs=(P("rep", "shard"), P("rep", "shard")),
        check_vma=False,
    )
```

time: 70.3 us -> 66.9 us (0.952)
  waiting for transfers between devices: 22.3 us -> 12.7 us
  starting transfers between devices: 28.9 us -> 34.1 us
  other arithmetic: 5.46 us -> 2.56 us
  Pallas kernels: 8.75 us -> 11.6 us
  local copies, waits for them, and re-layouts: 3.57 us -> 4.67 us
    all_to_all x1, waiting for transfers between devices: 7.27 us -> 0.05 us  [body(): lax.all_to_all(picked, 'shard', split_axis=0, concat_axis=0, tiled=True)]
    ppermute x4 -> x6, starting transfers between devices: 10.1 us -> 16.6 us  [move(): lax.ppermute(down, 'rep', pairs_down)]
    ppermute x4 -> x6, waiting for transfers between devices: 12.3 us -> 7.75 us  [move(): lax.ppermute(up, 'rep', pairs_up)]
    pallas_call x3 -> x6, Pallas kernels: 4.48 us -> 7.83 us  [the longest x3 2.77 us: add_own(): pl.pallas_call(add_kernel, in_specs=[pl.BlockSpec(memory_space=pltpu.VMEM...]
    dynamic_slice x2 -> x4, local copies, waits for them, and re-layouts: 2.34 us -> 4.66 us  [mine(): return lax.dynamic_slice(source, (chunk * B + start, 0), (rows, B))]
    all_to_all x1, waiting for transfers between devices: 2.65 us -> 4.91 us  [body(): lax.all_to_all(packed, 'shard', split_axis=0, concat_axis=0, tiled=True)]
    convert_element_type x3 -> x2, other arithmetic: 4.45 us -> 2.49 us  [add(): return (a.astype(jnp.float32) + b.astype(jnp.float32)).astype(jnp.bfloat16)]
    unnamed x4, local copies, waits for them, and re-layouts: 1.23 us -> 0.01 us
  transfers between devices with their start and end apart: 10 -> 14, of which waited for: 4 -> 5; matrix products, arithmetic and copies ran while one was open for 9% -> 9% of each run, Pallas kernels for 9% -> 14%
where the time goes in v3:
time: 66.9 us; the launch traced here: 66.5 us
  starting transfers between devices  34.1 us (51%)
  waiting for transfers between devices  12.7 us (19%)
  Pallas kernels  11.6 us (17%)
  local copies, waits for them, and re-layouts  4.67 us (7%)
  other arithmetic  2.56 us (4%)
  between operations  0.87 us (1%)
    ppermute x6, starting transfers between devices, move(): lax.ppermute(down, 'rep', pairs_down)  16.6 us
    all_to_all x1, starting transfers between devices, body(): lax.all_to_all(packed, 'shard', split_axis=0, concat_axis=0, tiled=True)  8.05 us
    ppermute x6, waiting for transfers between devices, move(): lax.ppermute(up, 'rep', pairs_up)  7.75 us
    all_to_all x1, starting transfers between devices, body(): lax.all_to_all(picked, 'shard', split_axis=0, concat_axis=0, tiled=True)  5.84 us
    all_to_all x1, waiting for transfers between devices, body(): lax.all_to_all(packed, 'shard', split_axis=0, concat_axis=0, tiled=True)  4.91 us
    dynamic_slice x4, local copies, waits for them, and re-layouts, mine(): return lax.dynamic_slice(source, (chunk * B + start, 0), (rows, B))  4.66 us
    pallas_call x1, Pallas kernels, pack(): pl.pallas_call(pack_kernel, in_specs=[pl.BlockSpec(memory_space=pl.ANY)],...  3.75 us
    ppermute x6, starting transfers between devices, move(): lax.ppermute(up, 'rep', pairs_up)  3.59 us
  transfers between devices with their start and end apart: 14, of which 5 were waited for; matrix products, arithmetic and copies ran while one was open for 9% of the time, Pallas kernels for 14%

profile of v3, /device:TPU:1, one launch (start us, length us, event | category | flops | bytes accessed | tf_op | source)
XLA Modules:
  0.0 66.5 jit_solution(14514831109494104109)
XLA Ops:
  0.7 1.3 %dynamic-slice_bitcast_fusion.1 = (bf16[256,512]{1,0:T(8,128)(2,1)S(1)}, bf16[256,512]{1,0:T(8,128)(2,1)S(1)}, bf16[256,512]{1,0:T(8,128)(2,1)S(1)}, bf16[256,512]{1,0:T(8,128)(2,1)S(1)}) fusion(bf16[1,4096,512]{2,1,0:T(8,128)(2,1)} %param.4, s32[]{:T(128)S(6)} %select_n.47, s32[]{:T(128)S(6)} %select_n.48, s32[]{:T(128)S(6)} %select_n.46, s32[]{:T(128)S(6)} %select_n.45), kind=kLoop, calls=%fused_computation.9 | loop fusion | bytes 2097168 | tf_op jit(solution)/shard_map/dynamic_slice | solution.py:232
  2.0 2.5 %collective-permute-start = (bf16[512,512]{1,0:T(8,128)(2,1)S(1)}, bf16[512,512]{1,0:T(8,128)(2,1)S(1)}, u32[]{:S(2)}, u32[]{:S(2)}) collective-permute-start(bf16[512,512]{1,0:T(8,128)(2,1)S(1)} %pad_maximum_fusion), channel_id=1, source_target_pairs={{0,32},{32,64},{64,96},{96,128},{128,160},{160,192},{192,224},{224... | collective-permute-start | bytes 1572872 | tf_op jit(solution)/shard_map/ppermute | solution.py:228
  4.6 4.0 %collective-permute-start.1 = (bf16[512,512]{1,0:T(8,128)(2,1)S(1)}, bf16[512,512]{1,0:T(8,128)(2,1)}, u32[]{:S(2)}, u32[]{:S(2)}) collective-permute-start(bf16[512,512]{1,0:T(8,128)(2,1)S(1)} %pad_maximum_fusion.1), channel_id=1, source_target_pairs={{0,224},{32,0},{64,32},{96,64},{128,96},{160,128},{192,160},{224,1... | collective-permute-start | bytes 1572872 | tf_op jit(solution)/shard_map/ppermute | solution.py:228
  8.6 3.7 %pack.1 = bf16[32,13,16,128]{3,2,1,0:T(8,128)(2,1)} custom-call(f32[1,1,3,2,512,512]{5,4,3,2,1,0:T(8,128)} %roots_ref.1), custom_call_target="tpu_custom_call" | custom-call | bytes 8388608 | tf_op jit(solution)/shard_map/pack/pallas_call | solution.py:66
  12.3 8.1 %all-to-all-start = ((bf16[32,13,16,128]{3,2,1,0:T(8,128)(2,1)}), bf16[32,13,16,128]{3,2,1,0:T(8,128)(2,1)S(1)}, u32[]{:S(2)}, u32[]{:S(2)}) async-start(bf16[32,13,16,128]{3,2,1,0:T(8,128)(2,1)} %pack.1), calls=%async_computation | async-start | bytes 3407872 | tf_op jit(solution)/shard_map/all_to_all | solution.py:268
  20.5 0.0 collective-permute-done
  20.5 0.0 collective-permute-done.1
  20.5 1.2 %fusion = (bf16[256,512]{1,0:T(8,128)(2,1)S(1)}, bf16[256,512]{1,0:T(8,128)(2,1)S(1)}) fusion(bf16[1,4096,512]{2,1,0:T(8,128)(2,1)} %param.4, s32[]{:T(128)S(6)} %select_n.50, bf16[512,512]{1,0:T(8,128)(2,1)} %collective-permute-done.1, s32[]{:T(128)S(6)} %select_n.49, bf16[512,512]{1,0:T(8,128)(2,1)S(1)} %collective-permute-done), kind=kLoop, calls=%fused_computation.3 | loop fusion | flops 1048576 | bytes 1572872 | tf_op jit(solution)/shard_map/convert_element_type | solution.py:235
  21.7 0.1 collective-permute-start.4
  21.8 2.7 %collective-permute-start.5 = (bf16[256,512]{1,0:T(8,128)(2,1)S(1)}, bf16[256,512]{1,0:T(8,128)(2,1)S(1)}, u32[]{:S(2)}, u32[]{:S(2)}) collective-permute-start(bf16[256,512]{1,0:T(8,128)(2,1)S(1)} %get-tuple-element.25), channel_id=1, source_target_pairs={{0,224},{32,0},{64,32},{96,64},{128,96},{160,128},{192,160},{224,1... | collective-permute-start | bytes 786440 | tf_op jit(solution)/shard_map/ppermute | solution.py:228
  24.5 1.2 %add_convert_fusion = (bf16[256,512]{1,0:T(8,128)(2,1)S(1)}, bf16[256,512]{1,0:T(8,128)(2,1)S(1)}) fusion(bf16[4096,512]{1,0:T(8,128)(2,1)} %bitcast.15, s32[]{:T(128)S(6)} %select_n.52, bf16[512,512]{1,0:T(8,128)(2,1)} %collective-permute-done.1, s32[]{:T(128)S(6)} %select_n.51, bf16[512,512]{1,0:T(8,128)(2,1)S(1)} %collective-permute-done), kind=kLoop, calls=%fused_computation.6 | loop fusion | flops 1048576 | bytes 1572872 | tf_op jit(solution)/shard_map/convert_element_type | solution.py:235
  25.7 0.1 collective-permute-start.2
  25.8 2.7 %collective-permute-start.3 = (bf16[256,512]{1,0:T(8,128)(2,1)S(1)}, bf16[256,512]{1,0:T(8,128)(2,1)S(1)}, u32[]{:S(2)}, u32[]{:S(2)}) collective-permute-start(bf16[256,512]{1,0:T(8,128)(2,1)S(1)} %get-tuple-element.30), channel_id=1, source_target_pairs={{0,224},{32,0},{64,32},{96,64},{128,96},{160,128},{192,160},{224,1... | collective-permute-start | bytes 786440 | tf_op jit(solution)/shard_map/ppermute | solution.py:228
  28.5 1.3 %constant_dynamic-slice_fusion.2 = (bf16[256,512]{1,0:T(8,128)(2,1)S(1)}, bf16[256,512]{1,0:T(8,128)(2,1)S(1)}, bf16[256,512]{1,0:T(8,128)(2,1)S(1)}, bf16[256,512]{1,0:T(8,128)(2,1)S(1)}) fusion(bf16[4096,512]{1,0:T(8,128)(2,1)} %bitcast.16, s32[]{:T(128)S(6)} %select_n.57, s32[]{:T(128)S(6)} %select_n.56, s32[]{:T(128)S(6)} %select_n.54, s32[]{:T(128)S(6)} %select_n.53), kind=kLoop, calls=%fused_computation.14 | loop fusion | bytes 2097168 | tf_op jit(solution)/shard_map/dynamic_slice | solution.py:232
  29.8 0.3 collective-permute-done.4.up_ref
  30.0 0.0 collective-permute-done.5.down_ref
  30.0 0.8 %long_3.1 = (bf16[256,512]{1,0:T(8,128)(2,1)}, bf16[256,512]{1,0:T(8,128)(2,1)S(1)}) custom-call(bf16[256,512]{1,0:T(8,128)(2,1)S(1)} %collective-permute-done.4.up_ref, bf16[256,512]{1,0:T(8,128)(2,1)S(1)} %collective-permute-done.5.down_ref, bf16[256,512]{1,0:T(8,128)(2,1)S(1)} %get-tuple-element.45.up_own_ref, ...), custom_call_target="tpu_custom_call" | custom-call | flops 4000000000 | bytes 3145728 | tf_op jit(solution)/shard_map/long_3/pallas_call | solution.py:211
  30.8 0.3 collective-permute-start.6
  31.1 2.4 %collective-permute-start.7 = (bf16[256,512]{1,0:T(8,128)(2,1)S(1)}, bf16[256,512]{1,0:T(8,128)(2,1)}, u32[]{:S(2)}, u32[]{:S(2)}) collective-permute-start(bf16[256,512]{1,0:T(8,128)(2,1)S(1)} %get-tuple-element.36), channel_id=1, source_target_pairs={{0,224},{32,0},{64,32},{96,64},{128,96},{160,128},{192,160},{224,1... | collective-permute-start | bytes 786440 | tf_op jit(solution)/shard_map/ppermute | solution.py:228
  33.5 2.2 %collective-permute-done.2.up_ref = bf16[256,512]{1,0:T(8,128)(2,1)S(1)} collective-permute-done((bf16[256,512]{1,0:T(8,128)(2,1)S(1)}, bf16[256,512]{1,0:T(8,128)(2,1)S(1)}, u32[]{:S(2)}, u32[]{:S(2)}) %collective-permute-start.2) | collective-permute-done | bytes 262176 | tf_op jit(solution)/shard_map/ppermute | solution.py:228
  35.6 0.0 collective-permute-done.3.down_ref
  35.6 0.0 copy-start.1
  35.6 0.1 short_3.1
  35.8 0.4 collective-permute-start.9
  36.2 2.4 %collective-permute-start.10 = (bf16[256,512]{1,0:T(8,128)(2,1)S(1)}, bf16[256,512]{1,0:T(8,128)(2,1)S(1)}, u32[]{:S(2)}, u32[]{:S(2)}) collective-permute-start(bf16[256,512]{1,0:T(8,128)(2,1)S(1)} %get-tuple-element.33), channel_id=1, source_target_pairs={{0,224},{32,0},{64,32},{96,64},{128,96},{160,128},{192,160},{224,1... | collective-permute-start | bytes 786440 | tf_op jit(solution)/shard_map/ppermute | solution.py:228
  38.5 1.1 %constant_dynamic-slice_fusion = (bf16[256,512]{1,0:T(8,128)(2,1)S(1)}, bf16[256,512]{1,0:T(8,128)(2,1)S(1)}) fusion(bf16[4096,512]{1,0:T(8,128)(2,1)} %bitcast.17, s32[]{:T(128)S(6)} %select_n.59, s32[]{:T(128)S(6)} %select_n.58), kind=kLoop, calls=%fused_computation.12 | loop fusion | bytes 1048584 | tf_op jit(solution)/shard_map/dynamic_slice | solution.py:232
  39.6 4.9 %all-to-all-done.in_ref = bf16[32,13,16,128]{3,2,1,0:T(8,128)(2,1)S(1)} async-done(((bf16[32,13,16,128]{3,2,1,0:T(8,128)(2,1)}), bf16[32,13,16,128]{3,2,1,0:T(8,128)(2,1)S(1)}, u32[]{:S(2)}, u32[]{:S(2)}) %all-to-all-start) | async-done | bytes 1703968 | tf_op jit(solution)/shard_map/all_to_all | solution.py:268
  44.5 0.0 copy-done.1
  44.5 1.1 %pick.1 = bf16[32,5,16,128]{3,2,1,0:T(8,128)(2,1)} custom-call(s32[1,32]{1,0:T(1,128)S(1)} %copy-done.1, bf16[32,13,16,128]{3,2,1,0:T(8,128)(2,1)S(1)} %all-to-all-done.in_ref), custom_call_target="tpu_custom_call" | custom-call | bytes 3145728 | tf_op jit(solution)/shard_map/pick/pallas_call | solution.py:100
  45.6 5.8 %all-to-all-start.1 = ((bf16[32,5,16,128]{3,2,1,0:T(8,128)(2,1)}), bf16[32,5,16,128]{3,2,1,0:T(8,128)(2,1)S(1)}, u32[]{:S(2)}, u32[]{:S(2)}) async-start(bf16[32,5,16,128]{3,2,1,0:T(8,128)(2,1)} %pick.1), calls=%async_computation.1 | async-start | bytes 1310720 | tf_op jit(solution)/shard_map/all_to_all | solution.py:270
  51.4 0.0 collective-permute-done.6.up_ref
  51.5 0.0 collective-permute-done.7.down_ref
  51.5 0.0 copy-start
  51.5 1.9 %long_4.1 = (bf16[256,512]{1,0:T(8,128)(2,1)}, bf16[256,512]{1,0:T(8,128)(2,1)S(1)}) custom-call(bf16[256,512]{1,0:T(8,128)(2,1)} %collective-permute-done.6.up_ref, bf16[256,512]{1,0:T(8,128)(2,1)} %collective-permute-done.7.down_ref, bf16[256,512]{1,0:T(8,128)(2,1)S(1)} %get-tuple-element.43.up_own_ref, bf16[256,512]{1,0:T(8,128)(2,1)S(1)} %get-tuple-element.42.down_own_ref), custom_call_target="tpu_custom_call" | custom-call | flops 4000000000 | bytes 3145728 | tf_op jit(solution)/shard_map/long_4/pallas_call | solution.py:211
  53.4 0.2 collective-permute-start.8
  53.5 2.5 %collective-permute-start.11 = (bf16[256,512]{1,0:T(8,128)(2,1)S(1)}, bf16[256,512]{1,0:T(8,128)(2,1)S(1)}, u32[]{:S(2)}, u32[]{:S(2)}) collective-permute-start(bf16[256,512]{1,0:T(8,128)(2,1)S(1)} %get-tuple-element.38), channel_id=1, source_target_pairs={{0,224},{32,0},{64,32},{96,64},{128,96},{160,128},{192,160},{224,1... | collective-permute-start | bytes 786440 | tf_op jit(solution)/shard_map/ppermute | solution.py:228
  56.0 1.1 %constant_dynamic-slice_fusion.4.own_ref = bf16[512,512]{1,0:T(8,128)(2,1)S(1)} fusion(bf16[4096,512]{1,0:T(8,128)(2,1)} %bitcast.18, s32[]{:T(128)S(6)} %select_n.55), kind=kLoop, calls=%fused_computation.16 | loop fusion | bytes 1048580 | tf_op jit(solution)/shard_map/dynamic_slice | solution.py:232
  57.1 0.0 collective-permute-done.9.up_b_ref
  57.1 0.0 collective-permute-done.10.down_a_ref
  57.1 5.3 %collective-permute-done.8.up_a_ref = bf16[256,512]{1,0:T(8,128)(2,1)S(1)} collective-permute-done((bf16[256,512]{1,0:T(8,128)(2,1)}, bf16[256,512]{1,0:T(8,128)(2,1)S(1)}, u32[]{:S(2)}, u32[]{:S(2)}) %collective-permute-start.8) | collective-permute-done | bytes 262176 | tf_op jit(solution)/shard_map/ppermute | solution.py:228
  62.5 0.0 collective-permute-done.11.down_b_ref
  62.5 0.0 copy-done
  62.5 1.9 %adam.1 = (bf16[512,512]{1,0:T(8,128)(2,1)S(1)}, f32[512,512]{1,0:T(8,128)}, f32[1,128]{1,0:T(1,128)S(1)}) custom-call(bf16[512,512]{1,0:T(8,128)(2,1)S(1)} %constant_dynamic-slice_fusion.4.own_ref, bf16[256,512]{1,0:T(8,128)(2,1)S(1)} %collective-permute-done.8.up_a_ref, bf16[256,512]{1,0:T(8,128)(2,1)S(1)} %collective-permute-done.9.up_b_ref, ...), custom_call_target="tpu_custom_call" | custom-call | bytes 5242880 | tf_op jit(solution)/shard_map/adam/pallas_call | solution.py:137
  64.3 0.1 all-to-all-done.1.in_ref
  64.4 2.1 %direction.1 = bf16[512,512]{1,0:T(8,128)(2,1)} custom-call(bf16[32,5,16,128]{3,2,1,0:T(8,128)(2,1)S(1)} %all-to-all-done.1.in_ref, bf16[512,512]{1,0:T(8,128)(2,1)S(1)} %get-tuple-element.39.gradient_ref, f32[1,128]{1,0:T(1,128)S(1)} %get-tuple-element.40.target_ref), custom_call_target="tpu_custom_call" | custom-call | flops 536870912 | bytes 2097152 | tf_op jit(solution)/shard_map/direction/pallas_call | solution.py:184
  (2 shorter events, 0.1 us)
Async XLA Ops:
  2.0 18.5 %collective-permute-start = (bf16[512,512]{1,0:T(8,128)(2,1)S(1)}, bf16[512,512]{1,0:T(8,128)(2,1)S(1)}, u32[]{:S(2)}, u32[]{:S(2)}) collective-permute-start(bf16[512,512]{1,0:T(8,128)(2,1)S(1)} %pad_maximum_fusion), channel_id=1, source_target_pairs={{0,32},{32,64},{64,96},{96,128},{128,160},{160,192},{192,224},{224... | collective-permute-start | bytes 1572872 | tf_op jit(solution)/shard_map/ppermute | solution.py:228
  4.6 15.9 %collective-permute-start.1 = (bf16[512,512]{1,0:T(8,128)(2,1)S(1)}, bf16[512,512]{1,0:T(8,128)(2,1)}, u32[]{:S(2)}, u32[]{:S(2)}) collective-permute-start(bf16[512,512]{1,0:T(8,128)(2,1)S(1)} %pad_maximum_fusion.1), channel_id=1, source_target_pairs={{0,224},{32,0},{64,32},{96,64},{128,96},{160,128},{192,160},{224,1... | collective-permute-start | bytes 1572872 | tf_op jit(solution)/shard_map/ppermute | solution.py:228
  12.3 32.1 %all-to-all-start = ((bf16[32,13,16,128]{3,2,1,0:T(8,128)(2,1)}), bf16[32,13,16,128]{3,2,1,0:T(8,128)(2,1)S(1)}, u32[]{:S(2)}, u32[]{:S(2)}) async-start(bf16[32,13,16,128]{3,2,1,0:T(8,128)(2,1)} %pack.1), calls=%async_computation | async-start | bytes 3407872 | tf_op jit(solution)/shard_map/all_to_all | solution.py:268
  21.7 8.3 %collective-permute-start.4 = (bf16[256,512]{1,0:T(8,128)(2,1)S(1)}, bf16[256,512]{1,0:T(8,128)(2,1)S(1)}, u32[]{:S(2)}, u32[]{:S(2)}) collective-permute-start(bf16[256,512]{1,0:T(8,128)(2,1)S(1)} %get-tuple-element.24), channel_id=1, source_target_pairs={{0,32},{32,64},{64,96},{96,128},{128,160},{160,192},{192,224},{224... | collective-permute-start | bytes 786440 | tf_op jit(solution)/shard_map/ppermute | solution.py:228
  21.8 8.2 %collective-permute-start.5 = (bf16[256,512]{1,0:T(8,128)(2,1)S(1)}, bf16[256,512]{1,0:T(8,128)(2,1)S(1)}, u32[]{:S(2)}, u32[]{:S(2)}) collective-permute-start(bf16[256,512]{1,0:T(8,128)(2,1)S(1)} %get-tuple-element.25), channel_id=1, source_target_pairs={{0,224},{32,0},{64,32},{96,64},{128,96},{160,128},{192,160},{224,1... | collective-permute-start | bytes 786440 | tf_op jit(solution)/shard_map/ppermute | solution.py:228
  25.7 9.9 %collective-permute-start.2 = (bf16[256,512]{1,0:T(8,128)(2,1)S(1)}, bf16[256,512]{1,0:T(8,128)(2,1)S(1)}, u32[]{:S(2)}, u32[]{:S(2)}) collective-permute-start(bf16[256,512]{1,0:T(8,128)(2,1)S(1)} %get-tuple-element.29), channel_id=1, source_target_pairs={{0,32},{32,64},{64,96},{96,128},{128,160},{160,192},{192,224},{224... | collective-permute-start | bytes 786440 | tf_op jit(solution)/shard_map/ppermute | solution.py:228
  25.8 9.8 %collective-permute-start.3 = (bf16[256,512]{1,0:T(8,128)(2,1)S(1)}, bf16[256,512]{1,0:T(8,128)(2,1)S(1)}, u32[]{:S(2)}, u32[]{:S(2)}) collective-permute-start(bf16[256,512]{1,0:T(8,128)(2,1)S(1)} %get-tuple-element.30), channel_id=1, source_target_pairs={{0,224},{32,0},{64,32},{96,64},{128,96},{160,128},{192,160},{224,1... | collective-permute-start | bytes 786440 | tf_op jit(solution)/shard_map/ppermute | solution.py:228
  30.8 20.7 %collective-permute-start.6 = (bf16[256,512]{1,0:T(8,128)(2,1)}, bf16[256,512]{1,0:T(8,128)(2,1)}, u32[]{:S(2)}, u32[]{:S(2)}) collective-permute-start(bf16[256,512]{1,0:T(8,128)(2,1)} %get-tuple-element.35), channel_id=1, source_target_pairs={{0,32},{32,64},{64,96},{96,128},{128,160},{160,192},{192,224},{224... | collective-permute-start | bytes 786440 | tf_op jit(solution)/shard_map/ppermute | solution.py:228
  31.1 20.4 %collective-permute-start.7 = (bf16[256,512]{1,0:T(8,128)(2,1)S(1)}, bf16[256,512]{1,0:T(8,128)(2,1)}, u32[]{:S(2)}, u32[]{:S(2)}) collective-permute-start(bf16[256,512]{1,0:T(8,128)(2,1)S(1)} %get-tuple-element.36), channel_id=1, source_target_pairs={{0,224},{32,0},{64,32},{96,64},{128,96},{160,128},{192,160},{224,1... | collective-permute-start | bytes 786440 | tf_op jit(solution)/shard_map/ppermute | solution.py:228
  35.6 8.9 %copy-start.1 = (s32[1,32]{1,0:T(1,128)S(1)}, s32[1,32]{1,0:T(1,128)}, u32[]{:S(2)}) copy-start(s32[1,32]{1,0:T(1,128)} %owner_ref.1) | copy-start | bytes 388
  35.8 21.4 %collective-permute-start.9 = (bf16[256,512]{1,0:T(8,128)(2,1)S(1)}, bf16[256,512]{1,0:T(8,128)(2,1)S(1)}, u32[]{:S(2)}, u32[]{:S(2)}) collective-permute-start(bf16[256,512]{1,0:T(8,128)(2,1)S(1)} %get-tuple-element.32), channel_id=1, source_target_pairs={{0,32},{32,64},{64,96},{96,128},{128,160},{160,192},{192,224},{224... | collective-permute-start | bytes 786440 | tf_op jit(solution)/shard_map/ppermute | solution.py:228
  36.2 21.0 %collective-permute-start.10 = (bf16[256,512]{1,0:T(8,128)(2,1)S(1)}, bf16[256,512]{1,0:T(8,128)(2,1)S(1)}, u32[]{:S(2)}, u32[]{:S(2)}) collective-permute-start(bf16[256,512]{1,0:T(8,128)(2,1)S(1)} %get-tuple-element.33), channel_id=1, source_target_pairs={{0,224},{32,0},{64,32},{96,64},{128,96},{160,128},{192,160},{224,1... | collective-permute-start | bytes 786440 | tf_op jit(solution)/shard_map/ppermute | solution.py:228
  45.6 18.8 %all-to-all-start.1 = ((bf16[32,5,16,128]{3,2,1,0:T(8,128)(2,1)}), bf16[32,5,16,128]{3,2,1,0:T(8,128)(2,1)S(1)}, u32[]{:S(2)}, u32[]{:S(2)}) async-start(bf16[32,5,16,128]{3,2,1,0:T(8,128)(2,1)} %pick.1), calls=%async_computation.1 | async-start | bytes 1310720 | tf_op jit(solution)/shard_map/all_to_all | solution.py:270
  51.5 11.0 %copy-start = (f32[512,512]{1,0:T(8,128)S(1)}, f32[512,512]{1,0:T(8,128)}, u32[]{:S(2)}) copy-start(f32[512,512]{1,0:T(8,128)} %moment_ref.1) | copy-start | bytes 3145732
  53.4 9.1 %collective-permute-start.8 = (bf16[256,512]{1,0:T(8,128)(2,1)}, bf16[256,512]{1,0:T(8,128)(2,1)S(1)}, u32[]{:S(2)}, u32[]{:S(2)}) collective-permute-start(bf16[256,512]{1,0:T(8,128)(2,1)} %get-tuple-element.37), channel_id=1, source_target_pairs={{0,32},{32,64},{64,96},{96,128},{128,160},{160,192},{192,224},{224... | collective-permute-start | bytes 786440 | tf_op jit(solution)/shard_map/ppermute | solution.py:228
  53.5 8.9 %collective-permute-start.11 = (bf16[256,512]{1,0:T(8,128)(2,1)S(1)}, bf16[256,512]{1,0:T(8,128)(2,1)S(1)}, u32[]{:S(2)}, u32[]{:S(2)}) collective-permute-start(bf16[256,512]{1,0:T(8,128)(2,1)S(1)} %get-tuple-element.38), channel_id=1, source_target_pairs={{0,224},{32,0},{64,32},{96,64},{128,96},{160,128},{192,160},{224,1... | collective-permute-start | bytes 786440 | tf_op jit(solution)/shard_map/ppermute | solution.py:228

commit v4 on v3

--- a/solution.py
+++ b/solution.py
@@ -20,9 +20,9 @@
     return lax.broadcasted_iota(jnp.int32, shape, 0), lax.broadcasted_iota(jnp.int32, shape, 1)
 
 
-def pack_kernel(roots_ref, out_ref, held, sems):
+def pack_kernel(roots_ref, result_ref, held, out_ref, sems, out_sems):
     slots = roots_ref.shape[2]
-    tiles = out_ref.shape[1]
+    tiles = result_ref.shape[1]
     chunk = LANES // ROWS
     copies = {}
     for k in range(slots):
@@ -37,6 +37,7 @@
                 copies[k, i, side].start()
     row, col = iotas((LANES, LANES))
     diagonal = [jnp.zeros((LANES, LANES), jnp.float32)] * QUARTERS
+    stores = []
     for k in range(slots):
         for i in range(QUARTERS):
             rows = slice(i * LANES, (i + 1) * LANES)
@@ -54,10 +55,21 @@
                 out_ref[i * chunk : (i + 1) * chunk, QUARTERS * k + j] = block.astype(
                     jnp.bfloat16
                 ).reshape(chunk, ROWS, LANES)
-    for i in range(QUARTERS):
-        out_ref[i * chunk : (i + 1) * chunk, tiles - 1] = (
-            diagonal[i].astype(jnp.bfloat16).reshape(chunk, ROWS, LANES)
-        )
+            members = slice(i * chunk, (i + 1) * chunk)
+            ready = slice(QUARTERS * k, QUARTERS * (k + 1))
+            if k == slots - 1:
+                out_ref[members, tiles - 1] = (
+                    diagonal[i].astype(jnp.bfloat16).reshape(chunk, ROWS, LANES)
+                )
+                ready = slice(QUARTERS * k, tiles)
+            stores.append(
+                pltpu.make_async_copy(
+                    out_ref.at[members, ready], result_ref.at[members, ready], out_sems.at[k, i]
+                )
+            )
+            stores[-1].start()
+    for store in stores:
+        store.wait()
 
 
 def pack(roots, devices):
@@ -66,11 +78,13 @@
     return pl.pallas_call(
         pack_kernel,
         in_specs=[pl.BlockSpec(memory_space=pl.ANY)],
-        out_specs=pl.BlockSpec(memory_space=pltpu.VMEM),
+        out_specs=pl.BlockSpec(memory_space=pl.ANY),
         out_shape=jax.ShapeDtypeStruct((devices, tiles, ROWS, LANES), jnp.bfloat16),
         scratch_shapes=[
             pltpu.VMEM((slots, 2, B, B), jnp.float32),
+            pltpu.VMEM((devices, tiles, ROWS, LANES), jnp.bfloat16),
             pltpu.SemaphoreType.DMA((slots, QUARTERS, 2)),
+            pltpu.SemaphoreType.DMA((slots, QUARTERS)),
         ],
         compiler_params=pltpu.CompilerParams(vmem_limit_bytes=58 * 1024 * 1024),
         cost_estimate=pl.CostEstimate(flops=0, bytes_accessed=8 * 1024 * 1024, transcendentals=0),
@@ -144,7 +158,7 @@
             jax.ShapeDtypeStruct((1, LANES), jnp.float32),
         ],
         compiler_params=pltpu.CompilerParams(vmem_limit_bytes=16 * 1024 * 1024),
-        cost_estimate=pl.CostEstimate(flops=0, bytes_accessed=5 * 1024 * 1024, transcendentals=0),
+        cost_estimate=pl.CostEstimate(flops=20*10**8, bytes_accessed=5 * 1024 * 1024, transcendentals=0),
         name="adam",
     )(*sums, moment)
 
@@ -257,7 +271,8 @@
     sent = add_own(*short, parts(1, 1, later), "short_3")
     short = move(*sent)
     later, _ = barrier((later, sent))
-    long = move(*add_own(*long, parts(1, 0, later), "long_4"))
+    own = parts(1, 0, later)
+    long = move(*barrier((add(long[0], own[0]), add(long[1], own[1]))))
     return mine(0, source=later), long[0], short[0], short[1], long[1]
 
 

time: 66.9 us -> 66 us (0.987)
  Pallas kernels: 11.6 us -> 10.1 us
  waiting for transfers between devices: 12.7 us -> 14.1 us
  other arithmetic: 2.56 us -> 3.89 us
  starting transfers between devices: 34.1 us -> 33 us
  local copies, waits for them, and re-layouts: 4.67 us -> 3.6 us
    ppermute x6, starting transfers between devices: 16.6 us -> 14.4 us  [move(): lax.ppermute(down, 'rep', pairs_down)]
    ppermute x6, starting transfers between devices: 3.59 us -> 5.33 us  [move(): lax.ppermute(up, 'rep', pairs_up)]
    convert_element_type x2 -> x3, other arithmetic: 2.49 us -> 3.82 us  [add(): return (a.astype(jnp.float32) + b.astype(jnp.float32)).astype(jnp.bfloat16)]
    pallas_call x3 -> x2, Pallas kernels: 2.77 us -> 1.63 us  [add_own(): pl.pallas_call(add_kernel, in_specs=[pl.BlockSpec(memory_space=pltpu.VMEM...]
    dynamic_slice x4 -> x3, local copies, waits for them, and re-layouts: 4.66 us -> 3.6 us  [mine(): return lax.dynamic_slice(source, (chunk * B + start, 0), (rows, B))]
    all_to_all x1, waiting for transfers between devices: 4.91 us -> 5.61 us  [body(): lax.all_to_all(packed, 'shard', split_axis=0, concat_axis=0, tiled=True)]
  transfers between devices with their start and end apart: 14 -> 14, of which waited for: 5 -> 5; matrix products, arithmetic and copies ran while one was open for 9% -> 9% of each run, Pallas kernels for 14% -> 12%
where the time goes in v4:
time: 66 us; the launch traced here: 65.5 us
  starting transfers between devices  33 us (50%)
  waiting for transfers between devices  14.1 us (21%)
  Pallas kernels  10.1 us (15%)
  other arithmetic  3.89 us (6%)
  local copies, waits for them, and re-layouts  3.6 us (5%)
  between operations  0.87 us (1%)
    ppermute x6, starting transfers between devices, move(): lax.ppermute(down, 'rep', pairs_down)  14.4 us
    all_to_all x1, starting transfers between devices, body(): lax.all_to_all(packed, 'shard', split_axis=0, concat_axis=0, tiled=True)  8.05 us
    ppermute x6, waiting for transfers between devices, move(): lax.ppermute(up, 'rep', pairs_up)  7.7 us
    all_to_all x1, waiting for transfers between devices, body(): lax.all_to_all(packed, 'shard', split_axis=0, concat_axis=0, tiled=True)  5.61 us
    ppermute x6, starting transfers between devices, move(): lax.ppermute(up, 'rep', pairs_up)  5.33 us
    all_to_all x1, starting transfers between devices, body(): lax.all_to_all(picked, 'shard', split_axis=0, concat_axis=0, tiled=True)  5.23 us
    convert_element_type x3, other arithmetic, add(): return (a.astype(jnp.float32) + b.astype(jnp.float32)).astype(jnp.bfloat16)  3.82 us
    dynamic_slice x3, local copies, waits for them, and re-layouts, mine(): return lax.dynamic_slice(source, (chunk * B + start, 0), (rows, B))  3.6 us
  transfers between devices with their start and end apart: 14, of which 5 were waited for; matrix products, arithmetic and copies ran while one was open for 9% of the time, Pallas kernels for 12%

profile of v4, /device:TPU:1, one launch (start us, length us, event | category | flops | bytes accessed | tf_op | source)
XLA Modules:
  0.0 65.5 jit_solution(14687792928035558701)
XLA Ops:
  0.7 1.3 %dynamic-slice_bitcast_fusion.1 = (bf16[256,512]{1,0:T(8,128)(2,1)S(1)}, bf16[256,512]{1,0:T(8,128)(2,1)S(1)}, bf16[256,512]{1,0:T(8,128)(2,1)S(1)}, bf16[256,512]{1,0:T(8,128)(2,1)S(1)}) fusion(bf16[1,4096,512]{2,1,0:T(8,128)(2,1)} %param.4, s32[]{:T(128)S(6)} %select_n.47, s32[]{:T(128)S(6)} %select_n.48, s32[]{:T(128)S(6)} %select_n.46, s32[]{:T(128)S(6)} %select_n.45), kind=kLoop, calls=%fused_computation.11 | loop fusion | bytes 2097168 | tf_op jit(solution)/shard_map/dynamic_slice | solution.py:246
  2.0 2.5 %collective-permute-start = (bf16[512,512]{1,0:T(8,128)(2,1)S(1)}, bf16[512,512]{1,0:T(8,128)(2,1)S(1)}, u32[]{:S(2)}, u32[]{:S(2)}) collective-permute-start(bf16[512,512]{1,0:T(8,128)(2,1)S(1)} %pad_maximum_fusion), channel_id=1, source_target_pairs={{0,32},{32,64},{64,96},{96,128},{128,160},{160,192},{192,224},{224... | collective-permute-start | bytes 1572872 | tf_op jit(solution)/shard_map/ppermute | solution.py:242
  4.6 4.0 %collective-permute-start.1 = (bf16[512,512]{1,0:T(8,128)(2,1)S(1)}, bf16[512,512]{1,0:T(8,128)(2,1)}, u32[]{:S(2)}, u32[]{:S(2)}) collective-permute-start(bf16[512,512]{1,0:T(8,128)(2,1)S(1)} %pad_maximum_fusion.1), channel_id=1, source_target_pairs={{0,224},{32,0},{64,32},{96,64},{128,96},{160,128},{192,160},{224,1... | collective-permute-start | bytes 1572872 | tf_op jit(solution)/shard_map/ppermute | solution.py:242
  8.6 3.4 %pack.1 = bf16[32,13,16,128]{3,2,1,0:T(8,128)(2,1)} custom-call(f32[1,1,3,2,512,512]{5,4,3,2,1,0:T(8,128)} %roots_ref.1), custom_call_target="tpu_custom_call" | custom-call | bytes 8388608 | tf_op jit(solution)/shard_map/pack/pallas_call | solution.py:78
  12.0 8.1 %all-to-all-start = ((bf16[32,13,16,128]{3,2,1,0:T(8,128)(2,1)}), bf16[32,13,16,128]{3,2,1,0:T(8,128)(2,1)S(1)}, u32[]{:S(2)}, u32[]{:S(2)}) async-start(bf16[32,13,16,128]{3,2,1,0:T(8,128)(2,1)} %pack.1), calls=%async_computation | async-start | bytes 3407872 | tf_op jit(solution)/shard_map/all_to_all | solution.py:283
  20.1 0.0 collective-permute-done
  20.1 0.0 collective-permute-done.1
  20.1 1.2 %fusion = (bf16[256,512]{1,0:T(8,128)(2,1)S(1)}, bf16[256,512]{1,0:T(8,128)(2,1)S(1)}) fusion(bf16[1,4096,512]{2,1,0:T(8,128)(2,1)} %param.4, s32[]{:T(128)S(6)} %select_n.50, bf16[512,512]{1,0:T(8,128)(2,1)} %collective-permute-done.1, s32[]{:T(128)S(6)} %select_n.49, bf16[512,512]{1,0:T(8,128)(2,1)S(1)} %collective-permute-done), kind=kLoop, calls=%fused_computation.3 | loop fusion | flops 1048576 | bytes 1572872 | tf_op jit(solution)/shard_map/convert_element_type | solution.py:249
  21.4 0.1 collective-permute-start.4
  21.5 2.7 %collective-permute-start.5 = (bf16[256,512]{1,0:T(8,128)(2,1)S(1)}, bf16[256,512]{1,0:T(8,128)(2,1)S(1)}, u32[]{:S(2)}, u32[]{:S(2)}) collective-permute-start(bf16[256,512]{1,0:T(8,128)(2,1)S(1)} %get-tuple-element.25), channel_id=1, source_target_pairs={{0,224},{32,0},{64,32},{96,64},{128,96},{160,128},{192,160},{224,1... | collective-permute-start | bytes 786440 | tf_op jit(solution)/shard_map/ppermute | solution.py:242
  24.1 1.2 %add_convert_fusion.2 = (bf16[256,512]{1,0:T(8,128)(2,1)S(1)}, bf16[256,512]{1,0:T(8,128)(2,1)S(1)}) fusion(bf16[4096,512]{1,0:T(8,128)(2,1)} %bitcast.15, s32[]{:T(128)S(6)} %select_n.52, bf16[512,512]{1,0:T(8,128)(2,1)} %collective-permute-done.1, s32[]{:T(128)S(6)} %select_n.51, bf16[512,512]{1,0:T(8,128)(2,1)S(1)} %collective-permute-done), kind=kLoop, calls=%fused_computation.8 | loop fusion | flops 1048576 | bytes 1572872 | tf_op jit(solution)/shard_map/convert_element_type | solution.py:249
  25.4 0.1 collective-permute-start.2
  25.5 2.7 %collective-permute-start.3 = (bf16[256,512]{1,0:T(8,128)(2,1)S(1)}, bf16[256,512]{1,0:T(8,128)(2,1)S(1)}, u32[]{:S(2)}, u32[]{:S(2)}) collective-permute-start(bf16[256,512]{1,0:T(8,128)(2,1)S(1)} %get-tuple-element.30), channel_id=1, source_target_pairs={{0,224},{32,0},{64,32},{96,64},{128,96},{160,128},{192,160},{224,1... | collective-permute-start | bytes 786440 | tf_op jit(solution)/shard_map/ppermute | solution.py:242
  28.1 1.3 %constant_dynamic-slice_fusion = (bf16[256,512]{1,0:T(8,128)(2,1)S(1)}, bf16[256,512]{1,0:T(8,128)(2,1)S(1)}, bf16[256,512]{1,0:T(8,128)(2,1)S(1)}, bf16[256,512]{1,0:T(8,128)(2,1)S(1)}) fusion(bf16[4096,512]{1,0:T(8,128)(2,1)} %bitcast.16, s32[]{:T(128)S(6)} %select_n.57, s32[]{:T(128)S(6)} %select_n.56, s32[]{:T(128)S(6)} %select_n.54, s32[]{:T(128)S(6)} %select_n.53), kind=kLoop, calls=%fused_computation.14 | loop fusion | bytes 2097168 | tf_op jit(solution)/shard_map/dynamic_slice | solution.py:246
  29.4 0.0 collective-permute-done.4.up_ref
  29.4 0.0 collective-permute-done.5.down_ref
  29.4 0.9 %long_3.1 = (bf16[256,512]{1,0:T(8,128)(2,1)}, bf16[256,512]{1,0:T(8,128)(2,1)}) custom-call(bf16[256,512]{1,0:T(8,128)(2,1)S(1)} %collective-permute-done.4.up_ref, bf16[256,512]{1,0:T(8,128)(2,1)S(1)} %collective-permute-done.5.down_ref, bf16[256,512]{1,0:T(8,128)(2,1)S(1)} %get-tuple-element.45.up_own_ref, bf16[256,512]{1,0:T(8,128)(2,1)S(1)} %get-tuple-element.44.down_own_ref), custom_call_target="tpu_custom_call" | custom-call | flops 4000000000 | bytes 3145728 | tf_op jit(solution)/shard_map/long_3/pallas_call | solution.py:225
  30.3 2.2 %collective-permute-start.7 = (bf16[256,512]{1,0:T(8,128)(2,1)}, bf16[256,512]{1,0:T(8,128)(2,1)}, u32[]{:S(2)}, u32[]{:S(2)}) collective-permute-start(bf16[256,512]{1,0:T(8,128)(2,1)} %get-tuple-element.36), channel_id=1, source_target_pairs={{0,224},{32,0},{64,32},{96,64},{128,96},{160,128},{192,160},{224,1... | collective-permute-start | bytes 786440 | tf_op jit(solution)/shard_map/ppermute | solution.py:242
  32.5 0.0 collective-permute-start.6
  32.5 2.6 %collective-permute-done.2.up_ref = bf16[256,512]{1,0:T(8,128)(2,1)S(1)} collective-permute-done((bf16[256,512]{1,0:T(8,128)(2,1)S(1)}, bf16[256,512]{1,0:T(8,128)(2,1)S(1)}, u32[]{:S(2)}, u32[]{:S(2)}) %collective-permute-start.2) | collective-permute-done | bytes 262176 | tf_op jit(solution)/shard_map/ppermute | solution.py:242
  35.1 0.0 collective-permute-done.3.down_ref
  35.1 0.0 copy-start
  35.1 0.8 %short_3.1 = (bf16[256,512]{1,0:T(8,128)(2,1)}, bf16[256,512]{1,0:T(8,128)(2,1)S(1)}) custom-call(bf16[256,512]{1,0:T(8,128)(2,1)S(1)} %collective-permute-done.2.up_ref, bf16[256,512]{1,0:T(8,128)(2,1)S(1)} %collective-permute-done.3.down_ref, bf16[256,512]{1,0:T(8,128)(2,1)S(1)} %get-tuple-element.47.up_own_ref, ...), custom_call_target="tpu_custom_call" | custom-call | flops 4000000000 | bytes 3145728 | tf_op jit(solution)/shard_map/short_3/pallas_call | solution.py:225
  35.8 0.0 copy-start.1
  35.8 0.9 %collective-permute-start.9 = (bf16[256,512]{1,0:T(8,128)(2,1)}, bf16[256,512]{1,0:T(8,128)(2,1)S(1)}, u32[]{:S(2)}, u32[]{:S(2)}) collective-permute-start(bf16[256,512]{1,0:T(8,128)(2,1)} %get-tuple-element.32), channel_id=1, source_target_pairs={{0,32},{32,64},{64,96},{96,128},{128,160},{160,192},{192,224},{224... | collective-permute-start | bytes 786440 | tf_op jit(solution)/shard_map/ppermute | solution.py:242
  36.7 1.8 %collective-permute-start.10 = (bf16[256,512]{1,0:T(8,128)(2,1)S(1)}, bf16[256,512]{1,0:T(8,128)(2,1)S(1)}, u32[]{:S(2)}, u32[]{:S(2)}) collective-permute-start(bf16[256,512]{1,0:T(8,128)(2,1)S(1)} %get-tuple-element.33), channel_id=1, source_target_pairs={{0,224},{32,0},{64,32},{96,64},{128,96},{160,128},{192,160},{224,1... | collective-permute-start | bytes 786440 | tf_op jit(solution)/shard_map/ppermute | solution.py:242
  38.5 5.6 %all-to-all-done.in_ref = bf16[32,13,16,128]{3,2,1,0:T(8,128)(2,1)S(1)} async-done(((bf16[32,13,16,128]{3,2,1,0:T(8,128)(2,1)}), bf16[32,13,16,128]{3,2,1,0:T(8,128)(2,1)S(1)}, u32[]{:S(2)}, u32[]{:S(2)}) %all-to-all-start) | async-done | bytes 1703968 | tf_op jit(solution)/shard_map/all_to_all | solution.py:283
  44.1 0.0 copy-done
  44.1 1.1 %pick.1 = bf16[32,5,16,128]{3,2,1,0:T(8,128)(2,1)} custom-call(s32[1,32]{1,0:T(1,128)S(1)} %copy-done, bf16[32,13,16,128]{3,2,1,0:T(8,128)(2,1)S(1)} %all-to-all-done.in_ref), custom_call_target="tpu_custom_call" | custom-call | bytes 3145728 | tf_op jit(solution)/shard_map/pick/pallas_call | solution.py:114
  45.2 5.2 %all-to-all-start.1 = ((bf16[32,5,16,128]{3,2,1,0:T(8,128)(2,1)}), bf16[32,5,16,128]{3,2,1,0:T(8,128)(2,1)S(1)}, u32[]{:S(2)}, u32[]{:S(2)}) async-start(bf16[32,5,16,128]{3,2,1,0:T(8,128)(2,1)} %pick.1), calls=%async_computation.1 | async-start | bytes 1310720 | tf_op jit(solution)/shard_map/all_to_all | solution.py:285
  50.5 0.0 collective-permute-done.7
  50.5 0.0 collective-permute-done.6
  50.5 1.3 %add_convert_fusion = (bf16[256,512]{1,0:T(8,128)(2,1)S(1)}, bf16[256,512]{1,0:T(8,128)(2,1)S(1)}) fusion(bf16[256,512]{1,0:T(8,128)(2,1)} %collective-permute-done.7, bf16[4096,512]{1,0:T(8,128)(2,1)} %bitcast.17, s32[]{:T(128)S(6)} %select_n.59, s32[]{:T(128)S(6)} %select_n.58, bf16[256,512]{1,0:T(8,128)(2,1)} %collective-permute-done.6), kind=kLoop, calls=%fused_computation.6 | loop fusion | flops 1048576 | bytes 1572872 | tf_op jit(solution)/shard_map/convert_element_type | solution.py:249
  51.8 1.7 %collective-permute-start.8 = (bf16[256,512]{1,0:T(8,128)(2,1)S(1)}, bf16[256,512]{1,0:T(8,128)(2,1)S(1)}, u32[]{:S(2)}, u32[]{:S(2)}) collective-permute-start(bf16[256,512]{1,0:T(8,128)(2,1)S(1)} %get-tuple-element.37), channel_id=1, source_target_pairs={{0,32},{32,64},{64,96},{96,128},{128,160},{160,192},{192,224},{224... | collective-permute-start | bytes 786440 | tf_op jit(solution)/shard_map/ppermute | solution.py:242
  53.6 1.0 %collective-permute-start.11 = (bf16[256,512]{1,0:T(8,128)(2,1)S(1)}, bf16[256,512]{1,0:T(8,128)(2,1)S(1)}, u32[]{:S(2)}, u32[]{:S(2)}) collective-permute-start(bf16[256,512]{1,0:T(8,128)(2,1)S(1)} %get-tuple-element.38), channel_id=1, source_target_pairs={{0,224},{32,0},{64,32},{96,64},{128,96},{160,128},{192,160},{224,1... | collective-permute-start | bytes 786440 | tf_op jit(solution)/shard_map/ppermute | solution.py:242
  54.6 1.1 %constant_dynamic-slice_fusion.2.own_ref = bf16[512,512]{1,0:T(8,128)(2,1)S(1)} fusion(bf16[4096,512]{1,0:T(8,128)(2,1)} %bitcast.18, s32[]{:T(128)S(6)} %select_n.55), kind=kLoop, calls=%fused_computation.16 | loop fusion | bytes 1048580 | tf_op jit(solution)/shard_map/dynamic_slice | solution.py:246
  55.7 0.0 collective-permute-done.9.up_b_ref
  55.7 0.0 collective-permute-done.10.down_a_ref
  55.7 5.1 %collective-permute-done.8.up_a_ref = bf16[256,512]{1,0:T(8,128)(2,1)S(1)} collective-permute-done((bf16[256,512]{1,0:T(8,128)(2,1)S(1)}, bf16[256,512]{1,0:T(8,128)(2,1)S(1)}, u32[]{:S(2)}, u32[]{:S(2)}) %collective-permute-start.8) | collective-permute-done | bytes 262176 | tf_op jit(solution)/shard_map/ppermute | solution.py:242
  60.8 0.3 collective-permute-done.11.down_b_ref
  61.1 0.0 copy-done.1
  61.1 1.9 %adam.1 = (bf16[512,512]{1,0:T(8,128)(2,1)S(1)}, f32[512,512]{1,0:T(8,128)}, f32[1,128]{1,0:T(1,128)S(1)}) custom-call(bf16[512,512]{1,0:T(8,128)(2,1)S(1)} %constant_dynamic-slice_fusion.2.own_ref, bf16[256,512]{1,0:T(8,128)(2,1)S(1)} %collective-permute-done.8.up_a_ref, bf16[256,512]{1,0:T(8,128)(2,1)S(1)} %collective-permute-done.9.up_b_ref, ...), custom_call_target="tpu_custom_call" | custom-call | flops 2000000000 | bytes 5242880 | tf_op jit(solution)/shard_map/adam/pallas_call | solution.py:151
  63.0 0.4 all-to-all-done.1.in_ref
  63.4 2.1 %direction.1 = bf16[512,512]{1,0:T(8,128)(2,1)} custom-call(bf16[32,5,16,128]{3,2,1,0:T(8,128)(2,1)S(1)} %all-to-all-done.1.in_ref, bf16[512,512]{1,0:T(8,128)(2,1)S(1)} %get-tuple-element.39.gradient_ref, f32[1,128]{1,0:T(1,128)S(1)} %get-tuple-element.40.target_ref), custom_call_target="tpu_custom_call" | custom-call | flops 536870912 | bytes 2097152 | tf_op jit(solution)/shard_map/direction/pallas_call | solution.py:198
  (2 shorter events, 0.1 us)
Async XLA Ops:
  2.0 18.1 %collective-permute-start = (bf16[512,512]{1,0:T(8,128)(2,1)S(1)}, bf16[512,512]{1,0:T(8,128)(2,1)S(1)}, u32[]{:S(2)}, u32[]{:S(2)}) collective-permute-start(bf16[512,512]{1,0:T(8,128)(2,1)S(1)} %pad_maximum_fusion), channel_id=1, source_target_pairs={{0,32},{32,64},{64,96},{96,128},{128,160},{160,192},{192,224},{224... | collective-permute-start | bytes 1572872 | tf_op jit(solution)/shard_map/ppermute | solution.py:242
  4.6 15.6 %collective-permute-start.1 = (bf16[512,512]{1,0:T(8,128)(2,1)S(1)}, bf16[512,512]{1,0:T(8,128)(2,1)}, u32[]{:S(2)}, u32[]{:S(2)}) collective-permute-start(bf16[512,512]{1,0:T(8,128)(2,1)S(1)} %pad_maximum_fusion.1), channel_id=1, source_target_pairs={{0,224},{32,0},{64,32},{96,64},{128,96},{160,128},{192,160},{224,1... | collective-permute-start | bytes 1572872 | tf_op jit(solution)/shard_map/ppermute | solution.py:242
  12.0 32.1 %all-to-all-start = ((bf16[32,13,16,128]{3,2,1,0:T(8,128)(2,1)}), bf16[32,13,16,128]{3,2,1,0:T(8,128)(2,1)S(1)}, u32[]{:S(2)}, u32[]{:S(2)}) async-start(bf16[32,13,16,128]{3,2,1,0:T(8,128)(2,1)} %pack.1), calls=%async_computation | async-start | bytes 3407872 | tf_op jit(solution)/shard_map/all_to_all | solution.py:283
  21.4 8.0 %collective-permute-start.4 = (bf16[256,512]{1,0:T(8,128)(2,1)S(1)}, bf16[256,512]{1,0:T(8,128)(2,1)S(1)}, u32[]{:S(2)}, u32[]{:S(2)}) collective-permute-start(bf16[256,512]{1,0:T(8,128)(2,1)S(1)} %get-tuple-element.24), channel_id=1, source_target_pairs={{0,32},{32,64},{64,96},{96,128},{128,160},{160,192},{192,224},{224... | collective-permute-start | bytes 786440 | tf_op jit(solution)/shard_map/ppermute | solution.py:242
  21.5 7.9 %collective-permute-start.5 = (bf16[256,512]{1,0:T(8,128)(2,1)S(1)}, bf16[256,512]{1,0:T(8,128)(2,1)S(1)}, u32[]{:S(2)}, u32[]{:S(2)}) collective-permute-start(bf16[256,512]{1,0:T(8,128)(2,1)S(1)} %get-tuple-element.25), channel_id=1, source_target_pairs={{0,224},{32,0},{64,32},{96,64},{128,96},{160,128},{192,160},{224,1... | collective-permute-start | bytes 786440 | tf_op jit(solution)/shard_map/ppermute | solution.py:242
  25.4 9.7 %collective-permute-start.2 = (bf16[256,512]{1,0:T(8,128)(2,1)S(1)}, bf16[256,512]{1,0:T(8,128)(2,1)S(1)}, u32[]{:S(2)}, u32[]{:S(2)}) collective-permute-start(bf16[256,512]{1,0:T(8,128)(2,1)S(1)} %get-tuple-element.29), channel_id=1, source_target_pairs={{0,32},{32,64},{64,96},{96,128},{128,160},{160,192},{192,224},{224... | collective-permute-start | bytes 786440 | tf_op jit(solution)/shard_map/ppermute | solution.py:242
  25.5 9.6 %collective-permute-start.3 = (bf16[256,512]{1,0:T(8,128)(2,1)S(1)}, bf16[256,512]{1,0:T(8,128)(2,1)S(1)}, u32[]{:S(2)}, u32[]{:S(2)}) collective-permute-start(bf16[256,512]{1,0:T(8,128)(2,1)S(1)} %get-tuple-element.30), channel_id=1, source_target_pairs={{0,224},{32,0},{64,32},{96,64},{128,96},{160,128},{192,160},{224,1... | collective-permute-start | bytes 786440 | tf_op jit(solution)/shard_map/ppermute | solution.py:242
  30.3 20.2 %collective-permute-start.7 = (bf16[256,512]{1,0:T(8,128)(2,1)}, bf16[256,512]{1,0:T(8,128)(2,1)}, u32[]{:S(2)}, u32[]{:S(2)}) collective-permute-start(bf16[256,512]{1,0:T(8,128)(2,1)} %get-tuple-element.36), channel_id=1, source_target_pairs={{0,224},{32,0},{64,32},{96,64},{128,96},{160,128},{192,160},{224,1... | collective-permute-start | bytes 786440 | tf_op jit(solution)/shard_map/ppermute | solution.py:242
  32.5 18.0 %collective-permute-start.6 = (bf16[256,512]{1,0:T(8,128)(2,1)}, bf16[256,512]{1,0:T(8,128)(2,1)}, u32[]{:S(2)}, u32[]{:S(2)}) collective-permute-start(bf16[256,512]{1,0:T(8,128)(2,1)} %get-tuple-element.35), channel_id=1, source_target_pairs={{0,32},{32,64},{64,96},{96,128},{128,160},{160,192},{192,224},{224... | collective-permute-start | bytes 786440 | tf_op jit(solution)/shard_map/ppermute | solution.py:242
  35.1 9.1 %copy-start = (s32[1,32]{1,0:T(1,128)S(1)}, s32[1,32]{1,0:T(1,128)}, u32[]{:S(2)}) copy-start(s32[1,32]{1,0:T(1,128)} %owner_ref.1) | copy-start | bytes 388
  35.8 25.3 %copy-start.1 = (f32[512,512]{1,0:T(8,128)S(1)}, f32[512,512]{1,0:T(8,128)}, u32[]{:S(2)}) copy-start(f32[512,512]{1,0:T(8,128)} %moment_ref.1) | copy-start | bytes 3145732
  35.8 19.8 %collective-permute-start.9 = (bf16[256,512]{1,0:T(8,128)(2,1)}, bf16[256,512]{1,0:T(8,128)(2,1)S(1)}, u32[]{:S(2)}, u32[]{:S(2)}) collective-permute-start(bf16[256,512]{1,0:T(8,128)(2,1)} %get-tuple-element.32), channel_id=1, source_target_pairs={{0,32},{32,64},{64,96},{96,128},{128,160},{160,192},{192,224},{224... | collective-permute-start | bytes 786440 | tf_op jit(solution)/shard_map/ppermute | solution.py:242
  36.7 19.0 %collective-permute-start.10 = (bf16[256,512]{1,0:T(8,128)(2,1)S(1)}, bf16[256,512]{1,0:T(8,128)(2,1)S(1)}, u32[]{:S(2)}, u32[]{:S(2)}) collective-permute-start(bf16[256,512]{1,0:T(8,128)(2,1)S(1)} %get-tuple-element.33), channel_id=1, source_target_pairs={{0,224},{32,0},{64,32},{96,64},{128,96},{160,128},{192,160},{224,1... | collective-permute-start | bytes 786440 | tf_op jit(solution)/shard_map/ppermute | solution.py:242
  45.2 18.2 %all-to-all-start.1 = ((bf16[32,5,16,128]{3,2,1,0:T(8,128)(2,1)}), bf16[32,5,16,128]{3,2,1,0:T(8,128)(2,1)S(1)}, u32[]{:S(2)}, u32[]{:S(2)}) async-start(bf16[32,5,16,128]{3,2,1,0:T(8,128)(2,1)} %pick.1), calls=%async_computation.1 | async-start | bytes 1310720 | tf_op jit(solution)/shard_map/all_to_all | solution.py:285
  51.8 9.0 %collective-permute-start.8 = (bf16[256,512]{1,0:T(8,128)(2,1)S(1)}, bf16[256,512]{1,0:T(8,128)(2,1)S(1)}, u32[]{:S(2)}, u32[]{:S(2)}) collective-permute-start(bf16[256,512]{1,0:T(8,128)(2,1)S(1)} %get-tuple-element.37), channel_id=1, source_target_pairs={{0,32},{32,64},{64,96},{96,128},{128,160},{160,192},{192,224},{224... | collective-permute-start | bytes 786440 | tf_op jit(solution)/shard_map/ppermute | solution.py:242
  53.6 7.6 %collective-permute-start.11 = (bf16[256,512]{1,0:T(8,128)(2,1)S(1)}, bf16[256,512]{1,0:T(8,128)(2,1)S(1)}, u32[]{:S(2)}, u32[]{:S(2)}) collective-permute-start(bf16[256,512]{1,0:T(8,128)(2,1)S(1)} %get-tuple-element.38), channel_id=1, source_target_pairs={{0,224},{32,0},{64,32},{96,64},{128,96},{160,128},{192,160},{224,1... | collective-permute-start | bytes 786440 | tf_op jit(solution)/shard_map/ppermute | solution.py:242

commit v5 on v4

--- a/solution.py
+++ b/solution.py
@@ -123,44 +123,55 @@
     )(owner, pieces)
 
 
+def ready_kernel(own_ref, up_b_ref, down_a_ref, known_ref):
+    first, second = slice(0, HALF), slice(HALF, B)
+    known_ref[first] = own_ref[first].astype(jnp.float32) + down_a_ref[...].astype(jnp.float32)
+    known_ref[second] = own_ref[second].astype(jnp.float32) + up_b_ref[...].astype(jnp.float32)
+
+
+def ready(own, up_b, down_a):
+    return pl.pallas_call(
+        ready_kernel,
+        in_specs=[pl.BlockSpec(memory_space=pltpu.VMEM)] * 3,
+        out_specs=pl.BlockSpec(memory_space=pltpu.VMEM),
+        out_shape=jax.ShapeDtypeStruct((B, B), jnp.float32),
+        compiler_params=pltpu.CompilerParams(vmem_limit_bytes=8 * 1024 * 1024),
+        cost_estimate=pl.CostEstimate(flops=0, bytes_accessed=4 * 1024 * 1024, transcendentals=0),
+        name="ready",
+    )(own, up_b, down_a)
+
+
 def adam_kernel(
-    own_ref, up_a_ref, up_b_ref, down_a_ref, down_b_ref, moment_ref,
-    gradient_ref, moment_out_ref, target_ref,
+    known_ref, moment_ref, up_a_ref, down_b_ref, gradient_ref, moment_out_ref, target_ref
 ):
     total = jnp.float32(0.0)
-    first, second = slice(0, HALF), slice(HALF, B)
-    for rows, up, down in (
-        (first, up_a_ref[...], down_a_ref[...]),
-        (second, up_b_ref[...], down_b_ref[...]),
-    ):
-        own = own_ref[rows].astype(jnp.float32)
-        summed = own + up.astype(jnp.float32) + down.astype(jnp.float32)
-        gradient = summed.astype(jnp.bfloat16)
+    for rows, last_ref in ((slice(0, HALF), up_a_ref), (slice(HALF, B), down_b_ref)):
+        gradient = (known_ref[rows] + last_ref[...].astype(jnp.float32)).astype(jnp.bfloat16)
         gradient_ref[rows] = gradient
         grad_float = gradient.astype(jnp.float32)
-        moment_new = (
-            moment_decay * moment_ref[rows] + (1.0 - moment_decay) * grad_float * grad_float
-        )
+        moment_new = moment_decay * moment_ref[rows] + (1.0 - moment_decay) * grad_float * grad_float
         moment_out_ref[rows] = moment_new
         adam_step = grad_float / (jnp.sqrt(moment_new) + adam_offset)
         total += jnp.sum(adam_step * adam_step)
     target_ref[...] = jnp.broadcast_to(jnp.sqrt(total), target_ref.shape)
 
 
-def adam(sums, moment):
+def adam(known, moment, up_a, down_b):
     return pl.pallas_call(
         adam_kernel,
-        in_specs=[pl.BlockSpec(memory_space=pltpu.VMEM)] * 6,
+        in_specs=[pl.BlockSpec(memory_space=pltpu.VMEM)] * 4,
         out_specs=[pl.BlockSpec(memory_space=pltpu.VMEM)] * 3,
         out_shape=[
             jax.ShapeDtypeStruct((B, B), jnp.bfloat16),
             jax.ShapeDtypeStruct((B, B), jnp.float32),
             jax.ShapeDtypeStruct((1, LANES), jnp.float32),
         ],
-        compiler_params=pltpu.CompilerParams(vmem_limit_bytes=16 * 1024 * 1024),
-        cost_estimate=pl.CostEstimate(flops=20*10**8, bytes_accessed=5 * 1024 * 1024, transcendentals=0),
+        compiler_params=pltpu.CompilerParams(vmem_limit_bytes=8 * 1024 * 1024),
+        cost_estimate=pl.CostEstimate(
+            flops=20 * 10**8, bytes_accessed=5 * 1024 * 1024, transcendentals=0
+        ),
         name="adam",
-    )(*sums, moment)
+    )(known, moment, up_a, down_b)
 
 
 def direction_kernel(in_ref, gradient_ref, target_ref, direction_ref, left_ref, right_ref):
@@ -229,6 +240,7 @@
         out_shape=[jax.ShapeDtypeStruct((HALF, B), jnp.bfloat16)] * 2,
         compiler_params=pltpu.CompilerParams(vmem_limit_bytes=8 * 1024 * 1024),
         cost_estimate=pl.CostEstimate(flops=flops, bytes_accessed=3 * 1024 * 1024, transcendentals=0),
+        input_output_aliases={2: 0, 3: 1} if name == "short_3" else {},
         name=name,
     )(up, down, *own)
 
@@ -283,7 +295,9 @@
     pieces = lax.all_to_all(packed, "shard", split_axis=0, concat_axis=0, tiled=True)
     picked = pick(owner, pieces)
     arrived = lax.all_to_all(picked, "shard", split_axis=0, concat_axis=0, tiled=True)
-    gradient, moment_new, target = adam(sums, moment)
+    own, up_a, up_b, down_a, down_b = sums
+    known = ready(own, up_b, down_a)
+    gradient, moment_new, target = adam(known, moment, up_a, down_b)
     return direct(arrived, gradient, target), moment_new
 
 

time: 66 us -> 65.8 us (level)
  Pallas kernels: 10.1 us -> 8.78 us
    pallas_call x2, Pallas kernels: 1.63 us -> 0.41 us  [add_own(): pl.pallas_call(add_kernel, in_specs=[pl.BlockSpec(memory_space=pltpu.VMEM...]
    ppermute x6, waiting for transfers between devices: 7.7 us -> 8.44 us  [move(): lax.ppermute(up, 'rep', pairs_up)]
  transfers between devices with their start and end apart: 14 -> 14, of which waited for: 5 -> 4; matrix products, arithmetic and copies ran while one was open for 9% -> 10% of each run, Pallas kernels for 12% -> 10%
where the time goes in v5:
time: 65.8 us; the launch traced here: 65.3 us
  starting transfers between devices  32.9 us (50%)
  waiting for transfers between devices  14.6 us (22%)
  Pallas kernels  8.78 us (13%)
  other arithmetic  4.52 us (7%)
  local copies, waits for them, and re-layouts  3.62 us (6%)
  between operations  0.89 us (1%)
    ppermute x6, starting transfers between devices, move(): lax.ppermute(down, 'rep', pairs_down)  14.6 us
    ppermute x6, waiting for transfers between devices, move(): lax.ppermute(up, 'rep', pairs_up)  8.44 us
    all_to_all x1, starting transfers between devices, body(): lax.all_to_all(packed, 'shard', split_axis=0, concat_axis=0, tiled=True)  8.05 us
    all_to_all x1, waiting for transfers between devices, body(): lax.all_to_all(packed, 'shard', split_axis=0, concat_axis=0, tiled=True)  5.93 us
    ppermute x6, starting transfers between devices, move(): lax.ppermute(up, 'rep', pairs_up)  5.25 us
    all_to_all x1, starting transfers between devices, body(): lax.all_to_all(picked, 'shard', split_axis=0, concat_axis=0, tiled=True)  5.04 us
    convert_element_type x3, other arithmetic, add(): return (a.astype(jnp.float32) + b.astype(jnp.float32)).astype(jnp.bfloat16)  4.44 us
    dynamic_slice x3, local copies, waits for them, and re-layouts, mine(): return lax.dynamic_slice(source, (chunk * B + start, 0), (rows, B))  3.62 us
  transfers between devices with their start and end apart: 14, of which 4 were waited for; matrix products, arithmetic and copies ran while one was open for 10% of the time, Pallas kernels for 10%

profile of v5, /device:TPU:1, one launch (start us, length us, event | category | flops | bytes accessed | tf_op | source)
XLA Modules:
  0.0 65.3 jit_solution(8906017017698194918)
XLA Ops:
  0.7 1.3 %dynamic-slice_bitcast_fusion.1 = (bf16[256,512]{1,0:T(8,128)(2,1)S(1)}, bf16[256,512]{1,0:T(8,128)(2,1)S(1)}, bf16[256,512]{1,0:T(8,128)(2,1)S(1)}, bf16[256,512]{1,0:T(8,128)(2,1)S(1)}) fusion(bf16[1,4096,512]{2,1,0:T(8,128)(2,1)} %param.4, s32[]{:T(128)S(6)} %select_n.47, s32[]{:T(128)S(6)} %select_n.48, s32[]{:T(128)S(6)} %select_n.46, s32[]{:T(128)S(6)} %select_n.45), kind=kLoop, calls=%fused_computation.11 | loop fusion | bytes 2097168 | tf_op jit(solution)/shard_map/dynamic_slice | solution.py:258
  2.0 2.5 %collective-permute-start = (bf16[512,512]{1,0:T(8,128)(2,1)S(1)}, bf16[512,512]{1,0:T(8,128)(2,1)S(1)}, u32[]{:S(2)}, u32[]{:S(2)}) collective-permute-start(bf16[512,512]{1,0:T(8,128)(2,1)S(1)} %pad_maximum_fusion), channel_id=1, source_target_pairs={{0,32},{32,64},{64,96},{96,128},{128,160},{160,192},{192,224},{224... | collective-permute-start | bytes 1572872 | tf_op jit(solution)/shard_map/ppermute | solution.py:254
  4.6 4.0 %collective-permute-start.1 = (bf16[512,512]{1,0:T(8,128)(2,1)S(1)}, bf16[512,512]{1,0:T(8,128)(2,1)}, u32[]{:S(2)}, u32[]{:S(2)}) collective-permute-start(bf16[512,512]{1,0:T(8,128)(2,1)S(1)} %pad_maximum_fusion.1), channel_id=1, source_target_pairs={{0,224},{32,0},{64,32},{96,64},{128,96},{160,128},{192,160},{224,1... | collective-permute-start | bytes 1572872 | tf_op jit(solution)/shard_map/ppermute | solution.py:254
  8.6 3.4 %pack.1 = bf16[32,13,16,128]{3,2,1,0:T(8,128)(2,1)} custom-call(f32[1,1,3,2,512,512]{5,4,3,2,1,0:T(8,128)} %roots_ref.1), custom_call_target="tpu_custom_call" | custom-call | bytes 8388608 | tf_op jit(solution)/shard_map/pack/pallas_call | solution.py:78
  12.0 8.1 %all-to-all-start = ((bf16[32,13,16,128]{3,2,1,0:T(8,128)(2,1)}), bf16[32,13,16,128]{3,2,1,0:T(8,128)(2,1)S(1)}, u32[]{:S(2)}, u32[]{:S(2)}) async-start(bf16[32,13,16,128]{3,2,1,0:T(8,128)(2,1)} %pack.1), calls=%async_computation | async-start | bytes 3407872 | tf_op jit(solution)/shard_map/all_to_all | solution.py:295
  20.1 0.0 collective-permute-done
  20.1 0.0 collective-permute-done.1
  20.1 1.2 %fusion = (bf16[256,512]{1,0:T(8,128)(2,1)S(1)}, bf16[256,512]{1,0:T(8,128)(2,1)S(1)}) fusion(bf16[1,4096,512]{2,1,0:T(8,128)(2,1)} %param.4, s32[]{:T(128)S(6)} %select_n.50, bf16[512,512]{1,0:T(8,128)(2,1)} %collective-permute-done.1, s32[]{:T(128)S(6)} %select_n.49, bf16[512,512]{1,0:T(8,128)(2,1)S(1)} %collective-permute-done), kind=kLoop, calls=%fused_computation.3 | loop fusion | flops 1048576 | bytes 1572872 | tf_op jit(solution)/shard_map/convert_element_type | solution.py:261
  21.4 0.1 collective-permute-start.6
  21.5 2.7 %collective-permute-start.7 = (bf16[256,512]{1,0:T(8,128)(2,1)S(1)}, bf16[256,512]{1,0:T(8,128)(2,1)S(1)}, u32[]{:S(2)}, u32[]{:S(2)}) collective-permute-start(bf16[256,512]{1,0:T(8,128)(2,1)S(1)} %get-tuple-element.25), channel_id=1, source_target_pairs={{0,224},{32,0},{64,32},{96,64},{128,96},{160,128},{192,160},{224,1... | collective-permute-start | bytes 786440 | tf_op jit(solution)/shard_map/ppermute | solution.py:254
  24.1 1.2 %add_convert_fusion.2 = (bf16[256,512]{1,0:T(8,128)(2,1)S(1)}, bf16[256,512]{1,0:T(8,128)(2,1)S(1)}) fusion(bf16[4096,512]{1,0:T(8,128)(2,1)} %bitcast.15, s32[]{:T(128)S(6)} %select_n.52, bf16[512,512]{1,0:T(8,128)(2,1)} %collective-permute-done.1, s32[]{:T(128)S(6)} %select_n.51, bf16[512,512]{1,0:T(8,128)(2,1)S(1)} %collective-permute-done), kind=kLoop, calls=%fused_computation.8 | loop fusion | flops 1048576 | bytes 1572872 | tf_op jit(solution)/shard_map/convert_element_type | solution.py:261
  25.4 0.1 collective-permute-start.2
  25.5 2.7 %collective-permute-start.3 = (bf16[256,512]{1,0:T(8,128)(2,1)S(1)}, bf16[256,512]{1,0:T(8,128)(2,1)S(1)}, u32[]{:S(2)}, u32[]{:S(2)}) collective-permute-start(bf16[256,512]{1,0:T(8,128)(2,1)S(1)} %get-tuple-element.30), channel_id=1, source_target_pairs={{0,224},{32,0},{64,32},{96,64},{128,96},{160,128},{192,160},{224,1... | collective-permute-start | bytes 786440 | tf_op jit(solution)/shard_map/ppermute | solution.py:254
  28.1 1.3 %constant_dynamic-slice_fusion = (bf16[256,512]{1,0:T(8,128)(2,1)S(1)}, bf16[256,512]{1,0:T(8,128)(2,1)S(1)}, bf16[256,512]{1,0:T(8,128)(2,1)S(1)}, bf16[256,512]{1,0:T(8,128)(2,1)S(1)}) fusion(bf16[4096,512]{1,0:T(8,128)(2,1)} %bitcast.16, s32[]{:T(128)S(6)} %select_n.57, s32[]{:T(128)S(6)} %select_n.56, s32[]{:T(128)S(6)} %select_n.54, s32[]{:T(128)S(6)} %select_n.53), kind=kLoop, calls=%fused_computation.14 | loop fusion | bytes 2097168 | tf_op jit(solution)/shard_map/dynamic_slice | solution.py:258
  29.4 0.0 collective-permute-done.6.up_ref
  29.4 0.0 collective-permute-done.7.down_ref
  29.4 0.1 long_3.1
  29.6 2.3 %collective-permute-start.9 = (bf16[256,512]{1,0:T(8,128)(2,1)S(1)}, bf16[256,512]{1,0:T(8,128)(2,1)S(1)}, u32[]{:S(2)}, u32[]{:S(2)}) collective-permute-start(bf16[256,512]{1,0:T(8,128)(2,1)S(1)} %get-tuple-element.36), channel_id=1, source_target_pairs={{0,224},{32,0},{64,32},{96,64},{128,96},{160,128},{192,160},{224,1... | collective-permute-start | bytes 786440 | tf_op jit(solution)/shard_map/ppermute | solution.py:254
  31.8 0.0 collective-permute-start.8
  31.8 3.2 %collective-permute-done.2.up_ref = bf16[256,512]{1,0:T(8,128)(2,1)S(1)} collective-permute-done((bf16[256,512]{1,0:T(8,128)(2,1)S(1)}, bf16[256,512]{1,0:T(8,128)(2,1)S(1)}, u32[]{:S(2)}, u32[]{:S(2)}) %collective-permute-start.2) | collective-permute-done | bytes 262176 | tf_op jit(solution)/shard_map/ppermute | solution.py:254
  35.1 0.0 collective-permute-done.3.down_ref
  35.1 0.0 copy-start
  35.1 0.3 short_3.1
  35.4 1.0 %collective-permute-start.4 = (bf16[256,512]{1,0:T(8,128)(2,1)S(1)}, bf16[256,512]{1,0:T(8,128)(2,1)S(1)}, u32[]{:S(2)}, u32[]{:S(2)}) collective-permute-start(bf16[256,512]{1,0:T(8,128)(2,1)S(1)} %get-tuple-element.32), channel_id=1, source_target_pairs={{0,32},{32,64},{64,96},{96,128},{128,160},{160,192},{192,224},{224... | collective-permute-start | bytes 786440 | tf_op jit(solution)/shard_map/ppermute | solution.py:254
  36.3 1.9 %collective-permute-start.5 = (bf16[256,512]{1,0:T(8,128)(2,1)S(1)}, bf16[256,512]{1,0:T(8,128)(2,1)S(1)}, u32[]{:S(2)}, u32[]{:S(2)}) collective-permute-start(bf16[256,512]{1,0:T(8,128)(2,1)S(1)} %get-tuple-element.33), channel_id=1, source_target_pairs={{0,224},{32,0},{64,32},{96,64},{128,96},{160,128},{192,160},{224,1... | collective-permute-start | bytes 786440 | tf_op jit(solution)/shard_map/ppermute | solution.py:254
  38.2 5.9 %all-to-all-done.in_ref = bf16[32,13,16,128]{3,2,1,0:T(8,128)(2,1)S(1)} async-done(((bf16[32,13,16,128]{3,2,1,0:T(8,128)(2,1)}), bf16[32,13,16,128]{3,2,1,0:T(8,128)(2,1)S(1)}, u32[]{:S(2)}, u32[]{:S(2)}) %all-to-all-start) | async-done | bytes 1703968 | tf_op jit(solution)/shard_map/all_to_all | solution.py:295
  44.1 0.0 copy-done
  44.1 1.1 %pick.1 = bf16[32,5,16,128]{3,2,1,0:T(8,128)(2,1)} custom-call(s32[1,32]{1,0:T(1,128)S(1)} %copy-done, bf16[32,13,16,128]{3,2,1,0:T(8,128)(2,1)S(1)} %all-to-all-done.in_ref), custom_call_target="tpu_custom_call" | custom-call | bytes 3145728 | tf_op jit(solution)/shard_map/pick/pallas_call | solution.py:114
  45.2 0.0 copy-start.1
  45.2 5.0 %all-to-all-start.1 = ((bf16[32,5,16,128]{3,2,1,0:T(8,128)(2,1)}), bf16[32,5,16,128]{3,2,1,0:T(8,128)(2,1)S(1)}, u32[]{:S(2)}, u32[]{:S(2)}) async-start(bf16[32,5,16,128]{3,2,1,0:T(8,128)(2,1)} %pick.1), calls=%async_computation.1 | async-start | bytes 1310720 | tf_op jit(solution)/shard_map/all_to_all | solution.py:297
  50.3 0.0 collective-permute-done.9
  50.3 0.0 collective-permute-done.8
  50.3 2.0 %add_convert_fusion = (bf16[256,512]{1,0:T(8,128)(2,1)S(1)}, bf16[256,512]{1,0:T(8,128)(2,1)}) fusion(bf16[256,512]{1,0:T(8,128)(2,1)S(1)} %collective-permute-done.9, bf16[4096,512]{1,0:T(8,128)(2,1)} %bitcast.17, s32[]{:T(128)S(6)} %select_n.59, s32[]{:T(128)S(6)} %select_n.58, bf16[256,512]{1,0:T(8,128)(2,1)} %collective-permute-done.8), kind=kLoop, calls=%fused_computation.6 | loop fusion | flops 1048576 | bytes 1572872 | tf_op jit(solution)/shard_map/convert_element_type | solution.py:261
  52.3 1.6 %collective-permute-start.10 = (bf16[256,512]{1,0:T(8,128)(2,1)}, bf16[256,512]{1,0:T(8,128)(2,1)S(1)}, u32[]{:S(2)}, u32[]{:S(2)}) collective-permute-start(bf16[256,512]{1,0:T(8,128)(2,1)} %get-tuple-element.37), channel_id=1, source_target_pairs={{0,32},{32,64},{64,96},{96,128},{128,160},{160,192},{192,224},{224... | collective-permute-start | bytes 786440 | tf_op jit(solution)/shard_map/ppermute | solution.py:254
  53.8 1.1 %collective-permute-start.11 = (bf16[256,512]{1,0:T(8,128)(2,1)S(1)}, bf16[256,512]{1,0:T(8,128)(2,1)S(1)}, u32[]{:S(2)}, u32[]{:S(2)}) collective-permute-start(bf16[256,512]{1,0:T(8,128)(2,1)S(1)} %get-tuple-element.38), channel_id=1, source_target_pairs={{0,224},{32,0},{64,32},{96,64},{128,96},{160,128},{192,160},{224,1... | collective-permute-start | bytes 786440 | tf_op jit(solution)/shard_map/ppermute | solution.py:254
  54.9 1.1 %constant_dynamic-slice_fusion.2.own_ref = bf16[512,512]{1,0:T(8,128)(2,1)S(1)} fusion(bf16[4096,512]{1,0:T(8,128)(2,1)} %bitcast.18, s32[]{:T(128)S(6)} %select_n.55), kind=kLoop, calls=%fused_computation.16 | loop fusion | bytes 1048580 | tf_op jit(solution)/shard_map/dynamic_slice | solution.py:258
  56.0 0.0 collective-permute-done.4.up_b_ref
  56.0 0.0 collective-permute-done.5.down_a_ref
  56.0 0.1 ready.1.known_ref
  56.2 5.2 %collective-permute-done.10.up_a_ref = bf16[256,512]{1,0:T(8,128)(2,1)S(1)} collective-permute-done((bf16[256,512]{1,0:T(8,128)(2,1)}, bf16[256,512]{1,0:T(8,128)(2,1)S(1)}, u32[]{:S(2)}, u32[]{:S(2)}) %collective-permute-start.10) | collective-permute-done | bytes 262176 | tf_op jit(solution)/shard_map/ppermute | solution.py:254
  61.4 0.0 collective-permute-done.11.down_b_ref
  61.4 0.0 copy-done.1
  61.4 1.7 %adam.1 = (bf16[512,512]{1,0:T(8,128)(2,1)S(1)}, f32[512,512]{1,0:T(8,128)}, f32[1,128]{1,0:T(1,128)S(1)}) custom-call(f32[512,512]{1,0:T(8,128)S(1)} %ready.1.known_ref, f32[512,512]{1,0:T(8,128)S(1)} %copy-done.1, bf16[256,512]{1,0:T(8,128)(2,1)S(1)} %collective-permute-done.10.up_a_ref, bf16[256,512]{1,0:T(8,128)(2,1)S(1)} %collective-permute-done.11.down_b_ref), custom_call_target="tpu_custom_call" | custom-call | flops 2000000000 | bytes 5242880 | tf_op jit(solution)/shard_map/adam/pallas_call | solution.py:160
  63.1 0.1 all-to-all-done.1.in_ref
  63.2 2.1 %direction.1 = bf16[512,512]{1,0:T(8,128)(2,1)} custom-call(bf16[32,5,16,128]{3,2,1,0:T(8,128)(2,1)S(1)} %all-to-all-done.1.in_ref, bf16[512,512]{1,0:T(8,128)(2,1)S(1)} %get-tuple-element.39.gradient_ref, f32[1,128]{1,0:T(1,128)S(1)} %get-tuple-element.40.target_ref), custom_call_target="tpu_custom_call" | custom-call | flops 536870912 | bytes 2097152 | tf_op jit(solution)/shard_map/direction/pallas_call | solution.py:209
  (2 shorter events, 0.1 us)
Async XLA Ops:
  2.0 18.1 %collective-permute-start = (bf16[512,512]{1,0:T(8,128)(2,1)S(1)}, bf16[512,512]{1,0:T(8,128)(2,1)S(1)}, u32[]{:S(2)}, u32[]{:S(2)}) collective-permute-start(bf16[512,512]{1,0:T(8,128)(2,1)S(1)} %pad_maximum_fusion), channel_id=1, source_target_pairs={{0,32},{32,64},{64,96},{96,128},{128,160},{160,192},{192,224},{224... | collective-permute-start | bytes 1572872 | tf_op jit(solution)/shard_map/ppermute | solution.py:254
  4.6 15.6 %collective-permute-start.1 = (bf16[512,512]{1,0:T(8,128)(2,1)S(1)}, bf16[512,512]{1,0:T(8,128)(2,1)}, u32[]{:S(2)}, u32[]{:S(2)}) collective-permute-start(bf16[512,512]{1,0:T(8,128)(2,1)S(1)} %pad_maximum_fusion.1), channel_id=1, source_target_pairs={{0,224},{32,0},{64,32},{96,64},{128,96},{160,128},{192,160},{224,1... | collective-permute-start | bytes 1572872 | tf_op jit(solution)/shard_map/ppermute | solution.py:254
  12.0 32.1 %all-to-all-start = ((bf16[32,13,16,128]{3,2,1,0:T(8,128)(2,1)}), bf16[32,13,16,128]{3,2,1,0:T(8,128)(2,1)S(1)}, u32[]{:S(2)}, u32[]{:S(2)}) async-start(bf16[32,13,16,128]{3,2,1,0:T(8,128)(2,1)} %pack.1), calls=%async_computation | async-start | bytes 3407872 | tf_op jit(solution)/shard_map/all_to_all | solution.py:295
  21.4 8.0 %collective-permute-start.6 = (bf16[256,512]{1,0:T(8,128)(2,1)S(1)}, bf16[256,512]{1,0:T(8,128)(2,1)S(1)}, u32[]{:S(2)}, u32[]{:S(2)}) collective-permute-start(bf16[256,512]{1,0:T(8,128)(2,1)S(1)} %get-tuple-element.24), channel_id=1, source_target_pairs={{0,32},{32,64},{64,96},{96,128},{128,160},{160,192},{192,224},{224... | collective-permute-start | bytes 786440 | tf_op jit(solution)/shard_map/ppermute | solution.py:254
  21.5 8.0 %collective-permute-start.7 = (bf16[256,512]{1,0:T(8,128)(2,1)S(1)}, bf16[256,512]{1,0:T(8,128)(2,1)S(1)}, u32[]{:S(2)}, u32[]{:S(2)}) collective-permute-start(bf16[256,512]{1,0:T(8,128)(2,1)S(1)} %get-tuple-element.25), channel_id=1, source_target_pairs={{0,224},{32,0},{64,32},{96,64},{128,96},{160,128},{192,160},{224,1... | collective-permute-start | bytes 786440 | tf_op jit(solution)/shard_map/ppermute | solution.py:254
  25.4 9.7 %collective-permute-start.2 = (bf16[256,512]{1,0:T(8,128)(2,1)S(1)}, bf16[256,512]{1,0:T(8,128)(2,1)S(1)}, u32[]{:S(2)}, u32[]{:S(2)}) collective-permute-start(bf16[256,512]{1,0:T(8,128)(2,1)S(1)} %get-tuple-element.29), channel_id=1, source_target_pairs={{0,32},{32,64},{64,96},{96,128},{128,160},{160,192},{192,224},{224... | collective-permute-start | bytes 786440 | tf_op jit(solution)/shard_map/ppermute | solution.py:254
  25.5 9.6 %collective-permute-start.3 = (bf16[256,512]{1,0:T(8,128)(2,1)S(1)}, bf16[256,512]{1,0:T(8,128)(2,1)S(1)}, u32[]{:S(2)}, u32[]{:S(2)}) collective-permute-start(bf16[256,512]{1,0:T(8,128)(2,1)S(1)} %get-tuple-element.30), channel_id=1, source_target_pairs={{0,224},{32,0},{64,32},{96,64},{128,96},{160,128},{192,160},{224,1... | collective-permute-start | bytes 786440 | tf_op jit(solution)/shard_map/ppermute | solution.py:254
  29.6 20.7 %collective-permute-start.9 = (bf16[256,512]{1,0:T(8,128)(2,1)S(1)}, bf16[256,512]{1,0:T(8,128)(2,1)S(1)}, u32[]{:S(2)}, u32[]{:S(2)}) collective-permute-start(bf16[256,512]{1,0:T(8,128)(2,1)S(1)} %get-tuple-element.36), channel_id=1, source_target_pairs={{0,224},{32,0},{64,32},{96,64},{128,96},{160,128},{192,160},{224,1... | collective-permute-start | bytes 786440 | tf_op jit(solution)/shard_map/ppermute | solution.py:254
  31.8 18.5 %collective-permute-start.8 = (bf16[256,512]{1,0:T(8,128)(2,1)S(1)}, bf16[256,512]{1,0:T(8,128)(2,1)}, u32[]{:S(2)}, u32[]{:S(2)}) collective-permute-start(bf16[256,512]{1,0:T(8,128)(2,1)S(1)} %get-tuple-element.35), channel_id=1, source_target_pairs={{0,32},{32,64},{64,96},{96,128},{128,160},{160,192},{192,224},{224... | collective-permute-start | bytes 786440 | tf_op jit(solution)/shard_map/ppermute | solution.py:254
  35.1 9.1 %copy-start = (s32[1,32]{1,0:T(1,128)S(1)}, s32[1,32]{1,0:T(1,128)}, u32[]{:S(2)}) copy-start(s32[1,32]{1,0:T(1,128)} %owner_ref.1) | copy-start | bytes 388
  35.4 20.7 %collective-permute-start.4 = (bf16[256,512]{1,0:T(8,128)(2,1)S(1)}, bf16[256,512]{1,0:T(8,128)(2,1)S(1)}, u32[]{:S(2)}, u32[]{:S(2)}) collective-permute-start(bf16[256,512]{1,0:T(8,128)(2,1)S(1)} %get-tuple-element.32), channel_id=1, source_target_pairs={{0,32},{32,64},{64,96},{96,128},{128,160},{160,192},{192,224},{224... | collective-permute-start | bytes 786440 | tf_op jit(solution)/shard_map/ppermute | solution.py:254
  36.3 19.7 %collective-permute-start.5 = (bf16[256,512]{1,0:T(8,128)(2,1)S(1)}, bf16[256,512]{1,0:T(8,128)(2,1)S(1)}, u32[]{:S(2)}, u32[]{:S(2)}) collective-permute-start(bf16[256,512]{1,0:T(8,128)(2,1)S(1)} %get-tuple-element.33), channel_id=1, source_target_pairs={{0,224},{32,0},{64,32},{96,64},{128,96},{160,128},{192,160},{224,1... | collective-permute-start | bytes 786440 | tf_op jit(solution)/shard_map/ppermute | solution.py:254
  45.2 16.2 %copy-start.1 = (f32[512,512]{1,0:T(8,128)S(1)}, f32[512,512]{1,0:T(8,128)}, u32[]{:S(2)}) copy-start(f32[512,512]{1,0:T(8,128)} %moment_ref.1) | copy-start | bytes 3145732
  45.2 18.0 %all-to-all-start.1 = ((bf16[32,5,16,128]{3,2,1,0:T(8,128)(2,1)}), bf16[32,5,16,128]{3,2,1,0:T(8,128)(2,1)S(1)}, u32[]{:S(2)}, u32[]{:S(2)}) async-start(bf16[32,5,16,128]{3,2,1,0:T(8,128)(2,1)} %pick.1), calls=%async_computation.1 | async-start | bytes 1310720 | tf_op jit(solution)/shard_map/all_to_all | solution.py:297
  52.3 9.1 %collective-permute-start.10 = (bf16[256,512]{1,0:T(8,128)(2,1)}, bf16[256,512]{1,0:T(8,128)(2,1)S(1)}, u32[]{:S(2)}, u32[]{:S(2)}) collective-permute-start(bf16[256,512]{1,0:T(8,128)(2,1)} %get-tuple-element.37), channel_id=1, source_target_pairs={{0,32},{32,64},{64,96},{96,128},{128,160},{160,192},{192,224},{224... | collective-permute-start | bytes 786440 | tf_op jit(solution)/shard_map/ppermute | solution.py:254
  53.8 7.6 %collective-permute-start.11 = (bf16[256,512]{1,0:T(8,128)(2,1)S(1)}, bf16[256,512]{1,0:T(8,128)(2,1)S(1)}, u32[]{:S(2)}, u32[]{:S(2)}) collective-permute-start(bf16[256,512]{1,0:T(8,128)(2,1)S(1)} %get-tuple-element.38), channel_id=1, source_target_pairs={{0,224},{32,0},{64,32},{96,64},{128,96},{160,128},{192,160},{224,1... | collective-permute-start | bytes 786440 | tf_op jit(solution)/shard_map/ppermute | solution.py:254

commit v6 on v5

--- a/solution.py
+++ b/solution.py
@@ -240,7 +240,7 @@
         out_shape=[jax.ShapeDtypeStruct((HALF, B), jnp.bfloat16)] * 2,
         compiler_params=pltpu.CompilerParams(vmem_limit_bytes=8 * 1024 * 1024),
         cost_estimate=pl.CostEstimate(flops=flops, bytes_accessed=3 * 1024 * 1024, transcendentals=0),
-        input_output_aliases={2: 0, 3: 1} if name == "short_3" else {},
+        input_output_aliases={2: 0, 3: 1} if name == "long_3" else {},
         name=name,
     )(up, down, *own)
 

time: 65.8 us -> 65.6 us (level)
  no operation moved by 1% of the time
where the time goes in v6:
time: 65.6 us; the launch traced here: 65.2 us
  starting transfers between devices  32.8 us (50%)
  waiting for transfers between devices  14.6 us (22%)
  Pallas kernels  8.78 us (13%)
  other arithmetic  4.52 us (7%)
  local copies, waits for them, and re-layouts  3.6 us (5%)
  between operations  0.88 us (1%)
    ppermute x6, starting transfers between devices, move(): lax.ppermute(down, 'rep', pairs_down)  14.6 us
    ppermute x6, waiting for transfers between devices, move(): lax.ppermute(up, 'rep', pairs_up)  8.28 us
    all_to_all x1, starting transfers between devices, body(): lax.all_to_all(packed, 'shard', split_axis=0, concat_axis=0, tiled=True)  8.05 us
    all_to_all x1, waiting for transfers between devices, body(): lax.all_to_all(packed, 'shard', split_axis=0, concat_axis=0, tiled=True)  6.1 us
    ppermute x6, starting transfers between devices, move(): lax.ppermute(up, 'rep', pairs_up)  5.25 us
    all_to_all x1, starting transfers between devices, body(): lax.all_to_all(picked, 'shard', split_axis=0, concat_axis=0, tiled=True)  4.88 us
    convert_element_type x3, other arithmetic, add(): return (a.astype(jnp.float32) + b.astype(jnp.float32)).astype(jnp.bfloat16)  4.44 us
    dynamic_slice x3, local copies, waits for them, and re-layouts, mine(): return lax.dynamic_slice(source, (chunk * B + start, 0), (rows, B))  3.6 us
  transfers between devices with their start and end apart: 14, of which 4 were waited for; matrix products, arithmetic and copies ran while one was open for 10% of the time, Pallas kernels for 10%

profile of v6, /device:TPU:1, one launch (start us, length us, event | category | flops | bytes accessed | tf_op | source)
XLA Modules:
  0.0 65.2 jit_solution(94353921207077165)
XLA Ops:
  0.7 1.3 %dynamic-slice_bitcast_fusion.1 = (bf16[256,512]{1,0:T(8,128)(2,1)S(1)}, bf16[256,512]{1,0:T(8,128)(2,1)S(1)}, bf16[256,512]{1,0:T(8,128)(2,1)S(1)}, bf16[256,512]{1,0:T(8,128)(2,1)S(1)}) fusion(bf16[1,4096,512]{2,1,0:T(8,128)(2,1)} %param.4, s32[]{:T(128)S(6)} %select_n.47, s32[]{:T(128)S(6)} %select_n.48, s32[]{:T(128)S(6)} %select_n.46, s32[]{:T(128)S(6)} %select_n.45), kind=kLoop, calls=%fused_computation.11 | loop fusion | bytes 2097168 | tf_op jit(solution)/shard_map/dynamic_slice | solution.py:258
  2.0 2.5 %collective-permute-start = (bf16[512,512]{1,0:T(8,128)(2,1)S(1)}, bf16[512,512]{1,0:T(8,128)(2,1)S(1)}, u32[]{:S(2)}, u32[]{:S(2)}) collective-permute-start(bf16[512,512]{1,0:T(8,128)(2,1)S(1)} %pad_maximum_fusion), channel_id=1, source_target_pairs={{0,32},{32,64},{64,96},{96,128},{128,160},{160,192},{192,224},{224... | collective-permute-start | bytes 1572872 | tf_op jit(solution)/shard_map/ppermute | solution.py:254
  4.6 4.0 %collective-permute-start.1 = (bf16[512,512]{1,0:T(8,128)(2,1)S(1)}, bf16[512,512]{1,0:T(8,128)(2,1)}, u32[]{:S(2)}, u32[]{:S(2)}) collective-permute-start(bf16[512,512]{1,0:T(8,128)(2,1)S(1)} %pad_maximum_fusion.1), channel_id=1, source_target_pairs={{0,224},{32,0},{64,32},{96,64},{128,96},{160,128},{192,160},{224,1... | collective-permute-start | bytes 1572872 | tf_op jit(solution)/shard_map/ppermute | solution.py:254
  8.6 3.4 %pack.1 = bf16[32,13,16,128]{3,2,1,0:T(8,128)(2,1)} custom-call(f32[1,1,3,2,512,512]{5,4,3,2,1,0:T(8,128)} %roots_ref.1), custom_call_target="tpu_custom_call" | custom-call | bytes 8388608 | tf_op jit(solution)/shard_map/pack/pallas_call | solution.py:78
  12.0 8.1 %all-to-all-start = ((bf16[32,13,16,128]{3,2,1,0:T(8,128)(2,1)}), bf16[32,13,16,128]{3,2,1,0:T(8,128)(2,1)S(1)}, u32[]{:S(2)}, u32[]{:S(2)}) async-start(bf16[32,13,16,128]{3,2,1,0:T(8,128)(2,1)} %pack.1), calls=%async_computation | async-start | bytes 3407872 | tf_op jit(solution)/shard_map/all_to_all | solution.py:295
  20.1 0.0 collective-permute-done
  20.1 0.0 collective-permute-done.1
  20.1 1.2 %fusion = (bf16[256,512]{1,0:T(8,128)(2,1)S(1)}, bf16[256,512]{1,0:T(8,128)(2,1)S(1)}) fusion(bf16[1,4096,512]{2,1,0:T(8,128)(2,1)} %param.4, s32[]{:T(128)S(6)} %select_n.50, bf16[512,512]{1,0:T(8,128)(2,1)} %collective-permute-done.1, s32[]{:T(128)S(6)} %select_n.49, bf16[512,512]{1,0:T(8,128)(2,1)S(1)} %collective-permute-done), kind=kLoop, calls=%fused_computation.3 | loop fusion | flops 1048576 | bytes 1572872 | tf_op jit(solution)/shard_map/convert_element_type | solution.py:261
  21.4 0.1 collective-permute-start.6
  21.5 2.7 %collective-permute-start.7 = (bf16[256,512]{1,0:T(8,128)(2,1)S(1)}, bf16[256,512]{1,0:T(8,128)(2,1)S(1)}, u32[]{:S(2)}, u32[]{:S(2)}) collective-permute-start(bf16[256,512]{1,0:T(8,128)(2,1)S(1)} %get-tuple-element.25), channel_id=1, source_target_pairs={{0,224},{32,0},{64,32},{96,64},{128,96},{160,128},{192,160},{224,1... | collective-permute-start | bytes 786440 | tf_op jit(solution)/shard_map/ppermute | solution.py:254
  24.1 1.2 %add_convert_fusion.2 = (bf16[256,512]{1,0:T(8,128)(2,1)S(1)}, bf16[256,512]{1,0:T(8,128)(2,1)S(1)}) fusion(bf16[4096,512]{1,0:T(8,128)(2,1)} %bitcast.15, s32[]{:T(128)S(6)} %select_n.52, bf16[512,512]{1,0:T(8,128)(2,1)} %collective-permute-done.1, s32[]{:T(128)S(6)} %select_n.51, bf16[512,512]{1,0:T(8,128)(2,1)S(1)} %collective-permute-done), kind=kLoop, calls=%fused_computation.8 | loop fusion | flops 1048576 | bytes 1572872 | tf_op jit(solution)/shard_map/convert_element_type | solution.py:261
  25.4 0.1 collective-permute-start.2
  25.5 2.7 %collective-permute-start.3 = (bf16[256,512]{1,0:T(8,128)(2,1)S(1)}, bf16[256,512]{1,0:T(8,128)(2,1)S(1)}, u32[]{:S(2)}, u32[]{:S(2)}) collective-permute-start(bf16[256,512]{1,0:T(8,128)(2,1)S(1)} %get-tuple-element.30), channel_id=1, source_target_pairs={{0,224},{32,0},{64,32},{96,64},{128,96},{160,128},{192,160},{224,1... | collective-permute-start | bytes 786440 | tf_op jit(solution)/shard_map/ppermute | solution.py:254
  28.1 1.3 %constant_dynamic-slice_fusion = (bf16[256,512]{1,0:T(8,128)(2,1)S(1)}, bf16[256,512]{1,0:T(8,128)(2,1)S(1)}, bf16[256,512]{1,0:T(8,128)(2,1)S(1)}, bf16[256,512]{1,0:T(8,128)(2,1)S(1)}) fusion(bf16[4096,512]{1,0:T(8,128)(2,1)} %bitcast.16, s32[]{:T(128)S(6)} %select_n.57, s32[]{:T(128)S(6)} %select_n.56, s32[]{:T(128)S(6)} %select_n.54, s32[]{:T(128)S(6)} %select_n.53), kind=kLoop, calls=%fused_computation.14 | loop fusion | bytes 2097168 | tf_op jit(solution)/shard_map/dynamic_slice | solution.py:258
  29.4 0.0 collective-permute-done.6.up_ref
  29.4 0.0 collective-permute-done.7.down_ref
  29.4 0.3 long_3.1
  29.7 2.3 %collective-permute-start.9 = (bf16[256,512]{1,0:T(8,128)(2,1)S(1)}, bf16[256,512]{1,0:T(8,128)(2,1)S(1)}, u32[]{:S(2)}, u32[]{:S(2)}) collective-permute-start(bf16[256,512]{1,0:T(8,128)(2,1)S(1)} %get-tuple-element.36), channel_id=1, source_target_pairs={{0,224},{32,0},{64,32},{96,64},{128,96},{160,128},{192,160},{224,1... | collective-permute-start | bytes 786440 | tf_op jit(solution)/shard_map/ppermute | solution.py:254
  32.0 0.0 collective-permute-start.8
  32.0 3.1 %collective-permute-done.2.up_ref = bf16[256,512]{1,0:T(8,128)(2,1)S(1)} collective-permute-done((bf16[256,512]{1,0:T(8,128)(2,1)S(1)}, bf16[256,512]{1,0:T(8,128)(2,1)S(1)}, u32[]{:S(2)}, u32[]{:S(2)}) %collective-permute-start.2) | collective-permute-done | bytes 262176 | tf_op jit(solution)/shard_map/ppermute | solution.py:254
  35.1 0.0 collective-permute-done.3.down_ref
  35.1 0.0 copy-start
  35.1 0.1 short_3.1
  35.2 1.0 %collective-permute-start.4 = (bf16[256,512]{1,0:T(8,128)(2,1)S(1)}, bf16[256,512]{1,0:T(8,128)(2,1)S(1)}, u32[]{:S(2)}, u32[]{:S(2)}) collective-permute-start(bf16[256,512]{1,0:T(8,128)(2,1)S(1)} %get-tuple-element.32), channel_id=1, source_target_pairs={{0,32},{32,64},{64,96},{96,128},{128,160},{160,192},{192,224},{224... | collective-permute-start | bytes 786440 | tf_op jit(solution)/shard_map/ppermute | solution.py:254
  36.2 1.9 %collective-permute-start.5 = (bf16[256,512]{1,0:T(8,128)(2,1)S(1)}, bf16[256,512]{1,0:T(8,128)(2,1)S(1)}, u32[]{:S(2)}, u32[]{:S(2)}) collective-permute-start(bf16[256,512]{1,0:T(8,128)(2,1)S(1)} %get-tuple-element.33), channel_id=1, source_target_pairs={{0,224},{32,0},{64,32},{96,64},{128,96},{160,128},{192,160},{224,1... | collective-permute-start | bytes 786440 | tf_op jit(solution)/shard_map/ppermute | solution.py:254
  38.0 6.1 %all-to-all-done.in_ref = bf16[32,13,16,128]{3,2,1,0:T(8,128)(2,1)S(1)} async-done(((bf16[32,13,16,128]{3,2,1,0:T(8,128)(2,1)}), bf16[32,13,16,128]{3,2,1,0:T(8,128)(2,1)S(1)}, u32[]{:S(2)}, u32[]{:S(2)}) %all-to-all-start) | async-done | bytes 1703968 | tf_op jit(solution)/shard_map/all_to_all | solution.py:295
  44.1 0.0 copy-done
  44.1 1.1 %pick.1 = bf16[32,5,16,128]{3,2,1,0:T(8,128)(2,1)} custom-call(s32[1,32]{1,0:T(1,128)S(1)} %copy-done, bf16[32,13,16,128]{3,2,1,0:T(8,128)(2,1)S(1)} %all-to-all-done.in_ref), custom_call_target="tpu_custom_call" | custom-call | bytes 3145728 | tf_op jit(solution)/shard_map/pick/pallas_call | solution.py:114
  45.2 0.0 copy-start.1
  45.2 4.9 %all-to-all-start.1 = ((bf16[32,5,16,128]{3,2,1,0:T(8,128)(2,1)}), bf16[32,5,16,128]{3,2,1,0:T(8,128)(2,1)S(1)}, u32[]{:S(2)}, u32[]{:S(2)}) async-start(bf16[32,5,16,128]{3,2,1,0:T(8,128)(2,1)} %pick.1), calls=%async_computation.1 | async-start | bytes 1310720 | tf_op jit(solution)/shard_map/all_to_all | solution.py:297
  50.1 0.0 collective-permute-done.9
  50.1 0.0 collective-permute-done.8
  50.2 2.0 %add_convert_fusion = (bf16[256,512]{1,0:T(8,128)(2,1)S(1)}, bf16[256,512]{1,0:T(8,128)(2,1)}) fusion(bf16[256,512]{1,0:T(8,128)(2,1)S(1)} %collective-permute-done.9, bf16[4096,512]{1,0:T(8,128)(2,1)} %bitcast.17, s32[]{:T(128)S(6)} %select_n.59, s32[]{:T(128)S(6)} %select_n.58, bf16[256,512]{1,0:T(8,128)(2,1)} %collective-permute-done.8), kind=kLoop, calls=%fused_computation.6 | loop fusion | flops 1048576 | bytes 1572872 | tf_op jit(solution)/shard_map/convert_element_type | solution.py:261
  52.1 1.6 %collective-permute-start.10 = (bf16[256,512]{1,0:T(8,128)(2,1)}, bf16[256,512]{1,0:T(8,128)(2,1)S(1)}, u32[]{:S(2)}, u32[]{:S(2)}) collective-permute-start(bf16[256,512]{1,0:T(8,128)(2,1)} %get-tuple-element.37), channel_id=1, source_target_pairs={{0,32},{32,64},{64,96},{96,128},{128,160},{160,192},{192,224},{224... | collective-permute-start | bytes 786440 | tf_op jit(solution)/shard_map/ppermute | solution.py:254
  53.7 1.1 %collective-permute-start.11 = (bf16[256,512]{1,0:T(8,128)(2,1)S(1)}, bf16[256,512]{1,0:T(8,128)(2,1)S(1)}, u32[]{:S(2)}, u32[]{:S(2)}) collective-permute-start(bf16[256,512]{1,0:T(8,128)(2,1)S(1)} %get-tuple-element.38), channel_id=1, source_target_pairs={{0,224},{32,0},{64,32},{96,64},{128,96},{160,128},{192,160},{224,1... | collective-permute-start | bytes 786440 | tf_op jit(solution)/shard_map/ppermute | solution.py:254
  54.8 1.1 %constant_dynamic-slice_fusion.2.own_ref = bf16[512,512]{1,0:T(8,128)(2,1)S(1)} fusion(bf16[4096,512]{1,0:T(8,128)(2,1)} %bitcast.18, s32[]{:T(128)S(6)} %select_n.55), kind=kLoop, calls=%fused_computation.16 | loop fusion | bytes 1048580 | tf_op jit(solution)/shard_map/dynamic_slice | solution.py:258
  55.9 0.0 collective-permute-done.4.up_b_ref
  55.9 0.0 collective-permute-done.5.down_a_ref
  55.9 0.1 ready.1.known_ref
  56.0 5.2 %collective-permute-done.10.up_a_ref = bf16[256,512]{1,0:T(8,128)(2,1)S(1)} collective-permute-done((bf16[256,512]{1,0:T(8,128)(2,1)}, bf16[256,512]{1,0:T(8,128)(2,1)S(1)}, u32[]{:S(2)}, u32[]{:S(2)}) %collective-permute-start.10) | collective-permute-done | bytes 262176 | tf_op jit(solution)/shard_map/ppermute | solution.py:254
  61.2 0.0 collective-permute-done.11.down_b_ref
  61.3 0.0 copy-done.1
  61.3 1.7 %adam.1 = (bf16[512,512]{1,0:T(8,128)(2,1)S(1)}, f32[512,512]{1,0:T(8,128)}, f32[1,128]{1,0:T(1,128)S(1)}) custom-call(f32[512,512]{1,0:T(8,128)S(1)} %ready.1.known_ref, f32[512,512]{1,0:T(8,128)S(1)} %copy-done.1, bf16[256,512]{1,0:T(8,128)(2,1)S(1)} %collective-permute-done.10.up_a_ref, bf16[256,512]{1,0:T(8,128)(2,1)S(1)} %collective-permute-done.11.down_b_ref), custom_call_target="tpu_custom_call" | custom-call | flops 2000000000 | bytes 5242880 | tf_op jit(solution)/shard_map/adam/pallas_call | solution.py:160
  62.9 0.1 all-to-all-done.1.in_ref
  63.1 2.1 %direction.1 = bf16[512,512]{1,0:T(8,128)(2,1)} custom-call(bf16[32,5,16,128]{3,2,1,0:T(8,128)(2,1)S(1)} %all-to-all-done.1.in_ref, bf16[512,512]{1,0:T(8,128)(2,1)S(1)} %get-tuple-element.39.gradient_ref, f32[1,128]{1,0:T(1,128)S(1)} %get-tuple-element.40.target_ref), custom_call_target="tpu_custom_call" | custom-call | flops 536870912 | bytes 2097152 | tf_op jit(solution)/shard_map/direction/pallas_call | solution.py:209
  (2 shorter events, 0.1 us)
Async XLA Ops:
  2.0 18.1 %collective-permute-start = (bf16[512,512]{1,0:T(8,128)(2,1)S(1)}, bf16[512,512]{1,0:T(8,128)(2,1)S(1)}, u32[]{:S(2)}, u32[]{:S(2)}) collective-permute-start(bf16[512,512]{1,0:T(8,128)(2,1)S(1)} %pad_maximum_fusion), channel_id=1, source_target_pairs={{0,32},{32,64},{64,96},{96,128},{128,160},{160,192},{192,224},{224... | collective-permute-start | bytes 1572872 | tf_op jit(solution)/shard_map/ppermute | solution.py:254
  4.6 15.6 %collective-permute-start.1 = (bf16[512,512]{1,0:T(8,128)(2,1)S(1)}, bf16[512,512]{1,0:T(8,128)(2,1)}, u32[]{:S(2)}, u32[]{:S(2)}) collective-permute-start(bf16[512,512]{1,0:T(8,128)(2,1)S(1)} %pad_maximum_fusion.1), channel_id=1, source_target_pairs={{0,224},{32,0},{64,32},{96,64},{128,96},{160,128},{192,160},{224,1... | collective-permute-start | bytes 1572872 | tf_op jit(solution)/shard_map/ppermute | solution.py:254
  12.0 32.1 %all-to-all-start = ((bf16[32,13,16,128]{3,2,1,0:T(8,128)(2,1)}), bf16[32,13,16,128]{3,2,1,0:T(8,128)(2,1)S(1)}, u32[]{:S(2)}, u32[]{:S(2)}) async-start(bf16[32,13,16,128]{3,2,1,0:T(8,128)(2,1)} %pack.1), calls=%async_computation | async-start | bytes 3407872 | tf_op jit(solution)/shard_map/all_to_all | solution.py:295
  21.4 8.0 %collective-permute-start.6 = (bf16[256,512]{1,0:T(8,128)(2,1)S(1)}, bf16[256,512]{1,0:T(8,128)(2,1)S(1)}, u32[]{:S(2)}, u32[]{:S(2)}) collective-permute-start(bf16[256,512]{1,0:T(8,128)(2,1)S(1)} %get-tuple-element.24), channel_id=1, source_target_pairs={{0,32},{32,64},{64,96},{96,128},{128,160},{160,192},{192,224},{224... | collective-permute-start | bytes 786440 | tf_op jit(solution)/shard_map/ppermute | solution.py:254
  21.5 7.9 %collective-permute-start.7 = (bf16[256,512]{1,0:T(8,128)(2,1)S(1)}, bf16[256,512]{1,0:T(8,128)(2,1)S(1)}, u32[]{:S(2)}, u32[]{:S(2)}) collective-permute-start(bf16[256,512]{1,0:T(8,128)(2,1)S(1)} %get-tuple-element.25), channel_id=1, source_target_pairs={{0,224},{32,0},{64,32},{96,64},{128,96},{160,128},{192,160},{224,1... | collective-permute-start | bytes 786440 | tf_op jit(solution)/shard_map/ppermute | solution.py:254
  25.4 9.7 %collective-permute-start.2 = (bf16[256,512]{1,0:T(8,128)(2,1)S(1)}, bf16[256,512]{1,0:T(8,128)(2,1)S(1)}, u32[]{:S(2)}, u32[]{:S(2)}) collective-permute-start(bf16[256,512]{1,0:T(8,128)(2,1)S(1)} %get-tuple-element.29), channel_id=1, source_target_pairs={{0,32},{32,64},{64,96},{96,128},{128,160},{160,192},{192,224},{224... | collective-permute-start | bytes 786440 | tf_op jit(solution)/shard_map/ppermute | solution.py:254
  25.5 9.6 %collective-permute-start.3 = (bf16[256,512]{1,0:T(8,128)(2,1)S(1)}, bf16[256,512]{1,0:T(8,128)(2,1)S(1)}, u32[]{:S(2)}, u32[]{:S(2)}) collective-permute-start(bf16[256,512]{1,0:T(8,128)(2,1)S(1)} %get-tuple-element.30), channel_id=1, source_target_pairs={{0,224},{32,0},{64,32},{96,64},{128,96},{160,128},{192,160},{224,1... | collective-permute-start | bytes 786440 | tf_op jit(solution)/shard_map/ppermute | solution.py:254
  29.7 20.4 %collective-permute-start.9 = (bf16[256,512]{1,0:T(8,128)(2,1)S(1)}, bf16[256,512]{1,0:T(8,128)(2,1)S(1)}, u32[]{:S(2)}, u32[]{:S(2)}) collective-permute-start(bf16[256,512]{1,0:T(8,128)(2,1)S(1)} %get-tuple-element.36), channel_id=1, source_target_pairs={{0,224},{32,0},{64,32},{96,64},{128,96},{160,128},{192,160},{224,1... | collective-permute-start | bytes 786440 | tf_op jit(solution)/shard_map/ppermute | solution.py:254
  32.0 18.2 %collective-permute-start.8 = (bf16[256,512]{1,0:T(8,128)(2,1)S(1)}, bf16[256,512]{1,0:T(8,128)(2,1)}, u32[]{:S(2)}, u32[]{:S(2)}) collective-permute-start(bf16[256,512]{1,0:T(8,128)(2,1)S(1)} %get-tuple-element.35), channel_id=1, source_target_pairs={{0,32},{32,64},{64,96},{96,128},{128,160},{160,192},{192,224},{224... | collective-permute-start | bytes 786440 | tf_op jit(solution)/shard_map/ppermute | solution.py:254
  35.1 9.1 %copy-start = (s32[1,32]{1,0:T(1,128)S(1)}, s32[1,32]{1,0:T(1,128)}, u32[]{:S(2)}) copy-start(s32[1,32]{1,0:T(1,128)} %owner_ref.1) | copy-start | bytes 388
  35.2 20.7 %collective-permute-start.4 = (bf16[256,512]{1,0:T(8,128)(2,1)S(1)}, bf16[256,512]{1,0:T(8,128)(2,1)S(1)}, u32[]{:S(2)}, u32[]{:S(2)}) collective-permute-start(bf16[256,512]{1,0:T(8,128)(2,1)S(1)} %get-tuple-element.32), channel_id=1, source_target_pairs={{0,32},{32,64},{64,96},{96,128},{128,160},{160,192},{192,224},{224... | collective-permute-start | bytes 786440 | tf_op jit(solution)/shard_map/ppermute | solution.py:254
  36.2 19.7 %collective-permute-start.5 = (bf16[256,512]{1,0:T(8,128)(2,1)S(1)}, bf16[256,512]{1,0:T(8,128)(2,1)S(1)}, u32[]{:S(2)}, u32[]{:S(2)}) collective-permute-start(bf16[256,512]{1,0:T(8,128)(2,1)S(1)} %get-tuple-element.33), channel_id=1, source_target_pairs={{0,224},{32,0},{64,32},{96,64},{128,96},{160,128},{192,160},{224,1... | collective-permute-start | bytes 786440 | tf_op jit(solution)/shard_map/ppermute | solution.py:254
  45.2 16.0 %copy-start.1 = (f32[512,512]{1,0:T(8,128)S(1)}, f32[512,512]{1,0:T(8,128)}, u32[]{:S(2)}) copy-start(f32[512,512]{1,0:T(8,128)} %moment_ref.1) | copy-start | bytes 3145732
  45.2 17.8 %all-to-all-start.1 = ((bf16[32,5,16,128]{3,2,1,0:T(8,128)(2,1)}), bf16[32,5,16,128]{3,2,1,0:T(8,128)(2,1)S(1)}, u32[]{:S(2)}, u32[]{:S(2)}) async-start(bf16[32,5,16,128]{3,2,1,0:T(8,128)(2,1)} %pick.1), calls=%async_computation.1 | async-start | bytes 1310720 | tf_op jit(solution)/shard_map/all_to_all | solution.py:297
  52.1 9.1 %collective-permute-start.10 = (bf16[256,512]{1,0:T(8,128)(2,1)}, bf16[256,512]{1,0:T(8,128)(2,1)S(1)}, u32[]{:S(2)}, u32[]{:S(2)}) collective-permute-start(bf16[256,512]{1,0:T(8,128)(2,1)} %get-tuple-element.37), channel_id=1, source_target_pairs={{0,32},{32,64},{64,96},{96,128},{128,160},{160,192},{192,224},{224... | collective-permute-start | bytes 786440 | tf_op jit(solution)/shard_map/ppermute | solution.py:254
  53.7 7.6 %collective-permute-start.11 = (bf16[256,512]{1,0:T(8,128)(2,1)S(1)}, bf16[256,512]{1,0:T(8,128)(2,1)S(1)}, u32[]{:S(2)}, u32[]{:S(2)}) collective-permute-start(bf16[256,512]{1,0:T(8,128)(2,1)S(1)} %get-tuple-element.38), channel_id=1, source_target_pairs={{0,224},{32,0},{64,32},{96,64},{128,96},{160,128},{192,160},{224,1... | collective-permute-start | bytes 786440 | tf_op jit(solution)/shard_map/ppermute | solution.py:254
